TPU v7x, 32 devices: a whole 2x2x4 slice. The times are simulated.
32 devices in a mesh: fsdp: 16 (over z, x, core), tp: 2 (over y).
Axes of the slice: x: 2, y: 2, z: 4, core: 2. Of those that a mesh axis runs over, the one named last changes fastest.
Arguments:
- tokens: bfloat16 [8192, 1024], P('fsdp'), may hold values from -6 to 6
- cotangent: bfloat16 [8192, 1024], P('fsdp'), may hold values from -6 to 6
- segments: int32 [8192], P('fsdp'), may hold values from 0 to 7, never falling along the last dimension, each value on 1 to 2000 neighbouring positions
- doc_batch: int32 [8], replicated, may hold values from 0 to 2
- ln1_gain: float32 [2, 1024], replicated, may hold values from 0.5 to 1.5
- ln1_bias: float32 [2, 1024], replicated, may hold values from -4 to 4
- w_qkv: bfloat16 [2, 1024, 3, 1024], P(None, 'fsdp', None, 'tp'), may hold values from -0.1875 to 0.1875
- b_qv: float32 [2, 2, 1024], P(None, None, 'tp'), may hold values from -6 to 6
- w_out: bfloat16 [2, 1024, 1024], P(None, 'tp', 'fsdp'), may hold values from -3 to 3
- b_out: float32 [2, 1024], replicated, may hold values from -4 to 4
- ln2_gain: float32 [2, 1024], replicated, may hold values from 0.5 to 1.5
- ln2_bias: float32 [2, 1024], replicated, may hold values from -4 to 4
- w_fc: bfloat16 [2, 1024, 4096], P(None, 'fsdp', 'tp'), may hold values from -0.1875 to 0.1875
- b_fc: float32 [2, 4096], P(None, 'tp'), may hold values from -4 to 4
- w_proj: bfloat16 [2, 4096, 1024], P(None, 'tp', 'fsdp'), may hold values from -0.09375 to 0.09375
- b_proj: float32 [2, 1024], replicated, may hold values from -4 to 4
Outputs:
- outputs: bfloat16 [8192, 1024], P('fsdp')
- grad_tokens: float32 [8192, 1024], P('fsdp')
- grad_ln1_gain: float32 [2, 1024], replicated
- grad_ln1_bias: float32 [2, 1024], replicated
- grad_w_qkv: float32 [2, 1024, 3, 1024], P(None, 'fsdp', None, 'tp')
- grad_b_qv: float32 [2, 2, 1024], P(None, None, 'tp')
- grad_w_out: float32 [2, 1024, 1024], P(None, 'tp', 'fsdp')
- grad_b_out: float32 [2, 1024], replicated
- grad_ln2_gain: float32 [2, 1024], replicated
- grad_ln2_bias: float32 [2, 1024], replicated
- grad_w_fc: float32 [2, 1024, 4096], P(None, 'fsdp', 'tp')
- grad_b_fc: float32 [2, 4096], P(None, 'tp')
- grad_w_proj: float32 [2, 4096, 1024], P(None, 'tp', 'fsdp')
- grad_b_proj: float32 [2, 1024], replicated
Inputs may be any that keep to these rules, and one draw needn't show every extreme that they name: `segments`: documents are contiguous and numbered in order, each of 1 to 2000 tokens, one of exactly 2000.
All inputs are finite; a program needn't handle non-finite values.
Results may differ from a plain program's by a relative error of at most 0.013.
Values may be sent and summed in bfloat16 or wider, within the bound.
A program may use at most 192 MiB of HBM per device.

v0:
```python
import jax
import jax.numpy as jnp
from jax import lax
from jax.sharding import PartitionSpec as P

HEAD_DIM = 64
LAYERS = 2
MB = 3
REACH = 4


EPS = 1e-05


def passed_along(shard, axis, by):
    devices = lax.axis_size(axis)
    pairs = [(i, i + by) for i in range(devices) if 0 <= i + by < devices]
    return lax.ppermute(shard, axis, pairs)


def norm_forward(inputs, gain_vec, bias_vec):
    row_mean = jnp.mean(inputs, -1, keepdims=True)
    centred = inputs - row_mean
    row_var = jnp.mean(centred * centred, -1, keepdims=True)
    inv_scale = lax.rsqrt(row_var + EPS)
    unit_rows = centred * inv_scale
    return (unit_rows * gain_vec + bias_vec, unit_rows, inv_scale)


def norm_backward(grad_rows, unit_rows, inv_scale, gain_vec):
    grad_gain = jnp.sum(grad_rows * unit_rows, 0)
    grad_bias = jnp.sum(grad_rows, 0)
    scaled = grad_rows * gain_vec
    grad_in = inv_scale * (
        scaled
        - jnp.mean(scaled, -1, keepdims=True)
        - unit_rows * jnp.mean(scaled * unit_rows, -1, keepdims=True)
    )
    return (grad_in, grad_gain, grad_bias)


def gelu_tanh(inputs):
    return (
        0.5
        * inputs
        * (1.0 + jnp.tanh(0.7978845608028654 * (inputs + 0.044715 * inputs * inputs * inputs)))
    )


def over_tp(partial_value):
    return lax.psum(partial_value, "tp")


def fetch_weights(w_qkv, w_out, w_fc, w_proj, layer_at):
    return (
        lax.all_gather(w_qkv[layer_at], "fsdp", axis=0, tiled=True),
        lax.all_gather(w_out[layer_at], "fsdp", axis=1, tiled=True),
        lax.all_gather(w_fc[layer_at], "fsdp", axis=0, tiled=True),
        lax.all_gather(w_proj[layer_at], "fsdp", axis=1, tiled=True),
    )


def earlier_keys(keys_here, values_here, segments):
    key_parts = []
    value_parts = []
    seg_parts = []
    for reach_by in range(REACH, 0, -1):
        key_far, value_far, seg_far = passed_along(
            (keys_here, values_here, segments), "fsdp", reach_by
        )
        key_parts.append(key_far)
        value_parts.append(value_far)
        seg_parts.append(seg_far)
    key_parts.append(keys_here)
    value_parts.append(values_here)
    seg_parts.append(segments)
    return (
        jnp.concatenate(key_parts, 0),
        jnp.concatenate(value_parts, 0),
        jnp.concatenate(seg_parts, 0),
    )


def return_key_grads(grad_keys, grad_values, row_count):
    own_keys = grad_keys[REACH * row_count :]
    own_values = grad_values[REACH * row_count :]
    for reach_by in range(1, REACH + 1):
        first_row = (REACH - reach_by) * row_count
        back_keys, back_values = passed_along(
            (
                grad_keys[first_row : first_row + row_count],
                grad_values[first_row : first_row + row_count],
            ),
            "fsdp",
            -reach_by,
        )
        own_keys = own_keys + back_keys
        own_values = own_values + back_values
    return (own_keys, own_values)


def split_heads(matrix, head_count):
    return matrix.reshape(matrix.shape[0], head_count, HEAD_DIM).transpose(1, 0, 2)


def join_heads(stacked):
    return stacked.transpose(1, 0, 2).reshape(stacked.shape[1], stacked.shape[0] * stacked.shape[2])


def head_scores(query_h, keys_h, allowed):
    raw_scores = jnp.einsum(
        "qd,kd->qk", query_h, keys_h, preferred_element_type=jnp.float32
    ) * HEAD_DIM ** (-0.5)
    return jnp.where(allowed, raw_scores, -jnp.inf)


def attend_forward(queries, keys_all, values_all, allowed, head_count):

    def one_head(triple):
        scores = head_scores(triple[0], triple[1], allowed)
        row_top = jnp.max(scores, -1, keepdims=True)
        expo_rows = jnp.exp(scores - row_top)
        row_total = jnp.sum(expo_rows, -1, keepdims=True)
        attn_probs = (expo_rows / row_total).astype(jnp.bfloat16)
        mixed_out = jnp.dot(attn_probs, triple[2], preferred_element_type=jnp.float32)
        return (mixed_out, (row_top + jnp.log(row_total))[:, 0])

    mixed_heads, log_total = lax.map(
        one_head,
        (
            split_heads(queries, head_count),
            split_heads(keys_all, head_count),
            split_heads(values_all, head_count),
        ),
    )
    return (join_heads(mixed_heads), log_total)


def attend_backward(queries, keys_all, values_all, grad_mixed, log_total, allowed, head_count):

    def one_head(group):
        query_h, keys_h, values_h, grad_h, total_h = group
        scores = head_scores(query_h, keys_h, allowed)
        attn_probs = jnp.exp(scores - total_h[:, None])
        probs_low = attn_probs.astype(jnp.bfloat16)
        grad_values = jnp.einsum("qk,qd->kd", probs_low, grad_h, preferred_element_type=jnp.float32)
        grad_probs = jnp.einsum("qd,kd->qk", grad_h, values_h, preferred_element_type=jnp.float32)
        grad_scores = (
            attn_probs * (grad_probs - jnp.sum(attn_probs * grad_probs, -1, keepdims=True))
        ).astype(jnp.bfloat16)
        grad_query = jnp.dot(
            grad_scores, keys_h, preferred_element_type=jnp.float32
        ) * HEAD_DIM ** (-0.5)
        grad_keys = jnp.einsum(
            "qk,qd->kd", grad_scores, query_h, preferred_element_type=jnp.float32
        ) * HEAD_DIM ** (-0.5)
        return (grad_query, grad_keys, grad_values)

    grad_query, grad_keys, grad_values = lax.map(
        one_head,
        (
            split_heads(queries, head_count),
            split_heads(keys_all, head_count),
            split_heads(values_all, head_count),
            split_heads(grad_mixed, head_count),
            log_total,
        ),
    )
    return (join_heads(grad_query), join_heads(grad_keys), join_heads(grad_values))


def shards(
    tokens,
    cotangent,
    segments,
    doc_batch,
    ln1_gain,
    ln1_bias,
    w_qkv,
    b_qv,
    w_out,
    b_out,
    ln2_gain,
    ln2_bias,
    w_fc,
    b_fc,
    w_proj,
    b_proj,
):
    row_count = tokens.shape[0]
    model_width = tokens.shape[1]
    head_cols = w_out.shape[1]
    head_count = head_cols // HEAD_DIM
    shard_index = lax.axis_index("fsdp")
    total_rows = row_count * lax.axis_size("fsdp")
    batch_ids = jnp.take(doc_batch, segments)
    onehot = (batch_ids[:, None] == jnp.arange(MB, dtype=jnp.int32)[None, :]).astype(jnp.float32)
    counts = lax.psum(jnp.sum(onehot, 0), "fsdp")
    row_weight = total_rows / (MB * jnp.sum(onehot * counts[None, :], 1))
    query_pos = shard_index * row_count + jnp.arange(row_count, dtype=jnp.int32)
    key_pos = (
        shard_index * row_count
        - REACH * row_count
        + jnp.arange((REACH + 1) * row_count, dtype=jnp.int32)
    )
    stream = tokens.astype(jnp.float32)
    stored = []
    for layer_at in range(LAYERS):
        weights = fetch_weights(w_qkv, w_out, w_fc, w_proj, layer_at)
        full_qkv, full_out, full_fc, full_proj = weights
        normed, unit_one, inv_one = norm_forward(stream, ln1_gain[layer_at], ln1_bias[layer_at])
        normed_low = normed.astype(jnp.bfloat16)
        bias_three = jnp.stack(
            [b_qv[layer_at, 0], jnp.zeros_like(b_qv[layer_at, 0]), b_qv[layer_at, 1]]
        )
        qkv = jnp.dot(
            normed_low,
            full_qkv.reshape(model_width, 3 * head_cols),
            preferred_element_type=jnp.float32,
        ).reshape(row_count, 3, head_cols)
        qkv_low = (qkv + bias_three[None]).astype(jnp.bfloat16)
        queries = qkv_low[:, 0]
        keys_here = qkv_low[:, 1]
        values_here = qkv_low[:, 2]
        keys_all, values_all, seg_keys = earlier_keys(keys_here, values_here, segments)
        allowed = (
            (segments[:, None] == seg_keys[None, :])
            & (key_pos[None, :] <= query_pos[:, None])
            & (key_pos[None, :] >= 0)
        )
        mixed, log_total = attend_forward(queries, keys_all, values_all, allowed, head_count)
        mixed_low = mixed.astype(jnp.bfloat16)
        middle = (
            stream
            + over_tp(jnp.dot(mixed_low, full_out, preferred_element_type=jnp.float32))
            + b_out[layer_at]
        )
        normed_two, unit_two, inv_two = norm_forward(middle, ln2_gain[layer_at], ln2_bias[layer_at])
        normed_two_low = normed_two.astype(jnp.bfloat16)
        hidden = (
            jnp.dot(normed_two_low, full_fc, preferred_element_type=jnp.float32) + b_fc[layer_at]
        )
        act_low = gelu_tanh(hidden).astype(jnp.bfloat16)
        stream = (
            middle
            + over_tp(jnp.dot(act_low, full_proj, preferred_element_type=jnp.float32))
            + b_proj[layer_at]
        )
        stored.append(
            (
                weights,
                unit_one,
                inv_one,
                normed_low,
                queries,
                keys_here,
                values_here,
                keys_all,
                values_all,
                allowed,
                log_total,
                mixed_low,
                unit_two,
                inv_two,
                normed_two_low,
                hidden,
                act_low,
            )
        )
    outputs = stream.astype(jnp.bfloat16)
    grad_state = cotangent.astype(jnp.float32) * row_weight[:, None]
    small_grads = [None] * LAYERS
    large_grads = [None] * LAYERS
    for layer_at in range(LAYERS - 1, -1, -1):
        (
            weights,
            unit_one,
            inv_one,
            normed_low,
            queries,
            keys_here,
            values_here,
            keys_kept,
            values_kept,
            allowed,
            log_total,
            mixed_low,
            unit_two,
            inv_two,
            normed_two_low,
            hidden,
            act_low,
        ) = stored[layer_at]
        full_qkv, full_out, full_fc, full_proj = fetch_weights(w_qkv, w_out, w_fc, w_proj, layer_at)
        grad_branch = grad_state.astype(jnp.bfloat16)
        grad_bproj = jnp.sum(grad_branch.astype(jnp.float32), 0)
        grad_wproj = jnp.einsum(
            "tf,td->fd", act_low, grad_branch, preferred_element_type=jnp.float32
        )
        grad_act = jnp.einsum(
            "td,fd->tf", grad_branch, full_proj, preferred_element_type=jnp.float32
        )
        gelu_value, gelu_pull = jax.vjp(gelu_tanh, hidden)
        grad_hidden = gelu_pull(grad_act)[0].astype(jnp.bfloat16)
        grad_bfc = jnp.sum(grad_hidden.astype(jnp.float32), 0)
        grad_wfc = jnp.einsum(
            "td,tf->df", normed_two_low, grad_hidden, preferred_element_type=jnp.float32
        )
        grad_normed_two = over_tp(
            jnp.einsum("tf,df->td", grad_hidden, full_fc, preferred_element_type=jnp.float32)
        )
        grad_middle, grad_gain_two, grad_bias_two = norm_backward(
            grad_normed_two, unit_two, inv_two, ln2_gain[layer_at]
        )
        grad_state = grad_state + grad_middle
        grad_attn = grad_state.astype(jnp.bfloat16)
        grad_bout = jnp.sum(grad_attn.astype(jnp.float32), 0)
        grad_wout = jnp.einsum(
            "tc,td->cd", mixed_low, grad_attn, preferred_element_type=jnp.float32
        )
        grad_mixed = jnp.einsum(
            "td,cd->tc", grad_attn, full_out, preferred_element_type=jnp.float32
        ).astype(jnp.bfloat16)
        keys_all, values_all = (keys_kept, values_kept)
        grad_query, grad_keys_all, grad_values_all = attend_backward(
            queries, keys_all, values_all, grad_mixed, log_total, allowed, head_count
        )
        grad_keys, grad_values = return_key_grads(grad_keys_all, grad_values_all, row_count)
        grad_qkv = jnp.stack([grad_query, grad_keys, grad_values], 1).astype(jnp.bfloat16)
        grad_bqv = jnp.sum(grad_qkv[:, 0::2].astype(jnp.float32), 0)
        grad_wqkv = jnp.einsum(
            "td,tcf->dcf", normed_low, grad_qkv, preferred_element_type=jnp.float32
        )
        grad_normed = over_tp(
            jnp.einsum("tcf,dcf->td", grad_qkv, full_qkv, preferred_element_type=jnp.float32)
        )
        grad_input, grad_gain_one, grad_bias_one = norm_backward(
            grad_normed, unit_one, inv_one, ln1_gain[layer_at]
        )
        grad_state = grad_state + grad_input
        large_grads[layer_at] = (
            lax.psum_scatter(grad_wqkv, "fsdp", scatter_dimension=0, tiled=True),
            lax.psum_scatter(grad_wout, "fsdp", scatter_dimension=1, tiled=True),
            lax.psum_scatter(grad_wfc, "fsdp", scatter_dimension=0, tiled=True),
            lax.psum_scatter(grad_wproj, "fsdp", scatter_dimension=1, tiled=True),
        )
        small_grads[layer_at] = lax.psum(
            (
                grad_gain_one,
                grad_bias_one,
                grad_bqv,
                grad_bout,
                grad_gain_two,
                grad_bias_two,
                grad_bfc,
                grad_bproj,
            ),
            "fsdp",
        )

    def stack_small(member):
        return jnp.stack([small_grads[layer_at][member] for layer_at in range(LAYERS)])

    def stack_large(member):
        return jnp.stack([large_grads[layer_at][member] for layer_at in range(LAYERS)])

    return (
        outputs,
        grad_state,
        stack_small(0),
        stack_small(1),
        stack_large(0),
        stack_small(2),
        stack_large(1),
        stack_small(3),
        stack_small(4),
        stack_small(5),
        stack_large(2),
        stack_small(6),
        stack_large(3),
        stack_small(7),
    )


def solution(mesh):
    placed = (
        P("fsdp", None),
        P("fsdp", None),
        P("fsdp"),
        P(),
        P(),
        P(),
        P(None, "fsdp", None, "tp"),
        P(None, None, "tp"),
        P(None, "tp", "fsdp"),
        P(),
        P(),
        P(),
        P(None, "fsdp", "tp"),
        P(None, "tp"),
        P(None, "tp", "fsdp"),
        P(),
    )
    return jax.shard_map(
        shards,
        mesh=mesh,
        in_specs=placed,
        out_specs=(
            P("fsdp", None),
            P("fsdp", None),
            P(),
            P(),
            P(None, "fsdp", None, "tp"),
            P(None, None, "tp"),
            P(None, "tp", "fsdp"),
            P(),
            P(),
            P(),
            P(None, "fsdp", "tp"),
            P(None, "tp"),
            P(None, "tp", "fsdp"),
            P(),
        ),
        check_vma=False,
    )
```

profile of v0, /device:TPU:0, one launch (start us, length us, event | category | flops | bytes accessed | tf_op | source)
XLA Modules:
  0.0 2614.1 jit_solution(8553252017848952046)
XLA Ops:
  157.8 59.7 %while.56 = (s32[]{:T(128)}, bf16[8,512,64]{1,2,0:T(8,128)(2,1)S(1)}, f32[8,512]{1,0:T(8,128)}, bf16[8,512,64]{2,1,0:T(8,128)(2,1)}, bf16[8,2560,64]{2,1,0:T(8,1...) while((s32[]{:T(128)}, ...), condition=%wide.region_5.6_spmd.clone, body=%wide.region_2.0_spmd.clone.sunk | while | flops 351272448 | bytes 17351304 | solution.py:128
  223.9 72.7 %all-reduce.11.cloned.1.call-done = f32[512,1024]{1,0:T(8,128)} async-done(((f32[512,1024]{1,0:T(8,128)}), f32[512,1024]{1,0:T(8,128)}) %all-reduce.11.cloned.1.call-update) | async-done | bytes 2097168 | tf_op jit(solution)/shard_map/psum | solution.py:51
  298.9 51.2 %all-gather.21.cloned.1.call-done = bf16[1,1024,2048]{2,1,0:T(8,128)(2,1)} async-done(((bf16[1,64,2048]{2,1,0:T(8,128)(2,1)}), bf16[1,1024,2048]{2,1,0:T(8,128)(2,1)}) %all-gather.21.cloned.1.call-update) | async-done | bytes 4194320 | tf_op jit(solution)/shard_map/all_gather | solution.py:58
  356.7 45.3 %all-gather.23.cloned.1.call-done = bf16[1,2048,1024]{1,2,0:T(8,128)(2,1)} async-done(((bf16[1,2048,64]{1,2,0:T(8,128)(2,1)}), bf16[1,2048,1024]{1,2,0:T(8,128)(2,1)}) %all-gather.23.cloned.1.call-update) | async-done | bytes 4194320 | tf_op jit(solution)/shard_map/all_gather | solution.py:59
  453.0 60.0 %all-reduce.13.cloned.1.call-done = f32[512,1024]{1,0:T(8,128)} async-done(((f32[512,1024]{1,0:T(8,128)}), f32[512,1024]{1,0:T(8,128)}) %all-reduce.13.cloned.1.call-update) | async-done | bytes 2097168 | tf_op jit(solution)/shard_map/psum | solution.py:51
  582.4 49.7 %while.57 = (s32[]{:T(128)}, bf16[8,512,64]{1,2,0:T(8,128)(2,1)S(1)}, f32[8,512]{1,0:T(8,128)S(1)}, bf16[8,512,64]{2,1,0:T(8,128)(2,1)}, bf16[8,2560,64]{2,1,0:T...) while((s32[]{:T(128)}, ...), condition=%wide.region_15.16_spmd.clone, body=%wide.region_12.15_spmd.clone.sunk | while | flops 351272448 | bytes 17351304 | solution.py:128
  637.2 71.5 %psum.179 = f32[3]{0:T(128)S(1)} all-reduce(f32[3]{0:T(128)S(1)} %convert_reduce_fusion.9), channel_id=1, replica_groups=mesh['fsdp'=16,'tp'=2] {'fsdp'}, use_global_device_ids=true, to_apply=%region_21.22 | all-reduce | flops 3 | bytes 24 | tf_op jit(solution)/shard_map/psum | solution.py:198
  739.7 49.3 %all-gather.29.cloned.1.call-done = bf16[1,1024,2048]{2,1,0:T(8,128)(2,1)} async-done(((bf16[1,64,2048]{2,1,0:T(8,128)(2,1)}), bf16[1,1024,2048]{2,1,0:T(8,128)(2,1)}) %all-gather.29.cloned.1.call-update) | async-done | bytes 4194320 | tf_op jit(solution)/shard_map/all_gather | solution.py:58
  855.7 61.4 %all-reduce.17.cloned.1.call-done = f32[512,1024]{1,0:T(8,128)} async-done(((f32[512,1024]{1,0:T(8,128)}), f32[512,1024]{1,0:T(8,128)}) %all-reduce.17.cloned.1.call-update) | async-done | bytes 2097168 | tf_op jit(solution)/shard_map/psum | solution.py:51
  933.9 101.1 %while.58 = (s32[]{:T(128)}, bf16[8,512,64]{1,2,0:T(8,128)(2,1)}, f32[8,2560,64]{1,2,0:T(8,128)}, f32[8,2560,64]{1,2,0:T(8,128)}, bf16[8,512,64]{2,1,0:T(8,128)(...) while((s32[]{:T(128)}, bf16[8,512,64]{1,2,0:T(8,128)(2,1)}, ...), condition=%wide.region_28.29_spmd.clone, body=%wide.region_26.28_spmd.clone.sunk | while | flops 856096256 | bytes 43296408 | solution.py:159
  1134.3 62.3 %collective-permute-done.23 = f32[512,512]{1,0:T(8,128)} collective-permute-done((f32[512,512]{1,0:T(8,128)}, f32[512,512]{1,0:T(8,128)}, u32[]{:S(2)}, u32[]{:S(2)}) %collective-permute-start.23) | collective-permute-done | bytes 1048608 | tf_op jit(solution)/shard_map/ppermute | solution.py:18
  1203.4 72.8 %all-reduce.19.cloned.1.call-done = f32[512,1024]{1,0:T(8,128)} async-done(((f32[512,1024]{1,0:T(8,128)}), f32[512,1024]{1,0:T(8,128)}) %all-reduce.19.cloned.1.call-update) | async-done | bytes 2097168 | tf_op jit(solution)/shard_map/psum | solution.py:51
  1295.4 62.6 %all-reduce.21.cloned.1.call-done = f32[512,1024]{1,0:T(8,128)} async-done(((f32[512,1024]{1,0:T(8,128)}), f32[512,1024]{1,0:T(8,128)}) %all-reduce.21.cloned.1.call-update) | async-done | bytes 2097168 | tf_op jit(solution)/shard_map/psum | solution.py:51
  1373.8 106.7 %while.59 = (s32[]{:T(128)}, bf16[8,512,64]{1,2,0:T(8,128)(2,1)}, f32[8,2560,64]{1,2,0:T(8,128)}, f32[8,2560,64]{1,2,0:T(8,128)}, bf16[8,512,64]{2,1,0:T(8,128)(...) while((s32[]{:T(128)}, bf16[8,512,64]{1,2,0:T(8,128)(2,1)}, ...), condition=%wide.region_37.38_spmd.clone, body=%wide.region_35.37_spmd.clone.sunk | while | flops 856096256 | bytes 43296408 | solution.py:159
  1581.6 60.6 %collective-permute-done.31 = f32[512,512]{1,0:T(8,128)} collective-permute-done((f32[512,512]{1,0:T(8,128)}, f32[512,512]{1,0:T(8,128)}, u32[]{:S(2)}, u32[]{:S(2)}) %collective-permute-start.31) | collective-permute-done | bytes 1048608 | tf_op jit(solution)/shard_map/ppermute | solution.py:18
  1661.9 105.1 %all-reduce.25.cloned.1.call-done = (f32[512,1024]{1,0:T(8,128)}, f32[512,1024]{1,0:T(8,128)}) async-done(((f32[512,1024]{1,0:T(8,128)}, f32[512,1024]{1,0:T(8,128)}), (f32[512,1024]{1,0:T(8,128)}, f32[512,1024]{1,0:T(8,128)})) %all-reduce.25.cloned.1.call-update) | async-done | bytes 4194320 | tf_op jit(solution)/shard_map/psum | solution.py:51
  1832.7 64.1 %reduce-scatter.13.cloned.1.call-done = f32[512,64]{0,1:T(8,128)} async-done(((f32[512,1024]{0,1:T(8,128)}), f32[512,64]{0,1:T(8,128)}) %reduce-scatter.13.cloned.1.call-update) | async-done | bytes 131088 | tf_op jit(solution)/shard_map/reduce_scatter | solution.py:343
  1903.8 88.4 %all-reduce.23.cloned.1.call-done = (f32[1,1024]{1,0:T(1,128)}, f32[1,1024]{1,0:T(1,128)}, f32[1,1024]{1,0:T(1,128)}, f32[1,1024]{1,0:T(1,128)}, f32[1,2,512]{2,...) async-done(((f32[1,1024]{1,0:T(1,128)}, f32[1,1024]{1,0:T(1,128)}, ...) | async-done | bytes 73744 | tf_op jit(solution)/shard_map/psum | solution.py:347
  2002.6 99.4 %reduce-scatter.23.cloned.1.call-done = f32[2048,64]{0,1:T(8,128)} async-done(((f32[2048,1024]{0,1:T(8,128)}), f32[2048,64]{0,1:T(8,128)}) %reduce-scatter.23.cloned.1.call-update) | async-done | bytes 524304 | tf_op jit(solution)/shard_map/reduce_scatter | solution.py:345
  2102.1 108.3 %reduce-scatter.21.cloned.1.call-done = f32[2048,64]{0,1:T(8,128)} async-done(((f32[2048,1024]{0,1:T(8,128)}), f32[2048,64]{0,1:T(8,128)}) %reduce-scatter.21.cloned.1.call-update) | async-done | bytes 524304 | tf_op jit(solution)/shard_map/reduce_scatter | solution.py:345
  2212.6 106.2 %reduce-scatter.19.cloned.1.call-done = f32[64,2048]{1,0:T(8,128)} async-done(((f32[1024,2048]{1,0:T(8,128)}), f32[64,2048]{1,0:T(8,128)}) %reduce-scatter.19.cloned.1.call-update) | async-done | bytes 524304 | tf_op jit(solution)/shard_map/reduce_scatter | solution.py:344
  2318.8 108.4 %reduce-scatter.17.cloned.1.call-done = f32[64,2048]{1,0:T(8,128)} async-done(((f32[1024,2048]{1,0:T(8,128)}), f32[64,2048]{1,0:T(8,128)}) %reduce-scatter.17.cloned.1.call-update) | async-done | bytes 524304 | tf_op jit(solution)/shard_map/reduce_scatter | solution.py:344
  2429.4 86.7 %reduce-scatter.11.cloned.1.call-done = f32[64,3,512]{2,0,1:T(8,128)} async-done(((f32[1024,3,512]{2,0,1:T(8,128)}), f32[64,3,512]{2,0,1:T(8,128)}) %reduce-scatter.11.cloned.1.call-update) | async-done | bytes 393232 | tf_op jit(solution)/shard_map/reduce_scatter | solution.py:342
  2516.1 88.8 %reduce-scatter.9.cloned.1.call-done = f32[64,3,512]{2,0,1:T(8,128)} async-done(((f32[1024,3,512]{2,0,1:T(8,128)}), f32[64,3,512]{2,0,1:T(8,128)}) %reduce-scatter.9.cloned.1.call-update) | async-done | bytes 393232 | tf_op jit(solution)/shard_map/reduce_scatter | solution.py:342
  (736 shorter events, 1072.1 us)
Async XLA Ops:
  9.0 208.5 %all-gather.19.cloned.1.call-start = ((), (), s32[]{:S(2)}) async-start(), calls=%async_computation.23 | async-start | bytes 1114112 | tf_op jit(solution)/shard_map/all_gather | solution.py:57
  79.4 217.2 %all-reduce.11.cloned.1.call-start = ((), (), s32[]{:S(2)}) async-start(), calls=%async_computation.8 | async-start | bytes 4194304 | tf_op jit(solution)/shard_map/psum | solution.py:51
  221.1 129.0 %all-gather.21.cloned.1.call-start = ((), (), s32[]{:S(2)}) async-start(), calls=%async_computation.24 | async-start | bytes 4456448 | tf_op jit(solution)/shard_map/all_gather | solution.py:58
  222.0 180.0 %all-gather.23.cloned.1.call-start = ((), (), s32[]{:S(2)}) async-start(), calls=%async_computation.25 | async-start | bytes 4456448 | tf_op jit(solution)/shard_map/all_gather | solution.py:59
  222.9 225.4 %all-gather.25.cloned.1.call-start = ((), (), s32[]{:S(2)}) async-start(), calls=%async_computation.26 | async-start | bytes 3342336 | tf_op jit(solution)/shard_map/all_gather | solution.py:56
  223.5 289.5 %all-reduce.13.cloned.1.call-start = ((), (), s32[]{:S(2)}) async-start(), calls=%async_computation.9 | async-start | bytes 4194304 | tf_op jit(solution)/shard_map/psum | solution.py:51
  409.6 222.5 %all-gather.27.cloned.1.call-start = ((), (), s32[]{:S(2)}) async-start(), calls=%async_computation.27 | async-start | bytes 1114112 | tf_op jit(solution)/shard_map/all_gather | solution.py:57
  552.3 183.9 %all-reduce.15.cloned.1.call-start = ((), (), s32[]{:S(2)}) async-start(), calls=%async_computation.10 | async-start | bytes 4194304 | tf_op jit(solution)/shard_map/psum | solution.py:51
  635.7 153.3 %all-gather.29.cloned.1.call-start = ((), (), s32[]{:S(2)}) async-start(), calls=%async_computation.28 | async-start | bytes 4456448 | tf_op jit(solution)/shard_map/all_gather | solution.py:58
  636.3 204.8 %all-gather.31.cloned.1.call-start = ((), (), s32[]{:S(2)}) async-start(), calls=%async_computation.29 | async-start | bytes 4456448 | tf_op jit(solution)/shard_map/all_gather | solution.py:59
  637.0 280.1 %all-reduce.17.cloned.1.call-start = ((), (), s32[]{:S(2)}) async-start(), calls=%async_computation.11 | async-start | bytes 4194304 | tf_op jit(solution)/shard_map/psum | solution.py:51
  855.5 420.7 %all-reduce.19.cloned.1.call-start = ((), (), s32[]{:S(2)}) async-start(), calls=%async_computation.12 | async-start | bytes 4194304 | tf_op jit(solution)/shard_map/psum | solution.py:51
  1093.4 103.2 %collective-permute-start.23 = (f32[512,512]{1,0:T(8,128)}, f32[512,512]{1,0:T(8,128)}, u32[]{:S(2)}, u32[]{:S(2)}) collective-permute-start(f32[512,512]{1,0:T(8,128)} %copy.157), channel_id=1, source_target_pairs={{8,0},{10,2},{12,4},{14,6},{16,8},{18,10},{20,12},{22,14},{24,16},... | collective-permute-start | bytes 3145736 | tf_op jit(solution)/shard_map/ppermute | solution.py:18
  1203.3 154.7 %all-reduce.21.cloned.1.call-start = ((), (), s32[]{:S(2)}) async-start(), calls=%async_computation.13 | async-start | bytes 4194304 | tf_op jit(solution)/shard_map/psum | solution.py:51
  1295.0 472.1 %all-reduce.25.cloned.1.call-start = ((), (), s32[]{:S(2)}) async-start(), calls=%async_computation.31 | async-start | bytes 8388608 | tf_op jit(solution)/shard_map/psum | solution.py:51
  1648.9 183.8 %reduce-scatter.15.cloned.1.call-start = ((), (), s32[]{:S(2)}) async-start(), calls=%async_computation.17 | async-start | bytes 2228224 | tf_op jit(solution)/shard_map/reduce_scatter | solution.py:343
  1653.6 243.3 %reduce-scatter.13.cloned.1.call-start = ((), (), s32[]{:S(2)}) async-start(), calls=%async_computation.16 | async-start | bytes 2228224 | tf_op jit(solution)/shard_map/reduce_scatter | solution.py:343
  1657.4 334.9 %all-reduce.23.cloned.1.call-start = ((), (), s32[]{:S(2)}) async-start(), calls=%async_computation.30 | async-start | bytes 147456 | tf_op jit(solution)/shard_map/psum | solution.py:347
  1770.2 331.9 %reduce-scatter.23.cloned.1.call-start = ((), (), s32[]{:S(2)}) async-start(), calls=%async_computation.21 | async-start | bytes 8912896 | tf_op jit(solution)/shard_map/reduce_scatter | solution.py:345
  1778.9 431.4 %reduce-scatter.21.cloned.1.call-start = ((), (), s32[]{:S(2)}) async-start(), calls=%async_computation.20 | async-start | bytes 8912896 | tf_op jit(solution)/shard_map/reduce_scatter | solution.py:345
  1787.9 530.8 %reduce-scatter.19.cloned.1.call-start = ((), (), s32[]{:S(2)}) async-start(), calls=%async_computation.19 | async-start | bytes 8912896 | tf_op jit(solution)/shard_map/reduce_scatter | solution.py:344
  1796.8 630.4 %reduce-scatter.17.cloned.1.call-start = ((), (), s32[]{:S(2)}) async-start(), calls=%async_computation.18 | async-start | bytes 8912896 | tf_op jit(solution)/shard_map/reduce_scatter | solution.py:344
  1805.0 711.1 %reduce-scatter.11.cloned.1.call-start = ((), (), s32[]{:S(2)}) async-start(), calls=%async_computation.15 | async-start | bytes 6684672 | tf_op jit(solution)/shard_map/reduce_scatter | solution.py:342
  1812.5 792.3 %reduce-scatter.9.cloned.1.call-start = ((), (), s32[]{:S(2)}) async-start(), calls=%async_computation.14 | async-start | bytes 6684672 | tf_op jit(solution)/shard_map/reduce_scatter | solution.py:342
  (152 other events, 8157.6 us)
Sparse Core Ops, SparseCore 0:
  10.8 48.1 all-gather.16
  79.5 36.9 all-gather.18
  221.2 75.2 all-reduce.10
  299.4 50.7 all-gather.20
  352.9 49.0 all-gather.22
  404.3 43.9 all-gather.24
  451.2 61.7 all-reduce.12
  552.4 45.2 all-gather.26
  635.8 100.3 all-reduce.14
  738.4 50.5 all-gather.28
  792.0 49.0 all-gather.30
  855.6 61.4 all-reduce.16
  1203.5 72.6 all-reduce.18
  1295.1 62.9 all-reduce.20
  1649.0 117.9 all-reduce.24
  1771.1 61.5 reduce-scatter.14
  1836.3 60.5 reduce-scatter.12
  1904.0 88.1 all-reduce.22
  1996.3 105.6 reduce-scatter.22
  2106.0 104.3 reduce-scatter.20
  2214.4 104.3 reduce-scatter.18
  2322.8 104.3 reduce-scatter.16
  2431.1 84.9 reduce-scatter.10
  2520.4 84.4 reduce-scatter.8
where the time goes:
time: 2630 us; the launch traced here: 2610 us
  waiting for transfers between devices  1720 us (65%)
  matrix products  403 us (15%)
  local copies, waits for them, and re-layouts  200 us (8%)
  starting transfers between devices  103 us (4%)
  other arithmetic  95.5 us (4%)
  blocking collectives  71.5 us (3%)
    psum x7, waiting for transfers between devices, over_tp(): return lax.psum(partial_value, 'tp')  462 us
    ppermute x36, waiting for transfers between devices, passed_along(): return lax.ppermute(shard, axis, pairs)  229 us
    reduce_scatter x2, waiting for transfers between devices, shards(): lax.psum_scatter(grad_wfc, 'fsdp', scatter_dimension=0, tiled=True)  215 us
    reduce_scatter x2, waiting for transfers between devices, shards(): lax.psum_scatter(grad_wproj, 'fsdp', scatter_dimension=1, tiled=True)  208 us
    reduce_scatter x2, waiting for transfers between devices, shards(): lax.psum_scatter(grad_wqkv, 'fsdp', scatter_dimension=0, tiled=True)  175 us
    dot_general x32, matrix products, head_scores(): jnp.einsum('qd,kd->qk', query_h, keys_h, preferred_element_type=jnp.float32)  107 us
    ppermute x36, starting transfers between devices, passed_along(): return lax.ppermute(shard, axis, pairs)  101 us
    all_gather x2, waiting for transfers between devices, fetch_weights(): lax.all_gather(w_fc[layer_at], 'fsdp', axis=0, tiled=True)  101 us
  transfers between devices with their start and end apart: 60, of which 34 were waited for; matrix products, arithmetic and copies ran while one was open for 14% of the time, Pallas kernels for 0%

commit v1 on v0

v1 whole, which is shorter than its diff:
```python
import functools

import jax
import jax.numpy as jnp
from jax import lax
from jax.experimental import pallas as pl
from jax.experimental.pallas import tpu as pltpu
from jax.sharding import PartitionSpec as P

HEAD_DIM = 64
LAYERS = 2
MB = 3
REACH = 4

EPS = 1e-05
GROUP = REACH
QB = 256
KB = 256
NEG = -1e30
F32 = jnp.float32
BF16 = jnp.bfloat16
VMEM_BYTES = 56 * 1024 * 1024
LAST = (((1,), (1,)), ((), ()))
FIRST = (((0,), (0,)), ((), ()))


def dot(left, right):
    return jnp.dot(left, right, preferred_element_type=F32)


def dot_last(left, right):
    return lax.dot_general(left, right, LAST, preferred_element_type=F32)


def shape(dims, dtype):
    return jax.ShapeDtypeStruct(dims, dtype)


def whole(dims):
    return pl.BlockSpec(dims, lambda *_: (0,) * len(dims))


def run_kernel(body, grid, scalars, ins, outs, scratch=(), flops=0, moved=0):
    return pl.pallas_call(
        body,
        grid_spec=pltpu.PrefetchScalarGridSpec(
            num_scalar_prefetch=1,
            grid=grid,
            in_specs=[spec for spec, _ in ins],
            out_specs=[spec for spec, _ in outs],
            scratch_shapes=list(scratch),
        ),
        out_shape=[out for _, out in outs],
        compiler_params=pltpu.CompilerParams(
            vmem_limit_bytes=VMEM_BYTES, dimension_semantics=("arbitrary",) * len(grid)
        ),
        cost_estimate=pl.CostEstimate(flops=flops, bytes_accessed=moved, transcendentals=0),
    )(scalars, *[array for _, array in ins])


def each_rows(count, chunk, body):
    def step(at, carry):
        body(pl.ds(pl.multiple_of(at * chunk, chunk), chunk))
        return carry

    lax.fori_loop(0, count // chunk, step, 0)


def norm_parts(rows):
    centred = rows - jnp.mean(rows, -1, keepdims=True)
    inv_scale = lax.rsqrt(jnp.mean(centred * centred, -1, keepdims=True) + EPS)
    return centred * inv_scale, inv_scale


def norm_pull(grad_rows, unit_rows, inv_scale, gain):
    scaled = grad_rows * gain
    return inv_scale * (
        scaled
        - jnp.mean(scaled, -1, keepdims=True)
        - unit_rows * jnp.mean(scaled * unit_rows, -1, keepdims=True)
    )


def eight_rows(rows):
    return jnp.sum(rows.reshape(rows.shape[0] // 8, 8, rows.shape[1]), 0)


def norm_qkv_body(summed, sc, *refs):
    if summed:
        base, own, got, badd, gain, bias, w, bq, stream, low, piece = refs
    else:
        base, gain, bias, w, bq, stream, low, piece = refs

    @pl.when(pl.program_id(0) == 0)
    def _():
        def rows(at):
            value = base[at, :].astype(F32)
            if summed:
                value = value + (own[at, :].astype(F32) + got[at, :].astype(F32)) + badd[...]
            stream[at, :] = value
            unit, _ = norm_parts(value)
            low[at, :] = (unit * gain[...] + bias[...]).astype(BF16)

        each_rows(base.shape[0], 32, rows)

    piece[0] = (dot(low[...], w[...]) + bq[...]).astype(BF16)


def norm_qkv(sc, base, sums, gain, bias, weights, first_block, bq):
    rows, width = base.shape
    cols = bq.shape[1] // GROUP
    ins = [(whole(base.shape), base)]
    if sums is not None:
        own, got, badd = sums
        ins += [(whole(own.shape), own), (whole(got.shape), got), (whole(badd.shape), badd)]
    ins += [
        (whole(gain.shape), gain),
        (whole(bias.shape), bias),
        (pl.BlockSpec((width, cols), lambda s, sc: (0, first_block + (sc[0] ^ s))), weights),
        (pl.BlockSpec((1, cols), lambda s, sc: (0, sc[0] ^ s)), bq),
    ]
    outs = [
        (whole((rows, width)), shape((rows, width), F32)),
        (whole((rows, width)), shape((rows, width), BF16)),
        (pl.BlockSpec((1, rows, cols), lambda s, sc: (s, 0, 0)), shape((GROUP, rows, cols), BF16)),
    ]
    return run_kernel(
        functools.partial(norm_qkv_body, sums is not None),
        (GROUP,),
        sc,
        ins,
        outs,
        flops=2 * rows * width * cols * GROUP,
        moved=rows * width * 12 + width * cols * GROUP * 2,
    )


def out_proj_body(sc, p0, p1, p2, p3, w, full, partial):
    cols = p1.shape[1]
    for s, piece in enumerate((p0, p1, p2, p3)):
        value = piece[0] if s == 0 else piece[...]
        full[:, pl.ds(pl.multiple_of((sc[0] ^ s) * cols, cols), cols)] = value
    tile = 256
    for at in range(0, partial.shape[1], tile):
        partial[:, at : at + tile] = dot_last(full[...], w[at : at + tile, :]).astype(BF16)


def out_proj(sc, mixed_all, got, weights):
    rows, cols = got[0].shape
    width = weights.shape[0]
    ins = [(whole((1, rows, cols)), mixed_all)]
    ins += [(whole((rows, cols)), piece) for piece in got]
    ins += [(whole((width, GROUP * cols)), weights)]
    outs = [
        (whole((rows, GROUP * cols)), shape((rows, GROUP * cols), BF16)),
        (whole((rows, width)), shape((rows, width), BF16)),
    ]
    return run_kernel(
        out_proj_body,
        (1,),
        sc,
        ins,
        outs,
        flops=2 * rows * width * GROUP * cols,
        moved=rows * width * 4 + width * GROUP * cols * 2,
    )


def gelu_rows(value):
    return 0.5 * value * (1.0 + jnp.tanh(0.7978845608028654 * (value + 0.044715 * value * value * value)))


def gelu_slope(value):
    square = value * value
    top = jnp.tanh(0.7978845608028654 * (value + 0.044715 * square * value))
    inner = 0.7978845608028654 * (1.0 + 3.0 * 0.044715 * square)
    return 0.5 * (1.0 + top) + 0.5 * value * (1.0 - top * top) * inner


def feed_body(
    sc, base, own, got, badd, gain, bias, fc, bfc, proj, middle, low, hidden, act, partial, total
):
    at_chunk = pl.program_id(0)

    @pl.when(at_chunk == 0)
    def _():
        def rows(at):
            value = base[at, :] + (own[at, :].astype(F32) + got[at, :].astype(F32)) + badd[...]
            middle[at, :] = value
            unit, _ = norm_parts(value)
            low[at, :] = (unit * gain[...] + bias[...]).astype(BF16)

        each_rows(base.shape[0], 32, rows)

    hidden[...] = dot(low[...], fc[...]) + bfc[...]

    def rows_act(at):
        act[at, :] = gelu_rows(hidden[at, :]).astype(BF16)

    each_rows(hidden.shape[0], 32, rows_act)
    part = dot_last(act[...], proj[...])

    @pl.when(at_chunk == 0)
    def _():
        total[...] = part

    @pl.when(at_chunk > 0)
    def _():
        total[...] += part

    @pl.when(at_chunk == pl.num_programs(0) - 1)
    def _():
        partial[...] = total[...].astype(BF16)


def feed(sc, base, own, got, badd, gain, bias, weights, fc_at, proj_at, bfc):
    rows, width = base.shape
    units, chunk = bfc.shape[1], 512
    ins = [
        (whole(base.shape), base),
        (whole(own.shape), own),
        (whole(got.shape), got),
        (whole(badd.shape), badd),
        (whole(gain.shape), gain),
        (whole(bias.shape), bias),
        (pl.BlockSpec((width, chunk), lambda j, sc: (0, fc_at // chunk + j)), weights),
        (pl.BlockSpec((1, chunk), lambda j, sc: (0, j)), bfc),
        (pl.BlockSpec((width, chunk), lambda j, sc: (0, proj_at // chunk + j)), weights),
    ]
    outs = [
        (whole((rows, width)), shape((rows, width), F32)),
        (whole((rows, width)), shape((rows, width), BF16)),
        (pl.BlockSpec((rows, chunk), lambda j, sc: (0, j)), shape((rows, units), F32)),
        (pl.BlockSpec((rows, chunk), lambda j, sc: (0, j)), shape((rows, units), BF16)),
        (whole((rows, width)), shape((rows, width), BF16)),
    ]
    return run_kernel(
        feed_body,
        (units // chunk,),
        sc,
        ins,
        outs,
        scratch=[pltpu.VMEM((rows, width), F32)],
        flops=4 * rows * width * units,
        moved=rows * width * 16 + width * units * 4 + rows * units * 6,
    )


def feed_pull_body(sc, grad, hidden, proj, fc, low, sum_low, slope_grad, sum_hidden, partial, total, grad_act):
    at_chunk = pl.program_id(0)

    @pl.when(at_chunk == 0)
    def _():
        sum_low[...] = jnp.zeros_like(sum_low)

        def rows(at):
            value = grad[at, :].astype(BF16)
            low[at, :] = value
            sum_low[...] += eight_rows(value.astype(F32))

        each_rows(grad.shape[0], 32, rows)

    grad_act[...] = dot(low[...], proj[...])
    sum_hidden[...] = jnp.zeros_like(sum_hidden)

    def rows_slope(at):
        value = (grad_act[at, :] * gelu_slope(hidden[at, :])).astype(BF16)
        slope_grad[at, :] = value
        sum_hidden[...] += eight_rows(value.astype(F32))

    each_rows(grad.shape[0], 32, rows_slope)
    part = dot_last(slope_grad[...], fc[...])

    @pl.when(at_chunk == 0)
    def _():
        total[...] = part

    @pl.when(at_chunk > 0)
    def _():
        total[...] += part

    @pl.when(at_chunk == pl.num_programs(0) - 1)
    def _():
        partial[...] = total[...].astype(BF16)


def feed_pull(sc, grad, hidden, weights, fc_at, proj_at):
    rows, width = grad.shape
    units, chunk = hidden.shape[1], 512
    ins = [
        (whole(grad.shape), grad),
        (pl.BlockSpec((rows, chunk), lambda j, sc: (0, j)), hidden),
        (pl.BlockSpec((width, chunk), lambda j, sc: (0, proj_at // chunk + j)), weights),
        (pl.BlockSpec((width, chunk), lambda j, sc: (0, fc_at // chunk + j)), weights),
    ]
    outs = [
        (whole((rows, width)), shape((rows, width), BF16)),
        (whole((8, width)), shape((8, width), F32)),
        (pl.BlockSpec((rows, chunk), lambda j, sc: (0, j)), shape((rows, units), BF16)),
        (pl.BlockSpec((8, chunk), lambda j, sc: (0, j)), shape((8, units), F32)),
        (whole((rows, width)), shape((rows, width), BF16)),
    ]
    return run_kernel(
        feed_pull_body,
        (units // chunk,),
        sc,
        ins,
        outs,
        scratch=[pltpu.VMEM((rows, width), F32), pltpu.VMEM((rows, chunk), F32)],
        flops=4 * rows * width * units,
        moved=rows * width * 8 + width * units * 4 + rows * units * 6,
    )


def norm_pull_rows(at, grad, own, got, inputs, gain, grad_new, sum_gain, sum_bias):
    grad_rows = own[at, :].astype(F32) + got[at, :].astype(F32)
    unit, inv_scale = norm_parts(inputs[at, :])
    value = grad[at, :] + norm_pull(grad_rows, unit, inv_scale, gain[...])
    grad_new[at, :] = value
    sum_gain[...] += eight_rows(grad_rows * unit)
    sum_bias[...] += eight_rows(grad_rows)
    return value


def mid_pull_body(sc, grad, own, got, inputs, gain, w, grad_new, low, pieces, sum_gain, sum_bias, sum_low, mixed):
    for total in (sum_gain, sum_bias, sum_low):
        total[...] = jnp.zeros_like(total)

    def rows(at):
        value = norm_pull_rows(at, grad, own, got, inputs, gain, grad_new, sum_gain, sum_bias)
        value = value.astype(BF16)
        low[at, :] = value
        sum_low[...] += eight_rows(value.astype(F32))

    each_rows(grad.shape[0], 32, rows)
    mixed[...] = dot(low[...], w[...]).astype(BF16)
    cols = pieces.shape[2]
    for s in range(GROUP):
        pieces[s] = mixed[:, pl.ds(pl.multiple_of((sc[0] ^ s) * cols, cols), cols)]


def mid_pull(sc, grad, own, got, inputs, gain, weights, out_cols):
    rows, width = grad.shape
    cols = out_cols // GROUP
    ins = [
        (whole(grad.shape), grad),
        (whole(own.shape), own),
        (whole(got.shape), got),
        (whole(inputs.shape), inputs),
        (whole(gain.shape), gain),
        (whole((width, out_cols)), weights),
    ]
    sums = (whole((8, width)), shape((8, width), F32))
    outs = [
        (whole((rows, width)), shape((rows, width), F32)),
        (whole((rows, width)), shape((rows, width), BF16)),
        (whole((GROUP, rows, cols)), shape((GROUP, rows, cols), BF16)),
        sums,
        sums,
        sums,
    ]
    return run_kernel(
        mid_pull_body,
        (1,),
        sc,
        ins,
        outs,
        scratch=[pltpu.VMEM((rows, out_cols), BF16)],
        flops=2 * rows * width * out_cols,
        moved=rows * width * 18 + width * out_cols * 2,
    )


def qkv_pull_body(sc, p0, p1, p2, p3, w, full, partial, sums):
    cols = p1.shape[1]
    for s, piece in enumerate((p0, p1, p2, p3)):
        value = piece[0] if s == 0 else piece[...]
        full[:, pl.ds(pl.multiple_of((sc[0] ^ s) * cols, cols), cols)] = value
    sums[...] = jnp.zeros_like(sums)

    def rows(at):
        sums[...] += eight_rows(full[at, :].astype(F32))

    each_rows(full.shape[0], 32, rows)
    tile = 256
    for at in range(0, partial.shape[1], tile):
        partial[:, at : at + tile] = dot_last(full[...], w[at : at + tile, :]).astype(BF16)


def qkv_pull(sc, own, got, weights, block_at):
    rows, cols = got[0].shape
    width, total = weights.shape[0], GROUP * cols
    ins = [(whole((1, rows, cols)), own)]
    ins += [(whole((rows, cols)), piece) for piece in got]
    ins += [(pl.BlockSpec((width, total), lambda j, sc: (0, block_at)), weights)]
    outs = [
        (whole((rows, total)), shape((rows, total), BF16)),
        (whole((rows, width)), shape((rows, width), BF16)),
        (whole((8, total)), shape((8, total), F32)),
    ]
    return run_kernel(
        qkv_pull_body,
        (1,),
        sc,
        ins,
        outs,
        flops=2 * rows * width * total,
        moved=rows * width * 6 + width * total * 2,
    )


def first_pull_body(sc, grad, own, got, inputs, gain, grad_new, sum_gain, sum_bias):
    for total in (sum_gain, sum_bias):
        total[...] = jnp.zeros_like(total)

    def rows(at):
        norm_pull_rows(at, grad, own, got, inputs, gain, grad_new, sum_gain, sum_bias)

    each_rows(grad.shape[0], 32, rows)


def first_pull(sc, grad, own, got, inputs, gain):
    rows, width = grad.shape
    arrays = (grad, own, got, inputs, gain)
    sums = (whole((8, width)), shape((8, width), F32))
    return run_kernel(
        first_pull_body,
        (1,),
        sc,
        [(whole(array.shape), array) for array in arrays],
        [(whole((rows, width)), shape((rows, width), F32)), sums, sums],
        moved=rows * width * 16,
    )


def weight_pull_body(first_steps, sc, x0, g0, x1, g1, out, flipped):
    at = pl.program_id(0)

    @pl.when(at == 0)
    def _():
        flipped[...] = x0[...].T

    @pl.when(at == first_steps)
    def _():
        flipped[...] = x1[...].T

    @pl.when(at < first_steps)
    def _():
        out[...] = dot(flipped[...], g0[...]).astype(BF16)

    @pl.when(at >= first_steps)
    def _():
        out[...] = dot(flipped[...], g1[...]).astype(BF16)


def weight_pull(sc, x0, g0, x1, g1):
    rows, width = x0.shape
    chunk = 512
    n0, n1 = g0.shape[1] // chunk, g1.shape[1] // chunk
    ins = [
        (whole(x0.shape), x0),
        (pl.BlockSpec((rows, chunk), lambda j, sc: (0, jnp.minimum(j, n0 - 1))), g0),
        (whole(x1.shape), x1),
        (pl.BlockSpec((rows, chunk), lambda j, sc: (0, jnp.maximum(j - n0, 0))), g1),
    ]
    outs = [
        (
            pl.BlockSpec((width, chunk), lambda j, sc: (0, j)),
            shape((width, (n0 + n1) * chunk), BF16),
        )
    ]
    return run_kernel(
        functools.partial(weight_pull_body, n0),
        (n0 + n1,),
        sc,
        ins,
        outs,
        scratch=[pltpu.VMEM((width, rows), BF16)],
        flops=2 * rows * width * (n0 + n1) * chunk,
        moved=rows * width * 4 + (rows + width) * (n0 + n1) * chunk * 2,
    )[0]


def doc_start_rows(sc, docs, positions):
    start = jnp.zeros_like(positions)
    for d in range(docs):
        first = sc[2 + d]
        start = jnp.where(first <= positions, jnp.maximum(start, first), start)
    return start


def doc_start_one(sc, docs, position):
    start = jnp.int32(0)
    for d in range(docs):
        first = sc[2 + d]
        start = jnp.where(first <= position, jnp.maximum(start, first), start)
    return start


def query_rows(sc, docs, block):
    first = sc[1] + block * QB
    position = first + lax.broadcasted_iota(jnp.int32, (1, QB), 1)
    start = doc_start_rows(sc, docs, position)
    return (
        jnp.concatenate([position, position], 1),
        jnp.concatenate([start, start], 1),
        doc_start_one(sc, docs, first),
    )


def head_stack(rows, scale):
    value = rows.astype(F32)
    if scale != 1.0:
        value = value * scale
    lane = lax.broadcasted_iota(jnp.int32, value.shape, 1)
    return jnp.concatenate(
        [jnp.where(lane < HEAD_DIM, value, 0.0), jnp.where(lane >= HEAD_DIM, value, 0.0)], 0
    ).astype(BF16)


def place_rows(sc, s, rows):
    return pl.ds(pl.multiple_of((sc[0] ^ s) * rows, rows), rows)


def spread(sc, pieces, first_col, cols, straight=None, flipped=None):
    for s, piece in enumerate(pieces):
        value = piece[s] if len(piece.shape) == 3 and piece.shape[0] > 1 else None
        if value is None:
            value = piece[0] if len(piece.shape) == 3 else piece[...]
        value = value[:, first_col : first_col + cols]
        at = place_rows(sc, s, value.shape[0])
        if straight is not None:
            straight[at, :] = value
        if flipped is not None:
            flipped[:, at] = value.T


def block_at(block, size):
    return pl.ds(pl.multiple_of(block * size, size), size)


def masked_scores(keys, queries, first_key, position, start):
    scores = dot_last(keys, queries)
    key_at = first_key + lax.broadcasted_iota(jnp.int32, (KB, 1), 0)
    return jnp.where((key_at >= start) & (key_at <= position), scores, NEG)


def flash_step(keys_ref, values_ref, queries, block, first_key, position, start, acc, carry):
    top, total = carry
    scores = masked_scores(keys_ref[block_at(block, KB), :], queries, first_key, position, start)
    top_new = jnp.maximum(top, jnp.max(scores, 0, keepdims=True))
    expo = jnp.exp(scores - top_new)
    shrink = jnp.exp(top - top_new)
    total = total * shrink + jnp.sum(expo, 0, keepdims=True)
    expo = expo.astype(BF16)
    for h in range(2):
        lanes = slice(h * QB, (h + 1) * QB)
        rows = slice(h * HEAD_DIM, (h + 1) * HEAD_DIM)
        values = values_ref[rows, block_at(block, KB)]
        acc[rows, :] = acc[rows, :] * shrink[:, lanes] + dot(values, expo[:, lanes])
    return top_new, total


def attend_own_body(docs, sc, p0, p1, p2, p3, acc, top_ref, total_ref, q_all, k_all, v_flip):
    block = pl.program_id(0)
    cols = q_all.shape[1]

    @pl.when(block == 0)
    def _():
        pieces = (p0, p1, p2, p3)
        spread(sc, pieces, 0, cols, straight=q_all)
        spread(sc, pieces, cols, cols, straight=k_all)
        spread(sc, pieces, 2 * cols, cols, flipped=v_flip)

    position, start, lowest = query_rows(sc, docs, block)
    queries = head_stack(q_all[block_at(block, QB), :], HEAD_DIM**-0.5)
    acc[...] = jnp.zeros_like(acc)
    least = jnp.maximum(lowest - sc[1], 0) // KB
    last = ((block + 1) * QB - 1) // KB

    def step(back, carry):
        at = last - back
        return flash_step(
            k_all, v_flip, queries, at, sc[1] + at * KB, position, start, acc, carry
        )

    top, total = lax.fori_loop(
        0,
        last - least + 1,
        step,
        (jnp.full((1, 2 * QB), NEG, F32), jnp.zeros((1, 2 * QB), F32)),
    )
    for h in range(2):
        top_ref[h : h + 1, :] = top[:, h * QB : (h + 1) * QB]
        total_ref[h : h + 1, :] = total[:, h * QB : (h + 1) * QB]


def piece_specs(pieces):
    out = []
    for array in pieces:
        dims = array.shape
        out.append((whole((1,) + dims[1:]) if len(dims) == 3 else whole(dims), array))
    return out


def attend_own(sc, docs, pieces):
    rows, cols = pieces[1].shape[0], pieces[1].shape[1] // 3
    span = GROUP * rows
    stat = (pl.BlockSpec((8, QB), lambda j, sc: (0, j)), shape((8, span), F32))
    return run_kernel(
        functools.partial(attend_own_body, docs),
        (span // QB,),
        sc,
        piece_specs(pieces),
        [(pl.BlockSpec((cols, QB), lambda j, sc: (0, j)), shape((cols, span), F32)), stat, stat],
        scratch=[
            pltpu.VMEM((span, cols), BF16),
            pltpu.VMEM((span, cols), BF16),
            pltpu.VMEM((cols, span), BF16),
        ],
        flops=span * span * cols * 2,
        moved=span * cols * 10,
    )


def attend_back_body(
    docs, sc, p0, p1, p2, p3, kv, acc_in, top_in, total_in, mixed, out, log_total, q_all, k_all, v_flip, acc
):
    block = pl.program_id(0)
    cols = q_all.shape[1]
    span = q_all.shape[0]

    @pl.when(block == 0)
    def _():
        spread(sc, (p0, p1, p2, p3), 0, cols, straight=q_all)
        spread(sc, (kv,) * GROUP, 0, cols, straight=k_all)
        spread(sc, (kv,) * GROUP, cols, cols, flipped=v_flip)

    position, start, lowest = query_rows(sc, docs, block)
    queries = head_stack(q_all[block_at(block, QB), :], HEAD_DIM**-0.5)
    acc[...] = acc_in[...]
    before = sc[1] - span
    least = jnp.maximum(lowest - before, 0) // KB

    def step(at, carry):
        return flash_step(k_all, v_flip, queries, at, before + at * KB, position, start, acc, carry)

    top, total = lax.fori_loop(
        least,
        span // KB,
        step,
        (
            jnp.concatenate([top_in[h : h + 1, :] for h in range(2)], 1),
            jnp.concatenate([total_in[h : h + 1, :] for h in range(2)], 1),
        ),
    )
    sums = top + jnp.log(total)
    share = 1.0 / total
    parts = []
    for h in range(2):
        lanes = slice(h * QB, (h + 1) * QB)
        log_total[h : h + 1, :] = sums[:, lanes]
        parts.append(acc[h * HEAD_DIM : (h + 1) * HEAD_DIM, :] * share[:, lanes])
    value = jnp.concatenate(parts, 0).T
    out[...] = value
    mixed[0] = value.astype(BF16)


def slot_spec(rows, cols):
    per = rows // QB
    return pl.BlockSpec((1, QB, cols), lambda j, sc: ((j // per) ^ sc[0], j % per, 0))


def attend_back(sc, docs, pieces, kv, acc, top, total):
    rows, cols = pieces[1].shape[0], pieces[1].shape[1] // 3
    span = GROUP * rows
    stat = pl.BlockSpec((8, QB), lambda j, sc: (0, j))
    ins = piece_specs(pieces) + [
        (whole(kv.shape), kv),
        (pl.BlockSpec((cols, QB), lambda j, sc: (0, j)), acc),
        (stat, top),
        (stat, total),
    ]
    outs = [
        (slot_spec(rows, cols), shape((GROUP, rows, cols), BF16)),
        (pl.BlockSpec((QB, cols), lambda j, sc: (j, 0)), shape((span, cols), F32)),
        (stat, shape((8, span), F32)),
    ]
    return run_kernel(
        functools.partial(attend_back_body, docs),
        (span // QB,),
        sc,
        ins,
        outs,
        scratch=[
            pltpu.VMEM((span, cols), BF16),
            pltpu.VMEM((span, cols), BF16),
            pltpu.VMEM((cols, span), BF16),
            pltpu.VMEM((cols, QB), F32),
        ],
        flops=span * span * cols * 2,
        moved=span * cols * 16,
    )


def pull_step(block, first_key, position, start, queries, grads, log_rows, delta, refs):
    k_all, v_all, k_flip, grad_k, grad_v, grad_q = refs
    at = block_at(block, KB)
    scores = masked_scores(k_all[at, :], queries, first_key, position, start)
    probs = jnp.exp(scores - log_rows)
    grad_probs = dot_last(v_all[at, :], grads)
    grad_scores = (probs * (grad_probs - delta)).astype(BF16)
    grad_v[at, :] += dot(probs.astype(BF16), grads)
    grad_k[at, :] += dot(grad_scores, queries)
    for h in range(2):
        rows = slice(h * HEAD_DIM, (h + 1) * HEAD_DIM)
        grad_q[rows, :] += dot(k_flip[rows, at], grad_scores[:, h * QB : (h + 1) * QB])


def pull_rows(block, q_all, g_all, out, log_total):
    queries = head_stack(q_all[block_at(block, QB), :], HEAD_DIM**-0.5)
    grad_rows = g_all[block_at(block, QB), :]
    grads = head_stack(grad_rows, 1.0)
    flipped = (grad_rows.astype(F32) * out[...]).T
    delta = jnp.concatenate(
        [
            jnp.sum(flipped[h * HEAD_DIM : (h + 1) * HEAD_DIM, :], 0, keepdims=True)
            for h in range(2)
        ],
        1,
    )
    log_rows = jnp.concatenate([log_total[h : h + 1, :] for h in range(2)], 1)
    return queries, grads, log_rows, delta


def pull_back_body(
    docs, sc, p0, p1, p2, p3, g0, g1, g2, g3, kv, out, log_total, grad_q, grad_kv,
    q_all, g_all, k_all, v_all, k_flip, grad_k, grad_v
):
    block = pl.program_id(0)
    span, cols = q_all.shape
    before = sc[1] - span

    @pl.when(block == 0)
    def _():
        spread(sc, (p0, p1, p2, p3), 0, cols, straight=q_all)
        spread(sc, (g0, g1, g2, g3), 0, cols, straight=g_all)
        spread(sc, (kv,) * GROUP, 0, cols, straight=k_all, flipped=k_flip)
        spread(sc, (kv,) * GROUP, cols, cols, straight=v_all)
        grad_k[...] = jnp.zeros_like(grad_k)
        grad_v[...] = jnp.zeros_like(grad_v)

    grad_q[...] = jnp.zeros_like(grad_q)
    position, start, lowest = query_rows(sc, docs, block)

    @pl.when(lowest < sc[1])
    def _():
        queries, grads, log_rows, delta = pull_rows(block, q_all, g_all, out, log_total)

        def step(at, carry):
            pull_step(
                at,
                before + at * KB,
                position,
                start,
                queries,
                grads,
                log_rows,
                delta,
                (k_all, v_all, k_flip, grad_k, grad_v, grad_q),
            )
            return carry

        lax.fori_loop(jnp.maximum(lowest - before, 0) // KB, span // KB, step, 0)

    @pl.when(block == pl.num_programs(0) - 1)
    def _():
        for s in range(GROUP):
            at = place_rows(sc, s, span // GROUP)
            grad_kv[s, :, :cols] = grad_k[at, :].astype(BF16)
            grad_kv[s, :, cols:] = grad_v[at, :].astype(BF16)


def pull_back(sc, docs, pieces, grads, kv, out, log_total):
    rows, cols = pieces[1].shape[0], pieces[1].shape[1] // 3
    span = GROUP * rows
    ins = piece_specs(pieces) + piece_specs(grads) + [
        (whole(kv.shape), kv),
        (pl.BlockSpec((QB, cols), lambda j, sc: (j, 0)), out),
        (pl.BlockSpec((8, QB), lambda j, sc: (0, j)), log_total),
    ]
    outs = [
        (pl.BlockSpec((cols, QB), lambda j, sc: (0, j)), shape((cols, span), F32)),
        (whole((GROUP, rows, 2 * cols)), shape((GROUP, rows, 2 * cols), BF16)),
    ]
    low = pltpu.VMEM((span, cols), BF16)
    return run_kernel(
        functools.partial(pull_back_body, docs),
        (span // QB,),
        sc,
        ins,
        outs,
        scratch=[
            low,
            low,
            low,
            low,
            pltpu.VMEM((cols, span), BF16),
            pltpu.VMEM((span, cols), F32),
            pltpu.VMEM((span, cols), F32),
        ],
        flops=span * span * cols * 4,
        moved=span * cols * 20,
    )


def pull_own_body(
    docs, sc, p0, p1, p2, p3, g0, g1, g2, g3, out, log_total, grad_q_in, grad_q_out, grad_kv,
    q_all, g_all, k_all, v_all, k_flip, grad_k, grad_v, grad_q
):
    block = pl.program_id(0)
    span, cols = q_all.shape

    @pl.when(block == 0)
    def _():
        pieces = (p0, p1, p2, p3)
        spread(sc, pieces, 0, cols, straight=q_all)
        spread(sc, (g0, g1, g2, g3), 0, cols, straight=g_all)
        spread(sc, pieces, cols, cols, straight=k_all, flipped=k_flip)
        spread(sc, pieces, 2 * cols, cols, straight=v_all)
        grad_k[...] = jnp.zeros_like(grad_k)
        grad_v[...] = jnp.zeros_like(grad_v)

    grad_q[...] = grad_q_in[...]
    position, start, lowest = query_rows(sc, docs, block)
    queries, grads, log_rows, delta = pull_rows(block, q_all, g_all, out, log_total)

    def step(at, carry):
        pull_step(
            at,
            sc[1] + at * KB,
            position,
            start,
            queries,
            grads,
            log_rows,
            delta,
            (k_all, v_all, k_flip, grad_k, grad_v, grad_q),
        )
        return carry

    last = ((block + 1) * QB - 1) // KB
    lax.fori_loop(jnp.maximum(lowest - sc[1], 0) // KB, last + 1, step, 0)
    grad_q_out[0] = (grad_q[...] * HEAD_DIM**-0.5).T.astype(BF16)

    @pl.when(block == pl.num_programs(0) - 1)
    def _():
        for s in range(GROUP):
            at = place_rows(sc, s, span // GROUP)
            grad_kv[s, :, :cols] = grad_k[at, :]
            grad_kv[s, :, cols:] = grad_v[at, :]


def pull_own(sc, docs, pieces, grads, out, log_total, grad_q):
    rows, cols = pieces[1].shape[0], pieces[1].shape[1] // 3
    span = GROUP * rows
    ins = piece_specs(pieces) + piece_specs(grads) + [
        (pl.BlockSpec((QB, cols), lambda j, sc: (j, 0)), out),
        (pl.BlockSpec((8, QB), lambda j, sc: (0, j)), log_total),
        (pl.BlockSpec((cols, QB), lambda j, sc: (0, j)), grad_q),
    ]
    outs = [
        (slot_spec(rows, cols), shape((GROUP, rows, cols), BF16)),
        (whole((GROUP, rows, 2 * cols)), shape((GROUP, rows, 2 * cols), F32)),
    ]
    low = pltpu.VMEM((span, cols), BF16)
    return run_kernel(
        functools.partial(pull_own_body, docs),
        (span // QB,),
        sc,
        ins,
        outs,
        scratch=[
            low,
            low,
            low,
            low,
            pltpu.VMEM((cols, span), BF16),
            pltpu.VMEM((span, cols), F32),
            pltpu.VMEM((span, cols), F32),
            pltpu.VMEM((cols, QB), F32),
        ],
        flops=span * span * cols * 5,
        moved=span * cols * 24,
    )


def swap_tp(value):
    return lax.ppermute(value, "tp", [(0, 1), (1, 0)])


def swap_fsdp(value, s):
    return lax.ppermute(value, "fsdp", [(i, i ^ s) for i in range(lax.axis_size("fsdp"))])


def shift_fsdp(value, by):
    size = lax.axis_size("fsdp")
    return lax.ppermute(value, "fsdp", [(i, i + by) for i in range(size) if 0 <= i + by < size])


def butterfly(value):
    s = 1
    while s < lax.axis_size("fsdp"):
        value = value + swap_fsdp(value, s)
        s *= 2
    return value


def trade(pieces):
    return [pieces] + [swap_fsdp(pieces[s], s) for s in range(1, GROUP)]


def gather(shard):
    return lax.all_gather(shard, "fsdp", axis=0, tiled=True)


def scatter_sum(full):
    return lax.psum_scatter(full, "fsdp", scatter_dimension=0, tiled=True)


def shards(
    tokens,
    cotangent,
    segments,
    doc_batch,
    ln1_gain,
    ln1_bias,
    w_qkv,
    b_qv,
    w_out,
    b_out,
    ln2_gain,
    ln2_bias,
    w_fc,
    b_fc,
    w_proj,
    b_proj,
):
    rows, width = tokens.shape
    depth = w_qkv.shape[1]
    out_cols = w_out.shape[1]
    units = w_fc.shape[2]
    cols = out_cols // GROUP
    docs = doc_batch.shape[0]
    me = lax.axis_index("fsdp")
    total_rows = rows * lax.axis_size("fsdp")

    def pack_qkv(l):
        return w_qkv[l].reshape(depth, 3, GROUP, cols).transpose(0, 2, 1, 3).reshape(depth, 3 * out_cols)

    def pack_rest(l):
        return [w_out[l].T, w_fc[l], w_proj[l].T]

    fc_at, proj_at = out_cols, out_cols + units
    rest_cols = out_cols + 2 * units
    full_a = gather(pack_qkv(0))
    full_b = gather(jnp.concatenate(pack_rest(0) + [pack_qkv(1)], 1))
    full_c = gather(jnp.concatenate(pack_rest(1), 1))
    qkv_of = ((full_a, 0), (full_b, rest_cols))
    rest_of = (full_b, full_c)

    doc_ids = jnp.arange(docs, dtype=jnp.int32)
    is_doc = segments[:, None] == doc_ids[None, :]
    doc_tokens = butterfly(jnp.sum(is_doc.astype(jnp.int32), 0))
    doc_first = jnp.cumsum(doc_tokens) - doc_tokens
    in_batch = doc_batch[:, None] == jnp.arange(MB, dtype=jnp.int32)[None, :]
    counts = jnp.sum(jnp.where(in_batch, doc_tokens[:, None], 0), 0)
    doc_count = jnp.sum(jnp.where(in_batch, counts[None, :], 0), 1)
    row_count = jnp.sum(jnp.where(is_doc, doc_count[None, :], 0), 1).astype(F32)
    row_weight = total_rows / (MB * row_count)
    sc = jnp.concatenate(
        [jnp.stack([me % GROUP, (me // GROUP) * (GROUP * rows)]).astype(jnp.int32), doc_first]
    )

    def bias_qkv(l):
        three = jnp.stack([b_qv[l, 0], jnp.zeros_like(b_qv[l, 0]), b_qv[l, 1]])
        return three.reshape(3, GROUP, cols).transpose(1, 0, 2).reshape(1, 3 * out_cols)

    def row(vector):
        return vector.reshape(1, vector.shape[0])

    stream, sums = tokens, None
    stored = []
    for l in range(LAYERS):
        weights, first = qkv_of[l]
        stream, low_one, pieces = norm_qkv(
            sc, stream, sums, row(ln1_gain[l]), row(ln1_bias[l]), weights, first // (3 * cols), bias_qkv(l)
        )
        pieces = trade(pieces)
        kv = jnp.stack([pieces[0][0, :, cols:]] + [piece[:, cols:] for piece in pieces[1:]])
        kv_back = shift_fsdp(kv, GROUP)
        acc, top, total = attend_own(sc, docs, pieces)
        mixed, out, log_total = attend_back(sc, docs, pieces, kv_back, acc, top, total)
        mixed = trade(mixed)
        mixed_full, part = out_proj(sc, mixed[0], mixed[1:], rest_of[l])
        middle, low_two, hidden, act, part_two = feed(
            sc,
            stream,
            part,
            swap_tp(part),
            row(b_out[l]),
            row(ln2_gain[l]),
            row(ln2_bias[l]),
            rest_of[l],
            fc_at,
            proj_at,
            row(b_fc[l]),
        )
        stored.append(
            (stream, low_one, pieces, kv_back, out, log_total, mixed_full, middle, low_two, hidden, act)
        )
        stream, sums = middle, (part_two, swap_tp(part_two), row(b_proj[l]))
    own, got, badd = sums
    outputs = (stream + (own.astype(F32) + got.astype(F32)) + badd).astype(BF16)

    grad = cotangent.astype(F32) * row_weight[:, None]
    small = [None] * LAYERS
    large = [None] * LAYERS
    for l in range(LAYERS - 1, -1, -1):
        stream, low_one, pieces, kv_back, out, log_total, mixed_full, middle, low_two, hidden, act = stored[l]
        low_proj, sum_bproj, grad_hidden, sum_bfc, part = feed_pull(
            sc, grad, hidden, rest_of[l], fc_at, proj_at
        )
        got = swap_tp(part)
        feed_grads = scatter_sum(weight_pull(sc, low_two, grad_hidden, low_proj, act))
        grad, low_out, grad_mixed, sum_gain_two, sum_bias_two, sum_bout = mid_pull(
            sc, grad, part, got, middle, row(ln2_gain[l]), rest_of[l], out_cols
        )
        grad_mixed = trade(grad_mixed)
        grad_q, grad_kv_back = pull_back(sc, docs, pieces, grad_mixed, kv_back, out, log_total)
        grad_kv_got = shift_fsdp(grad_kv_back, -GROUP)
        grad_q, grad_kv = pull_own(sc, docs, pieces, grad_mixed, out, log_total, grad_q)
        grad_pieces = jnp.concatenate([grad_q, (grad_kv + grad_kv_got.astype(F32)).astype(BF16)], 2)
        grad_pieces = trade(grad_pieces)
        weights, first = qkv_of[l]
        grad_qkv, part, sum_bqkv = qkv_pull(
            sc, grad_pieces[0], grad_pieces[1:], weights, first // (3 * out_cols)
        )
        got = swap_tp(part)
        attn_grads = scatter_sum(weight_pull(sc, low_one, grad_qkv, low_out, mixed_full))
        grad, sum_gain_one, sum_bias_one = first_pull(sc, grad, part, got, stream, row(ln1_gain[l]))
        sums = [sum_gain_one, sum_bias_one, sum_bqkv, sum_bout, sum_gain_two, sum_bias_two, sum_bfc, sum_bproj]
        small[l] = butterfly(jnp.concatenate([jnp.sum(value, 0) for value in sums]))
        large[l] = (feed_grads, attn_grads)

    def small_parts(vector):
        ends, at = [], 0
        for size in (width, width, 3 * out_cols, width, width, width, units, width):
            ends.append(vector[at : at + size])
            at += size
        three = ends[2].reshape(GROUP, 3, cols).transpose(1, 0, 2).reshape(3, out_cols)
        ends[2] = three[0::2]
        return ends

    small = [small_parts(vector) for vector in small]

    def stack_small(member):
        return jnp.stack([small[l][member] for l in range(LAYERS)])

    grad_wqkv = jnp.stack(
        [
            large[l][1][:, : 3 * out_cols]
            .reshape(depth, GROUP, 3, cols)
            .transpose(0, 2, 1, 3)
            .reshape(depth, 3, out_cols)
            for l in range(LAYERS)
        ]
    ).astype(F32)
    grad_wout = jnp.stack([large[l][1][:, 3 * out_cols :].T for l in range(LAYERS)]).astype(F32)
    grad_wfc = jnp.stack([large[l][0][:, :units] for l in range(LAYERS)]).astype(F32)
    grad_wproj = jnp.stack([large[l][0][:, units:].T for l in range(LAYERS)]).astype(F32)

    return (
        outputs,
        grad,
        stack_small(0),
        stack_small(1),
        grad_wqkv,
        stack_small(2),
        grad_wout,
        stack_small(3),
        stack_small(4),
        stack_small(5),
        grad_wfc,
        stack_small(6),
        grad_wproj,
        stack_small(7),
    )


def solution(mesh):
    placed = (
        P("fsdp", None),
        P("fsdp", None),
        P("fsdp"),
        P(),
        P(),
        P(),
        P(None, "fsdp", None, "tp"),
        P(None, None, "tp"),
        P(None, "tp", "fsdp"),
        P(),
        P(),
        P(),
        P(None, "fsdp", "tp"),
        P(None, "tp"),
        P(None, "tp", "fsdp"),
        P(),
    )
    return jax.shard_map(
        shards,
        mesh=mesh,
        in_specs=placed,
        out_specs=(
            P("fsdp", None),
            P("fsdp", None),
            P(),
            P(),
            P(None, "fsdp", None, "tp"),
            P(None, None, "tp"),
            P(None, "tp", "fsdp"),
            P(),
            P(),
            P(),
            P(None, "fsdp", "tp"),
            P(None, "tp"),
            P(None, "tp", "fsdp"),
            P(),
        ),
        check_vma=False,
    )
```

time: 2630 us -> 1010 us (0.38)
  waiting for transfers between devices: 1720 us -> 537 us
  matrix products: 403 us -> 0 us
  Pallas kernels: 0 us -> 310 us
  local copies, waits for them, and re-layouts: 200 us -> 38.6 us
  blocking collectives: 71.5 us -> 0 us
  other arithmetic: 95.5 us -> 28.8 us
  starting transfers between devices: 103 us -> 59.5 us
    psum x8 -> x0, waiting for transfers between devices: 550 us -> none  [the longest x7 462 us: over_tp(): return lax.psum(partial_value, 'tp')]
    reduce_scatter x8 -> x4, waiting for transfers between devices: 676 us -> 198 us  [scatter_sum(): return lax.psum_scatter(full, 'fsdp', scatter_dimension=0, tiled=True)]
    dot_general x136 -> x0, matrix products: 403 us -> none  [the longest x32 107 us: head_scores(): jnp.einsum('qd,kd->qk', query_h, keys_h, preferred_element_type=jnp.float32)]
    pallas_call x0 -> x26, Pallas kernels: none -> 310 us  [run_kernel(): pl.pallas_call(body, grid_spec=pltpu.PrefetchScalarGridSpec(num_scalar_pr...]
    all_gather x8 -> x3, waiting for transfers between devices: 266 us -> 47.4 us  [gather(): return lax.all_gather(shard, 'fsdp', axis=0, tiled=True)]
    psum x1 -> x0, blocking collectives: 71.5 us -> none  [shards(): counts = lax.psum(jnp.sum(onehot, 0), 'fsdp')]
    slice x37 -> x19, local copies, waits for them, and re-layouts: 75.1 us -> 8.67 us  [the longest x2 1.93 us: shards(): pieces[0][0, :, cols:]]
    ppermute x36 -> x48, waiting for transfers between devices: 229 us -> 291 us  [the longest x8 155 us: swap_tp(): return lax.ppermute(value, 'tp', [(0, 1), (1, 0)])]
  transfers between devices with their start and end apart: 60 -> 55, of which waited for: 34 -> 38; matrix products, arithmetic and copies ran while one was open for 14% -> 4% of each run, Pallas kernels for 0% -> 24%
where the time goes in v1:
time: 1010 us; the launch traced here: 990 us
  waiting for transfers between devices  537 us (53%)
  Pallas kernels  310 us (31%)
  starting transfers between devices  59.5 us (6%)
  local copies, waits for them, and re-layouts  38.6 us (4%)
  other arithmetic  28.8 us (3%)
  between operations  15.6 us (2%)
    pallas_call x26, Pallas kernels, run_kernel(): pl.pallas_call(body, grid_spec=pltpu.PrefetchScalarGridSpec(num_scalar_pr...  310 us
    reduce_scatter x4, waiting for transfers between devices, scatter_sum(): return lax.psum_scatter(full, 'fsdp', scatter_dimension=0, tiled=True)  198 us
    ppermute x8, waiting for transfers between devices, swap_tp(): return lax.ppermute(value, 'tp', [(0, 1), (1, 0)])  155 us
    ppermute x36, waiting for transfers between devices, swap_fsdp(): lax.ppermute(value, 'fsdp', [(i, i ^ s) for i in range(lax.axis_size('fsd...  104 us
    all_gather x3, waiting for transfers between devices, gather(): return lax.all_gather(shard, 'fsdp', axis=0, tiled=True)  47.4 us
    ppermute x36, starting transfers between devices, swap_fsdp(): lax.ppermute(value, 'fsdp', [(i, i ^ s) for i in range(lax.axis_size('fsd...  34.7 us
    ppermute x4, waiting for transfers between devices, shift_fsdp(): lax.ppermute(value, 'fsdp', [(i, i + by) for i in range(size) if 0 <= i +...  33.2 us
  transfers between devices with their start and end apart: 55, of which 38 were waited for; matrix products, arithmetic and copies ran while one was open for 4% of the time, Pallas kernels for 24%

profile of v1, /device:TPU:0, one launch (start us, length us, event | category | flops | bytes accessed | tf_op | source)
XLA Modules:
  0.0 990.1 jit_solution(2553519746231251811)
XLA Ops:
  28.1 30.8 %all-gather.4.cloned.1.call-done.refs_3_.w = bf16[1024,1536]{1,0:T(8,128)(2,1)} async-done(((bf16[64,1536]{1,0:T(8,128)(2,1)}), bf16[1024,1536]{1,0:T(8,128)(2,1)}) %all-gather.4.cloned.1.call-update) | async-done | bytes 3145744 | tf_op jit(solution)/shard_map/all_gather | solution.py:924
  73.3 14.9 %collective-permute-done.6.p3 = bf16[512,384]{1,0:T(8,128)(2,1)S(1)} collective-permute-done((bf16[512,384]{1,0:T(8,128)(2,1)S(1)}, bf16[512,384]{1,0:T(8,128)(2,1)S(1)}, u32[]{:S(2)}, u32[]{:S(2)}) %collective-permute-start.6) | collective-permute-done | bytes 393248 | tf_op jit(solution)/shard_map/ppermute | solution.py:903
  100.5 20.6 %shard_map.264 = (f32[128,2048]{1,0:T(8,128)}, f32[8,2048]{1,0:T(8,128)}, f32[8,2048]{1,0:T(8,128)}) custom-call(s32[10]{0:T(128)} %pad_add_fusion.sc, bf16[4,512,384]{2,1,0:T(8,128)(2,1)} %get-tuple-element.89.p0, bf16[512,384]{1,0:T(8,128)(2,1)} %copy-done.5, bf16[512,384]{1,0:T(8,128)(2,1)} %copy-done.4, bf16[512,384]{1,0:T(8,128)(2,1)} %copy-done.3), custom_call_target="tpu_custom_call" | custom-call | flops 1073741824 | bytes 2621440 | tf_op jit(solution)/shard_map/pallas_call | solution.py:44
  121.1 20.1 %collective-permute-done.7.kv = bf16[4,512,256]{2,1,0:T(8,128)(2,1)S(1)} collective-permute-done((bf16[4,512,256]{2,1,0:T(8,128)(2,1)S(1)}, bf16[4,512,256]{2,1,0:T(8,128)(2,1)S(1)}, u32[]{:S(2)}, u32[]{:S(2)}) %collective-permute-start.7) | collective-permute-done | bytes 1048608 | tf_op jit(solution)/shard_map/ppermute | solution.py:908
  157.5 16.6 %all-gather.6.cloned.1.call-done.w.fc.proj.refs_6_ = bf16[1024,6144]{1,0:T(8,128)(2,1)} async-done(((bf16[64,6144]{1,0:T(8,128)(2,1)}), bf16[1024,6144]{1,0:T(8,128)(2,1)}) %all-gather.6.cloned.1.call-update) | async-done | bytes 12582928 | tf_op jit(solution)/shard_map/all_gather | solution.py:924
  181.3 22.0 %collective-permute-done.11.got = bf16[512,1024]{1,0:T(8,128)(2,1)S(1)} collective-permute-done((bf16[512,1024]{1,0:T(8,128)(2,1)}, bf16[512,1024]{1,0:T(8,128)(2,1)S(1)}, u32[]{:S(2)}, u32[]{:S(2)}) %collective-permute-start.11) | collective-permute-done | bytes 1048608 | tf_op jit(solution)/shard_map/ppermute | solution.py:899
  204.3 18.8 %shard_map.267 = (f32[512,1024]{1,0:T(8,128)}, bf16[512,1024]{1,0:T(8,128)(2,1)}, f32[512,2048]{1,0:T(8,128)}, bf16[512,2048]{1,0:T(8,128)(2,1)}, bf16[512,1024]{1,0:T(8,128)(2,1)}) custom-call(s32[10]{0:T(128)} %pad_add_fusion.sc, f32[512,1024]{1,0:T(8,128)} %get-tuple-element.88.base.inputs, bf16[512,1024]{1,0:T(8,128)(2,1)} %get-tuple-element.94.own, ...), custom_call_target="tpu_custom_call" | custom-call | flops 4294967296 | bytes 23068672 | tf_op jit(solution)/shard_map/pallas_call | solution.py:44
  225.6 22.0 %collective-permute-done.12.refs_2_ = bf16[512,1024]{1,0:T(8,128)(2,1)S(1)} collective-permute-done((bf16[512,1024]{1,0:T(8,128)(2,1)}, bf16[512,1024]{1,0:T(8,128)(2,1)S(1)}, u32[]{:S(2)}, u32[]{:S(2)}) %collective-permute-start.12) | collective-permute-done | bytes 1048608 | tf_op jit(solution)/shard_map/ppermute | solution.py:899
  248.5 11.4 %shard_map.268 = (f32[512,1024]{1,0:T(8,128)}, bf16[512,1024]{1,0:T(8,128)(2,1)}, bf16[4,512,384]{2,1,0:T(8,128)(2,1)}) custom-call(s32[10]{0:T(128)} %pad_add_fusion.sc, f32[512,1024]{1,0:T(8,128)} %get-tuple-element.95.refs_0_.inputs, bf16[512,1024]{1,0:T(8,128)(2,1)} %get-tuple-element.96.refs_1_, bf16[512,1024]{1,0:T(8,128)(2,1)} %copy-done.13, ...), custom_call_target="tpu_custom_call" | custom-call | flops 1610612736 | bytes 9437184 | tf_op jit(solution)/shard_map/pallas_call | solution.py:44
  288.0 20.6 %shard_map.269 = (f32[128,2048]{1,0:T(8,128)}, f32[8,2048]{1,0:T(8,128)}, f32[8,2048]{1,0:T(8,128)}) custom-call(s32[10]{0:T(128)} %pad_add_fusion.sc, bf16[4,512,384]{2,1,0:T(8,128)(2,1)} %get-tuple-element.98.p0, bf16[512,384]{1,0:T(8,128)(2,1)} %copy-done.8, bf16[512,384]{1,0:T(8,128)(2,1)} %copy-done.7, bf16[512,384]{1,0:T(8,128)(2,1)} %copy-done.6), custom_call_target="tpu_custom_call" | custom-call | flops 1073741824 | bytes 2621440 | tf_op jit(solution)/shard_map/pallas_call | solution.py:44
  337.4 22.2 %collective-permute-done.20.got = bf16[512,1024]{1,0:T(8,128)(2,1)S(1)} collective-permute-done((bf16[512,1024]{1,0:T(8,128)(2,1)}, bf16[512,1024]{1,0:T(8,128)(2,1)S(1)}, u32[]{:S(2)}, u32[]{:S(2)}) %collective-permute-start.20) | collective-permute-done | bytes 1048608 | tf_op jit(solution)/shard_map/ppermute | solution.py:899
  360.7 18.3 %shard_map.272 = (f32[512,1024]{1,0:T(8,128)}, bf16[512,1024]{1,0:T(8,128)(2,1)}, f32[512,2048]{1,0:T(8,128)}, bf16[512,2048]{1,0:T(8,128)(2,1)}, bf16[512,1024]{1,0:T(8,128)(2,1)}) custom-call(s32[10]{0:T(128)} %pad_add_fusion.sc, f32[512,1024]{1,0:T(8,128)} %get-tuple-element.97.base.inputs, bf16[512,1024]{1,0:T(8,128)(2,1)} %get-tuple-element.103.own, ...), custom_call_target="tpu_custom_call" | custom-call | flops 4294967296 | bytes 23068672 | tf_op jit(solution)/shard_map/pallas_call | solution.py:44
  379.0 15.5 %shard_map.273 = (bf16[512,1024]{1,0:T(8,128)(2,1)}, f32[8,1024]{1,0:T(8,128)}, bf16[512,2048]{1,0:T(8,128)(2,1)}, f32[8,2048]{1,0:T(8,128)}, bf16[512,1024]{1,0:T(8,128)(2,1)}) custom-call(s32[10]{0:T(128)} %pad_add_fusion.sc, f32[512,1024]{1,0:T(8,128)} %convert_multiply_fusion.grad, f32[512,2048]{1,0:T(8,128)} %get-tuple-element.106.hidden, ...), custom_call_target="tpu_custom_call" | custom-call | flops 4294967296 | bytes 18874368 | tf_op jit(solution)/shard_map/pallas_call | solution.py:44
  395.8 23.2 %collective-permute-done.22.got = bf16[512,1024]{1,0:T(8,128)(2,1)S(1)} collective-permute-done((bf16[512,1024]{1,0:T(8,128)(2,1)}, bf16[512,1024]{1,0:T(8,128)(2,1)S(1)}, u32[]{:S(2)}, u32[]{:S(2)}) %collective-permute-start.22) | collective-permute-done | bytes 1048608 | tf_op jit(solution)/shard_map/ppermute | solution.py:899
  448.2 24.0 %shard_map.276 = (bf16[4,512,128]{2,1,0:T(8,128)(2,1)}, f32[4,512,256]{2,1,0:T(8,128)}) custom-call(s32[10]{0:T(128)} %pad_add_fusion.sc, bf16[4,512,384]{2,1,0:T(8,128)(2,1)} %get-tuple-element.98.p0, bf16[512,384]{1,0:T(8,128)(2,1)} %copy-done.8, bf16[512,384]{1,0:T(8,128)(2,1)} %copy-done.7, bf16[512,384]{1,0:T(8,128)(2,1)} %copy-done.6, ...), custom_call_target="tpu_custom_call" | custom-call | flops 2684354560 | bytes 6291456 | tf_op jit(solution)/shard_map/pallas_call | solution.py:44
  517.9 23.6 %collective-permute-done.30.got = bf16[512,1024]{1,0:T(8,128)(2,1)S(1)} collective-permute-done((bf16[512,1024]{1,0:T(8,128)(2,1)S(1)}, bf16[512,1024]{1,0:T(8,128)(2,1)S(1)}, u32[]{:S(2)}, u32[]{:S(2)}) %collective-permute-start.30) | collective-permute-done | bytes 1048608 | tf_op jit(solution)/shard_map/ppermute | solution.py:899
  551.9 15.5 %shard_map.279 = (bf16[512,1024]{1,0:T(8,128)(2,1)}, f32[8,1024]{1,0:T(8,128)}, bf16[512,2048]{1,0:T(8,128)(2,1)}, f32[8,2048]{1,0:T(8,128)}, bf16[512,1024]{1,0:T(8,128)(2,1)}) custom-call(s32[10]{0:T(128)} %pad_add_fusion.sc, f32[512,1024]{1,0:T(8,128)} %get-tuple-element.117.grad, f32[512,2048]{1,0:T(8,128)} %get-tuple-element.118.hidden, ...), custom_call_target="tpu_custom_call" | custom-call | flops 4294967296 | bytes 18874368 | tf_op jit(solution)/shard_map/pallas_call | solution.py:44
  568.7 23.0 %collective-permute-done.31.got = bf16[512,1024]{1,0:T(8,128)(2,1)S(1)} collective-permute-done((bf16[512,1024]{1,0:T(8,128)(2,1)}, bf16[512,1024]{1,0:T(8,128)(2,1)S(1)}, u32[]{:S(2)}, u32[]{:S(2)}) %collective-permute-start.31) | collective-permute-done | bytes 1048608 | tf_op jit(solution)/shard_map/ppermute | solution.py:899
  622.1 24.0 %shard_map.282 = (bf16[4,512,128]{2,1,0:T(8,128)(2,1)}, f32[4,512,256]{2,1,0:T(8,128)}) custom-call(s32[10]{0:T(128)} %pad_add_fusion.sc, bf16[4,512,384]{2,1,0:T(8,128)(2,1)} %get-tuple-element.89.p0, bf16[512,384]{1,0:T(8,128)(2,1)} %copy-done.5, bf16[512,384]{1,0:T(8,128)(2,1)} %copy-done.4, bf16[512,384]{1,0:T(8,128)(2,1)} %copy-done.3, ...), custom_call_target="tpu_custom_call" | custom-call | flops 2684354560 | bytes 6291456 | tf_op jit(solution)/shard_map/pallas_call | solution.py:44
  687.9 11.9 %shard_map.288 = bf16[1024,4096]{1,0:T(8,128)(2,1)} custom-call(s32[10]{0:T(128)} %pad_add_fusion.sc, bf16[512,1024]{1,0:T(8,128)(2,1)} %get-tuple-element.158.x0, bf16[512,2048]{1,0:T(8,128)(2,1)} %get-tuple-element.159.g0, bf16[512,1024]{1,0:T(8,128)(2,1)} %get-tuple-element.160.x1, bf16[512,2048]{1,0:T(8,128)(2,1)} %get-tuple-element.161.g1), custom_call_target="tpu_custom_call" | custom-call | flops 4294967296 | bytes 14680064 | tf_op jit(solution)/shard_map/pallas_call | solution.py:44
  699.9 12.2 %shard_map.287 = bf16[1024,4096]{1,0:T(8,128)(2,1)} custom-call(s32[10]{0:T(128)} %pad_add_fusion.sc, bf16[512,1024]{1,0:T(8,128)(2,1)} %get-tuple-element.154.x0, bf16[512,2048]{1,0:T(8,128)(2,1)} %get-tuple-element.155.g0, bf16[512,1024]{1,0:T(8,128)(2,1)} %get-tuple-element.156.x1, bf16[512,2048]{1,0:T(8,128)(2,1)} %get-tuple-element.157.g1), custom_call_target="tpu_custom_call" | custom-call | flops 4294967296 | bytes 14680064 | tf_op jit(solution)/shard_map/pallas_call | solution.py:44
  720.9 18.4 %collective-permute-done.39.got = bf16[512,1024]{1,0:T(8,128)(2,1)S(1)} collective-permute-done((bf16[512,1024]{1,0:T(8,128)(2,1)S(1)}, bf16[512,1024]{1,0:T(8,128)(2,1)S(1)}, u32[]{:S(2)}, u32[]{:S(2)}) %collective-permute-start.39) | collective-permute-done | bytes 1048608 | tf_op jit(solution)/shard_map/ppermute | solution.py:899
  780.2 91.0 %reduce-scatter.11.cloned.1.call-done = bf16[64,4096]{1,0:T(8,128)(2,1)} async-done(((bf16[1024,4096]{1,0:T(8,128)(2,1)}), bf16[64,4096]{1,0:T(8,128)(2,1)}) %reduce-scatter.11.cloned.1.call-update) | async-done | bytes 524304 | tf_op jit(solution)/shard_map/reduce_scatter | solution.py:928
  872.2 107.4 %reduce-scatter.9.cloned.1.call-done = bf16[64,4096]{1,0:T(8,128)(2,1)} async-done(((bf16[1024,4096]{1,0:T(8,128)(2,1)}), bf16[64,4096]{1,0:T(8,128)(2,1)}) %reduce-scatter.9.cloned.1.call-update) | async-done | bytes 524304 | tf_op jit(solution)/shard_map/reduce_scatter | solution.py:928
  (376 shorter events, 346.4 us)
Async XLA Ops:
  7.2 51.7 %all-gather.4.cloned.1.call-start = ((), (), s32[]{:S(2)}) async-start(), calls=%async_computation.4 | async-start | bytes 3342336 | tf_op jit(solution)/shard_map/all_gather | solution.py:924
  9.5 164.6 %all-gather.6.cloned.1.call-start = ((), (), s32[]{:S(2)}) async-start(), calls=%async_computation.5 | async-start | bytes 13369344 | tf_op jit(solution)/shard_map/all_gather | solution.py:924
  11.1 311.4 %all-gather.8.cloned.1.call-start = ((), (), s32[]{:S(2)}) async-start(), calls=%async_computation.6 | async-start | bytes 10027008 | tf_op jit(solution)/shard_map/all_gather | solution.py:924
  12.0 762.2 %reduce-scatter.7.cloned.1.call-start = ((), (), s32[]{:S(2)}) async-start(), calls=%async_computation.8 | async-start | bytes 4456448 | tf_op jit(solution)/shard_map/reduce_scatter | solution.py:928
  70.9 25.9 %collective-permute-start.5 = (bf16[512,384]{1,0:T(8,128)(2,1)S(1)}, bf16[512,384]{1,0:T(8,128)(2,1)S(1)}, u32[]{:S(2)}, u32[]{:S(2)}) collective-permute-start(bf16[512,384]{1,0:T(8,128)(2,1)S(1)} %get-tuple-element.172), channel_id=1, source_target_pairs={{0,4},{2,6},{4,0},{6,2},{8,12},{10,14},{12,8},{14,10},{16,20},{18,... | collective-permute-start | bytes 1179656 | tf_op jit(solution)/shard_map/ppermute | solution.py:903
  73.3 23.6 %collective-permute-start.4 = (bf16[512,384]{1,0:T(8,128)(2,1)S(1)}, bf16[512,384]{1,0:T(8,128)(2,1)S(1)}, u32[]{:S(2)}, u32[]{:S(2)}) collective-permute-start(bf16[512,384]{1,0:T(8,128)(2,1)S(1)} %get-tuple-element.173), channel_id=1, source_target_pairs={{0,2},{2,0},{4,6},{6,4},{8,10},{10,8},{12,14},{14,12},{16,18},{18,... | collective-permute-start | bytes 1179656 | tf_op jit(solution)/shard_map/ppermute | solution.py:903
  97.0 44.2 %collective-permute-start.7 = (bf16[4,512,256]{2,1,0:T(8,128)(2,1)S(1)}, bf16[4,512,256]{2,1,0:T(8,128)(2,1)S(1)}, u32[]{:S(2)}, u32[]{:S(2)}) collective-permute-start(bf16[4,512,256]{2,1,0:T(8,128)(2,1)S(1)} %pad_maximum_fusion.2), channel_id=1, source_target_pairs={{0,8},{2,10},{4,12},{6,14},{8,16},{10,18},{12,20},{14,22},{16,24},... | collective-permute-start | bytes 3145736 | tf_op jit(solution)/shard_map/ppermute | solution.py:908
  178.0 25.4 %collective-permute-start.11 = (bf16[512,1024]{1,0:T(8,128)(2,1)}, bf16[512,1024]{1,0:T(8,128)(2,1)S(1)}, u32[]{:S(2)}, u32[]{:S(2)}) collective-permute-start(bf16[512,1024]{1,0:T(8,128)(2,1)} %get-tuple-element.94.own), channel_id=1, source_target_pairs={{0,1},{1,0},{2,3},{3,2},{4,5},{5,4},{6,7},{7,6},{8,9},{9,8},{10,11... | collective-permute-start | bytes 3145736 | tf_op jit(solution)/shard_map/ppermute | solution.py:899
  223.1 24.4 %collective-permute-start.12 = (bf16[512,1024]{1,0:T(8,128)(2,1)}, bf16[512,1024]{1,0:T(8,128)(2,1)S(1)}, u32[]{:S(2)}, u32[]{:S(2)}) collective-permute-start(bf16[512,1024]{1,0:T(8,128)(2,1)} %get-tuple-element.96.refs_1_), channel_id=1, source_target_pairs={{0,1},{1,0},{2,3},{3,2},{4,5},{5,4},{6,7},{7,6},{8,9},{9,8},{10,11... | collective-permute-start | bytes 3145736 | tf_op jit(solution)/shard_map/ppermute | solution.py:899
  261.4 18.5 %collective-permute-start.14 = (bf16[512,384]{1,0:T(8,128)(2,1)S(1)}, bf16[512,384]{1,0:T(8,128)(2,1)S(1)}, u32[]{:S(2)}, u32[]{:S(2)}) collective-permute-start(bf16[512,384]{1,0:T(8,128)(2,1)S(1)} %get-tuple-element.169), channel_id=1, source_target_pairs={{0,4},{2,6},{4,0},{6,2},{8,12},{10,14},{12,8},{14,10},{16,20},{18,... | collective-permute-start | bytes 1179656 | tf_op jit(solution)/shard_map/ppermute | solution.py:903
  280.1 30.7 %collective-permute-start.16 = (bf16[4,512,256]{2,1,0:T(8,128)(2,1)S(1)}, bf16[4,512,256]{2,1,0:T(8,128)(2,1)S(1)}, u32[]{:S(2)}, u32[]{:S(2)}) collective-permute-start(bf16[4,512,256]{2,1,0:T(8,128)(2,1)S(1)} %pad_maximum_fusion.3), channel_id=1, source_target_pairs={{0,8},{2,10},{4,12},{6,14},{8,16},{10,18},{12,20},{14,22},{16,24},... | collective-permute-start | bytes 3145736 | tf_op jit(solution)/shard_map/ppermute | solution.py:908
  334.3 25.4 %collective-permute-start.20 = (bf16[512,1024]{1,0:T(8,128)(2,1)}, bf16[512,1024]{1,0:T(8,128)(2,1)S(1)}, u32[]{:S(2)}, u32[]{:S(2)}) collective-permute-start(bf16[512,1024]{1,0:T(8,128)(2,1)} %get-tuple-element.103.own), channel_id=1, source_target_pairs={{0,1},{1,0},{2,3},{3,2},{4,5},{5,4},{6,7},{7,6},{8,9},{9,8},{10,11... | collective-permute-start | bytes 3145736 | tf_op jit(solution)/shard_map/ppermute | solution.py:899
  394.5 24.6 %collective-permute-start.22 = (bf16[512,1024]{1,0:T(8,128)(2,1)}, bf16[512,1024]{1,0:T(8,128)(2,1)S(1)}, u32[]{:S(2)}, u32[]{:S(2)}) collective-permute-start(bf16[512,1024]{1,0:T(8,128)(2,1)} %get-tuple-element.107.own), channel_id=1, source_target_pairs={{0,1},{1,0},{2,3},{3,2},{4,5},{5,4},{6,7},{7,6},{8,9},{9,8},{10,11... | collective-permute-start | bytes 3145736 | tf_op jit(solution)/shard_map/ppermute | solution.py:899
  446.7 31.7 %collective-permute-start.26 = (bf16[4,512,256]{2,1,0:T(8,128)(2,1)}, bf16[4,512,256]{2,1,0:T(8,128)(2,1)S(1)}, u32[]{:S(2)}, u32[]{:S(2)}) collective-permute-start(bf16[4,512,256]{2,1,0:T(8,128)(2,1)} %get-tuple-element.115), channel_id=1, source_target_pairs={{8,0},{10,2},{12,4},{14,6},{16,8},{18,10},{20,12},{22,14},{24,16},... | collective-permute-start | bytes 3145736 | tf_op jit(solution)/shard_map/ppermute | solution.py:908
  481.3 19.1 %collective-permute-start.28 = (bf16[512,384]{1,0:T(8,128)(2,1)S(1)}, bf16[512,384]{1,0:T(8,128)(2,1)S(1)}, u32[]{:S(2)}, u32[]{:S(2)}) collective-permute-start(bf16[512,384]{1,0:T(8,128)(2,1)S(1)} %get-tuple-element.167), channel_id=1, source_target_pairs={{0,4},{2,6},{4,0},{6,2},{8,12},{10,14},{12,8},{14,10},{16,20},{18,... | collective-permute-start | bytes 1179656 | tf_op jit(solution)/shard_map/ppermute | solution.py:903
  515.3 261.1 %reduce-scatter.5.cloned.1.call-start = ((), (), s32[]{:S(2)}) async-start(), calls=%async_computation.7 | async-start | bytes 4456448 | tf_op jit(solution)/shard_map/reduce_scatter | solution.py:928
  516.5 25.0 %collective-permute-start.30 = (bf16[512,1024]{1,0:T(8,128)(2,1)S(1)}, bf16[512,1024]{1,0:T(8,128)(2,1)S(1)}, u32[]{:S(2)}, u32[]{:S(2)}) collective-permute-start(bf16[512,1024]{1,0:T(8,128)(2,1)S(1)} %copy-done.19), channel_id=1, source_target_pairs={{0,1},{1,0},{2,3},{3,2},{4,5},{5,4},{6,7},{7,6},{8,9},{9,8},{10,11... | collective-permute-start | bytes 3145736 | tf_op jit(solution)/shard_map/ppermute | solution.py:899
  567.3 24.4 %collective-permute-start.31 = (bf16[512,1024]{1,0:T(8,128)(2,1)}, bf16[512,1024]{1,0:T(8,128)(2,1)S(1)}, u32[]{:S(2)}, u32[]{:S(2)}) collective-permute-start(bf16[512,1024]{1,0:T(8,128)(2,1)} %get-tuple-element.119.own), channel_id=1, source_target_pairs={{0,1},{1,0},{2,3},{3,2},{4,5},{5,4},{6,7},{7,6},{8,9},{9,8},{10,11... | collective-permute-start | bytes 3145736 | tf_op jit(solution)/shard_map/ppermute | solution.py:899
  620.6 30.3 %collective-permute-start.35 = (bf16[4,512,256]{2,1,0:T(8,128)(2,1)}, bf16[4,512,256]{2,1,0:T(8,128)(2,1)S(1)}, u32[]{:S(2)}, u32[]{:S(2)}) collective-permute-start(bf16[4,512,256]{2,1,0:T(8,128)(2,1)} %get-tuple-element.127), channel_id=1, source_target_pairs={{8,0},{10,2},{12,4},{14,6},{16,8},{18,10},{20,12},{22,14},{24,16},... | collective-permute-start | bytes 3145736 | tf_op jit(solution)/shard_map/ppermute | solution.py:908
  687.8 183.3 %reduce-scatter.11.cloned.1.call-start = ((), (), s32[]{:S(2)}) async-start(), calls=%async_computation.10 | async-start | bytes 8912896 | tf_op jit(solution)/shard_map/reduce_scatter | solution.py:928
  699.8 279.8 %reduce-scatter.9.cloned.1.call-start = ((), (), s32[]{:S(2)}) async-start(), calls=%async_computation.9 | async-start | bytes 8912896 | tf_op jit(solution)/shard_map/reduce_scatter | solution.py:928
  713.3 26.0 %collective-permute-start.39 = (bf16[512,1024]{1,0:T(8,128)(2,1)S(1)}, bf16[512,1024]{1,0:T(8,128)(2,1)S(1)}, u32[]{:S(2)}, u32[]{:S(2)}) collective-permute-start(bf16[512,1024]{1,0:T(8,128)(2,1)S(1)} %copy-done.17), channel_id=1, source_target_pairs={{0,1},{1,0},{2,3},{3,2},{4,5},{5,4},{6,7},{7,6},{8,9},{9,8},{10,11... | collective-permute-start | bytes 3145736 | tf_op jit(solution)/shard_map/ppermute | solution.py:899
  714.5 46.6 %collective-permute-start.21 = (bf16[512,1024]{1,0:T(8,128)(2,1)S(1)}, bf16[512,1024]{1,0:T(8,128)(2,1)}, u32[]{:S(2)}, u32[]{:S(2)}) collective-permute-start(bf16[512,1024]{1,0:T(8,128)(2,1)S(1)} %copy-done.16), channel_id=1, source_target_pairs={{0,1},{1,0},{2,3},{3,2},{4,5},{5,4},{6,7},{7,6},{8,9},{9,8},{10,11... | collective-permute-start | bytes 3145736 | tf_op jit(solution)/shard_map/ppermute | solution.py:899
  718.5 33.0 %collective-permute-start.45 = (f32[9728]{0:T(1024)S(1)}, f32[9728]{0:T(1024)S(1)}, u32[]{:S(2)}, u32[]{:S(2)}) collective-permute-start(f32[9728]{0:T(1024)S(1)} %add.87), channel_id=1, source_target_pairs={{0,4},{2,6},{4,0},{6,2},{8,12},{10,14},{12,8},{14,10},{16,20},{18,... | collective-permute-start | bytes 116744 | tf_op jit(solution)/shard_map/ppermute | solution.py:903
  (93 other events, 643.0 us)
Sparse Core Ops, SparseCore 0:
  10.9 47.9 all-gather.3
  61.7 112.2 all-gather.5
  176.4 84.1 all-gather.7
  515.4 73.5 reduce-scatter.6
  688.0 74.2 reduce-scatter.4
  766.2 104.9 reduce-scatter.10
  875.2 104.3 reduce-scatter.8

commit v2 on v1

--- a/solution.py
+++ b/solution.py
@@ -15,6 +15,8 @@
 EPS = 1e-05
 GROUP = REACH
 QB = 256
+LN_ROWS = 128
+ACT_ROWS = 128
 KB = 256
 NEG = -1e30
 F32 = jnp.float32
@@ -101,7 +103,7 @@
             unit, _ = norm_parts(value)
             low[at, :] = (unit * gain[...] + bias[...]).astype(BF16)
 
-        each_rows(base.shape[0], 32, rows)
+        each_rows(base.shape[0], LN_ROWS, rows)
 
     piece[0] = (dot(low[...], w[...]) + bq[...]).astype(BF16)
 
@@ -190,14 +192,14 @@
             unit, _ = norm_parts(value)
             low[at, :] = (unit * gain[...] + bias[...]).astype(BF16)
 
-        each_rows(base.shape[0], 32, rows)
+        each_rows(base.shape[0], LN_ROWS, rows)
 
     hidden[...] = dot(low[...], fc[...]) + bfc[...]
 
     def rows_act(at):
         act[at, :] = gelu_rows(hidden[at, :]).astype(BF16)
 
-    each_rows(hidden.shape[0], 32, rows_act)
+    each_rows(hidden.shape[0], ACT_ROWS, rows_act)
     part = dot_last(act[...], proj[...])
 
     @pl.when(at_chunk == 0)
@@ -258,7 +260,7 @@
             low[at, :] = value
             sum_low[...] += eight_rows(value.astype(F32))
 
-        each_rows(grad.shape[0], 32, rows)
+        each_rows(grad.shape[0], LN_ROWS, rows)
 
     grad_act[...] = dot(low[...], proj[...])
     sum_hidden[...] = jnp.zeros_like(sum_hidden)
@@ -268,7 +270,7 @@
         slope_grad[at, :] = value
         sum_hidden[...] += eight_rows(value.astype(F32))
 
-    each_rows(grad.shape[0], 32, rows_slope)
+    each_rows(grad.shape[0], ACT_ROWS, rows_slope)
     part = dot_last(slope_grad[...], fc[...])
 
     @pl.when(at_chunk == 0)
@@ -332,7 +334,7 @@
         low[at, :] = value
         sum_low[...] += eight_rows(value.astype(F32))
 
-    each_rows(grad.shape[0], 32, rows)
+    each_rows(grad.shape[0], LN_ROWS, rows)
     mixed[...] = dot(low[...], w[...]).astype(BF16)
     cols = pieces.shape[2]
     for s in range(GROUP):
@@ -381,7 +383,7 @@
     def rows(at):
         sums[...] += eight_rows(full[at, :].astype(F32))
 
-    each_rows(full.shape[0], 32, rows)
+    each_rows(full.shape[0], LN_ROWS, rows)
     tile = 256
     for at in range(0, partial.shape[1], tile):
         partial[:, at : at + tile] = dot_last(full[...], w[at : at + tile, :]).astype(BF16)
@@ -416,7 +418,7 @@
     def rows(at):
         norm_pull_rows(at, grad, own, got, inputs, gain, grad_new, sum_gain, sum_bias)
 
-    each_rows(grad.shape[0], 32, rows)
+    each_rows(grad.shape[0], LN_ROWS, rows)
 
 
 def first_pull(sc, grad, own, got, inputs, gain):
@@ -433,24 +435,44 @@
     )
 
 
-def weight_pull_body(first_steps, sc, x0, g0, x1, g1, out, flipped):
+def flip_slots(sc, span, source, plain, flipped):
+    plain[...] = source[...].T
+    width = plain.shape[0]
+    groups = lax.axis_size("fsdp") // GROUP
+    depth = width // (GROUP * groups)
+    mine = sc[1] // span
+    slot = 0
+    for s in (0, 2, 1, 3):
+        for onward in range(groups):
+            owner = lax.rem(mine + onward, groups) * GROUP + (sc[0] ^ s)
+            flipped[slot * depth : (slot + 1) * depth, :] = plain[
+                pl.ds(pl.multiple_of(owner * depth, depth), depth), :
+            ]
+            slot += 1
+
+
+def weight_pull_body(first_steps, sc, x0, g0, x1, g1, keep, send, plain, flipped):
     at = pl.program_id(0)
+    half = keep.shape[0]
+    span = GROUP * x0.shape[0]
 
     @pl.when(at == 0)
     def _():
-        flipped[...] = x0[...].T
+        flip_slots(sc, span, x0, plain, flipped)
 
     @pl.when(at == first_steps)
     def _():
-        flipped[...] = x1[...].T
+        flip_slots(sc, span, x1, plain, flipped)
 
     @pl.when(at < first_steps)
     def _():
-        out[...] = dot(flipped[...], g0[...]).astype(BF16)
+        keep[...] = dot(flipped[:half, :], g0[...]).astype(BF16)
+        send[...] = dot(flipped[half:, :], g0[...]).astype(BF16)
 
     @pl.when(at >= first_steps)
     def _():
-        out[...] = dot(flipped[...], g1[...]).astype(BF16)
+        keep[...] = dot(flipped[:half, :], g1[...]).astype(BF16)
+        send[...] = dot(flipped[half:, :], g1[...]).astype(BF16)
 
 
 def weight_pull(sc, x0, g0, x1, g1):
@@ -463,22 +485,369 @@
         (whole(x1.shape), x1),
         (pl.BlockSpec((rows, chunk), lambda j, sc: (0, jnp.maximum(j - n0, 0))), g1),
     ]
-    outs = [
-        (
-            pl.BlockSpec((width, chunk), lambda j, sc: (0, j)),
-            shape((width, (n0 + n1) * chunk), BF16),
-        )
-    ]
+    half = (
+        pl.BlockSpec((width // 2, chunk), lambda j, sc: (0, j)),
+        shape((width // 2, (n0 + n1) * chunk), BF16),
+    )
     return run_kernel(
         functools.partial(weight_pull_body, n0),
         (n0 + n1,),
         sc,
         ins,
-        outs,
-        scratch=[pltpu.VMEM((width, rows), BF16)],
+        [half, half],
+        scratch=[pltpu.VMEM((width, rows), BF16), pltpu.VMEM((width, rows), BF16)],
         flops=2 * rows * width * (n0 + n1) * chunk,
         moved=rows * width * 4 + (rows + width) * (n0 + n1) * chunk * 2,
-    )[0]
+    )
+
+
+ROWS = 256
+MESH = pl.DeviceIdType.MESH
+
+
+class Links:
+    def __init__(self, send, recv):
+        self.send, self.recv, self.used = send, recv, 0
+        self.me = lax.axis_index("fsdp")
+        self.place = lax.rem(self.me, GROUP)
+        self.group = self.me // GROUP
+        self.groups = lax.axis_size("fsdp") // GROUP
+        self.other = 1 - lax.axis_index("tp")
+
+    def peer(self, s):
+        return {"fsdp": self.group * GROUP + (self.place ^ s)}
+
+    def beyond(self, by, s):
+        return {"fsdp": lax.rem(self.group + by, self.groups) * GROUP + (self.place ^ s)}
+
+    def copy(self, source, target, device):
+        at = self.used
+        self.used += 1
+        return pltpu.make_async_remote_copy(
+            src_ref=source,
+            dst_ref=target,
+            send_sem=self.send.at[at],
+            recv_sem=self.recv.at[at],
+            device_id=device,
+            device_id_type=MESH,
+        )
+
+    def swap(self, source, target):
+        return self.copy(source, target, {"tp": self.other})
+
+    def greet(self, devices):
+        barrier = pltpu.get_barrier_semaphore()
+        for device in devices:
+            pl.semaphore_signal(barrier, inc=1, device_id=device, device_id_type=MESH)
+        pl.semaphore_wait(barrier, len(devices))
+
+
+def columns(place, cols):
+    return pl.ds(pl.multiple_of(place * cols, cols), cols)
+
+
+def tiles(count, size, body):
+    def step(at, carry):
+        body(pl.ds(pl.multiple_of(at * size, size), size))
+        return carry
+
+    lax.fori_loop(0, count // size, step, 0)
+
+
+def rows_within(first, body):
+    def step(at, carry):
+        body(pl.ds(pl.multiple_of(first + at * LN_ROWS, LN_ROWS), LN_ROWS))
+        return carry
+
+    lax.fori_loop(0, ROWS // LN_ROWS, step, 0)
+
+
+def out_rows(rows, mixed, w, target):
+    def tile(at):
+        target[rows, at] = dot_last(mixed[rows, :], w[at, :]).astype(BF16)
+
+    tiles(w.shape[0], 256, tile)
+
+
+def norm_rows(first, base, sums, gain, bias, stream, low):
+    def body(at):
+        value = base[at, :].astype(F32)
+        if sums is not None:
+            own, got, badd = sums
+            value = value + (own[at, :].astype(F32) + got[at, :].astype(F32)) + badd[...]
+        stream[at, :] = value
+        unit, _ = norm_parts(value)
+        low[at, :] = (unit * gain[...] + bias[...]).astype(BF16)
+
+    rows_within(first, body)
+
+
+def feed_rows(rows, low, fc, bfc, hidden, act, proj, target):
+    def tile(at):
+        value = dot(low[rows, :], fc[:, at]) + bfc[:, at]
+        hidden[rows, at] = value
+        act[rows, at] = gelu_rows(value).astype(BF16)
+
+    tiles(fc.shape[1], 512, tile)
+
+    def tile_out(at):
+        target[rows, at] = dot_last(act[rows, :], proj[at, :]).astype(BF16)
+
+    tiles(proj.shape[0], 256, tile_out)
+
+
+def send_qkv(links, low, w, bq, ready, pieces, kv_back, kept):
+    cols = bq.shape[1] // GROUP
+    copies = []
+    order = (2, 3, 1, 0)
+    chunks = low.shape[0] // ROWS
+    for c in range(chunks):
+        rows = pl.ds(c * ROWS, ROWS)
+        across = {
+            s: links.copy(ready.at[s, rows], pieces.at[s, rows], links.peer(s)) for s in order if s
+        }
+        onward = {
+            s: links.copy(
+                ready.at[s, rows, pl.ds(cols // 3, 2 * cols // 3)],
+                kv_back.at[s, rows],
+                links.beyond(1, s),
+            )
+            for s in order
+        }
+        own = pltpu.make_async_copy(ready.at[0, rows], pieces.at[0, rows], kept.at[c])
+        copies.append((across, onward, own))
+    last = links.group == links.groups - 1
+
+    def start(c):
+        rows = pl.ds(c * ROWS, ROWS)
+        across, onward, own = copies[c]
+        for s in order:
+            at = columns(links.place ^ s, cols)
+            ready[s, rows, :] = (dot(low[rows, :], w[:, at]) + bq[:, at]).astype(BF16)
+            if s:
+                across[s].start()
+            else:
+                own.start()
+
+            @pl.when(jnp.logical_not(last))
+            def _():
+                onward[s].start()
+
+    def finish():
+        for across, onward, own in copies:
+            own.wait()
+            for s in order:
+                if s:
+                    across[s].wait()
+
+                @pl.when(jnp.logical_not(last))
+                def _():
+                    onward[s].wait_send()
+
+                @pl.when(links.group > 0)
+                def _():
+                    onward[s].wait_recv()
+
+    return start, finish
+
+
+def qkv_copies(rows):
+    return rows // ROWS * (2 * GROUP - 1)
+
+
+def first_body(
+    base, gain, bias, w_all, bq, stream, low, pieces, kv_back, w, ready, send, recv, load, kept
+):
+    links = Links(send, recv)
+    loaded = pltpu.make_async_copy(w_all, w, load.at[0])
+    loaded.start()
+    links.greet(
+        [links.peer(s) for s in range(1, GROUP)]
+        + [links.beyond(1, s) for s in range(GROUP)]
+        + [links.beyond(links.groups - 1, s) for s in range(GROUP)]
+    )
+    start, finish = send_qkv(links, low, w, bq, ready, pieces, kv_back, kept)
+    chunks = base.shape[0] // ROWS
+    for c in range(chunks):
+        norm_rows(c * ROWS, base, None, gain, bias, stream, low)
+        if c == 0:
+            loaded.wait()
+        start(c)
+    finish()
+
+
+ANY = pl.BlockSpec(memory_space=pl.ANY)
+VMEM = pl.BlockSpec(memory_space=pltpu.VMEM)
+
+
+def run_links(body, name, ins, outs, scratch, flops, moved):
+    return pl.pallas_call(
+        body,
+        in_specs=[spec for spec, _ in ins],
+        out_specs=[spec for spec, _ in outs],
+        out_shape=[out for _, out in outs],
+        scratch_shapes=list(scratch),
+        compiler_params=pltpu.CompilerParams(
+            vmem_limit_bytes=VMEM_BYTES, collective_id=name, has_side_effects=True
+        ),
+        cost_estimate=pl.CostEstimate(flops=flops, bytes_accessed=moved, transcendentals=0),
+    )(*[array for _, array in ins])
+
+
+def first_segment(base, gain, bias, weights, bq):
+    rows, width = base.shape
+    total = bq.shape[1]
+    cols = total // GROUP
+    copies = pltpu.SemaphoreType.DMA((qkv_copies(rows),))
+    return run_links(
+        first_body,
+        0,
+        [(VMEM, base), (VMEM, gain), (VMEM, bias), (ANY, weights), (VMEM, bq)],
+        [
+            (VMEM, shape((rows, width), F32)),
+            (VMEM, shape((rows, width), BF16)),
+            (ANY, shape((GROUP, rows, cols), BF16)),
+            (ANY, shape((GROUP, rows, 2 * cols // 3), BF16)),
+        ],
+        [
+            pltpu.VMEM((width, total), BF16),
+            pltpu.VMEM((GROUP, rows, cols), BF16),
+            copies,
+            copies,
+            pltpu.SemaphoreType.DMA((1,)),
+            pltpu.SemaphoreType.DMA((rows // ROWS,)),
+        ],
+        flops=2 * rows * width * total,
+        moved=rows * width * 8 + width * total * 2,
+    )
+
+
+def trade_mixed(links, mixed_all, mixed):
+    cols = mixed_all.shape[2]
+    copies = []
+    for c in range(mixed.shape[0] // ROWS):
+        rows = pl.ds(c * ROWS, ROWS)
+        copies.append(
+            [
+                links.copy(
+                    mixed_all.at[s, rows],
+                    mixed.at[rows, columns(links.place, cols)],
+                    links.peer(s),
+                )
+                for s in (2, 3, 1)
+            ]
+        )
+
+    def start():
+        for chunk in copies:
+            for one in chunk:
+                one.start()
+        mixed[:, columns(links.place, cols)] = mixed_all[0]
+
+    def wait(c):
+        for one in copies[c]:
+            one.wait_recv()
+
+    def finish():
+        for chunk in copies:
+            for one in chunk:
+                one.wait_send()
+
+    return start, wait, finish
+
+
+def between_body(
+    at, mixed_all, base, bout, gain_two, bias_two, bfc, bproj, gain, bias, bq, rest, qkv,
+    mixed, middle, low_two, hidden, act, stream, low, pieces, kv_back,
+    w_out, w_fc, w_proj, w_qkv, part, got, part_two, got_two, ready, send, recv, load, kept
+):
+    fc_at, proj_at, first = at
+    links = Links(send, recv)
+    loads = [
+        pltpu.make_async_copy(source.at[:, pl.ds(start, target.shape[1])], target, load.at[i])
+        for i, (source, start, target) in enumerate(
+            ((rest, 0, w_out), (rest, fc_at, w_fc), (rest, proj_at, w_proj), (qkv, first, w_qkv))
+        )
+    ]
+    for one in loads:
+        one.start()
+    links.greet(
+        [links.peer(s) for s in range(1, GROUP)]
+        + [links.beyond(1, s) for s in range(GROUP)]
+        + [links.beyond(links.groups - 1, s) for s in range(GROUP)]
+        + [{"tp": links.other}]
+    )
+    chunks = [pl.ds(c * ROWS, ROWS) for c in range(base.shape[0] // ROWS)]
+    start_mixed, wait_mixed, finish_mixed = trade_mixed(links, mixed_all, mixed)
+    swaps = [links.swap(part.at[rows], got.at[rows]) for rows in chunks]
+    swaps_two = [links.swap(part_two.at[rows], got_two.at[rows]) for rows in chunks]
+    start_qkv, finish_qkv = send_qkv(links, low, w_qkv, bq, ready, pieces, kv_back, kept)
+    start_mixed()
+    loads[0].wait()
+    for c, rows in enumerate(chunks):
+        wait_mixed(c)
+        out_rows(rows, mixed, w_out, part)
+        swaps[c].start()
+    loads[1].wait()
+    loads[2].wait()
+    for c, rows in enumerate(chunks):
+        swaps[c].wait()
+        norm_rows(c * ROWS, base, (part, got, bout), gain_two, bias_two, middle, low_two)
+        feed_rows(rows, low_two, w_fc, bfc, hidden, act, w_proj, part_two)
+        swaps_two[c].start()
+    loads[3].wait()
+    for c, rows in enumerate(chunks):
+        swaps_two[c].wait()
+        norm_rows(c * ROWS, middle, (part_two, got_two, bproj), gain, bias, stream, low)
+        start_qkv(c)
+    finish_mixed()
+    finish_qkv()
+
+
+def between_segment(mixed_all, base, vectors, bq, rest, fc_at, proj_at, qkv, first):
+    rows, width = base.shape
+    total = bq.shape[1]
+    cols = total // GROUP
+    out_cols = fc_at
+    units = proj_at - fc_at
+    chunks = rows // ROWS
+    copies = pltpu.SemaphoreType.DMA((qkv_copies(rows) + chunks * (GROUP - 1) + 2 * chunks,))
+    whole_f32 = (VMEM, shape((rows, width), F32))
+    whole_low = (VMEM, shape((rows, width), BF16))
+    return run_links(
+        functools.partial(between_body, (fc_at, proj_at, first)),
+        1,
+        [(VMEM, mixed_all), (VMEM, base)]
+        + [(VMEM, vector) for vector in vectors]
+        + [(VMEM, bq), (ANY, rest), (ANY, qkv)],
+        [
+            (VMEM, shape((rows, out_cols), BF16)),
+            whole_f32,
+            whole_low,
+            (VMEM, shape((rows, units), F32)),
+            (VMEM, shape((rows, units), BF16)),
+            whole_f32,
+            whole_low,
+            (ANY, shape((GROUP, rows, cols), BF16)),
+            (ANY, shape((GROUP, rows, 2 * cols // 3), BF16)),
+        ],
+        [
+            pltpu.VMEM((width, out_cols), BF16),
+            pltpu.VMEM((width, units), BF16),
+            pltpu.VMEM((width, units), BF16),
+            pltpu.VMEM((width, total), BF16),
+        ]
+        + [pltpu.VMEM((rows, width), BF16)] * 4
+        + [
+            pltpu.VMEM((GROUP, rows, cols), BF16),
+            copies,
+            copies,
+            pltpu.SemaphoreType.DMA((4,)),
+            pltpu.SemaphoreType.DMA((chunks,)),
+        ],
+        flops=2 * rows * width * (total + out_cols + 2 * units),
+        moved=rows * width * 20 + rows * units * 6 + width * (total + out_cols + 2 * units) * 2,
+    )
 
 
 def doc_start_rows(sc, docs, positions):
@@ -561,22 +930,25 @@
     return top_new, total
 
 
-def attend_own_body(docs, sc, p0, p1, p2, p3, acc, top_ref, total_ref, q_all, k_all, v_flip):
+def attend_body(docs, sc, p0, kv, mixed, out, log_total, q_all, k_all, v_flip, k_back, v_back, acc):
     block = pl.program_id(0)
-    cols = q_all.shape[1]
+    span, cols = q_all.shape
 
     @pl.when(block == 0)
     def _():
-        pieces = (p0, p1, p2, p3)
+        pieces = (p0,) * GROUP
         spread(sc, pieces, 0, cols, straight=q_all)
         spread(sc, pieces, cols, cols, straight=k_all)
         spread(sc, pieces, 2 * cols, cols, flipped=v_flip)
+        spread(sc, (kv,) * GROUP, 0, cols, straight=k_back)
+        spread(sc, (kv,) * GROUP, cols, cols, flipped=v_back)
 
     position, start, lowest = query_rows(sc, docs, block)
     queries = head_stack(q_all[block_at(block, QB), :], HEAD_DIM**-0.5)
     acc[...] = jnp.zeros_like(acc)
     least = jnp.maximum(lowest - sc[1], 0) // KB
     last = ((block + 1) * QB - 1) // KB
+    before = sc[1] - span
 
     def step(back, carry):
         at = last - back
@@ -584,75 +956,15 @@
             k_all, v_flip, queries, at, sc[1] + at * KB, position, start, acc, carry
         )
 
+    def step_back(at, carry):
+        return flash_step(
+            k_back, v_back, queries, at, before + at * KB, position, start, acc, carry
+        )
+
+    carry = (jnp.full((1, 2 * QB), NEG, F32), jnp.zeros((1, 2 * QB), F32))
+    carry = lax.fori_loop(0, last - least + 1, step, carry)
     top, total = lax.fori_loop(
-        0,
-        last - least + 1,
-        step,
-        (jnp.full((1, 2 * QB), NEG, F32), jnp.zeros((1, 2 * QB), F32)),
-    )
-    for h in range(2):
-        top_ref[h : h + 1, :] = top[:, h * QB : (h + 1) * QB]
-        total_ref[h : h + 1, :] = total[:, h * QB : (h + 1) * QB]
-
-
-def piece_specs(pieces):
-    out = []
-    for array in pieces:
-        dims = array.shape
-        out.append((whole((1,) + dims[1:]) if len(dims) == 3 else whole(dims), array))
-    return out
-
-
-def attend_own(sc, docs, pieces):
-    rows, cols = pieces[1].shape[0], pieces[1].shape[1] // 3
-    span = GROUP * rows
-    stat = (pl.BlockSpec((8, QB), lambda j, sc: (0, j)), shape((8, span), F32))
-    return run_kernel(
-        functools.partial(attend_own_body, docs),
-        (span // QB,),
-        sc,
-        piece_specs(pieces),
-        [(pl.BlockSpec((cols, QB), lambda j, sc: (0, j)), shape((cols, span), F32)), stat, stat],
-        scratch=[
-            pltpu.VMEM((span, cols), BF16),
-            pltpu.VMEM((span, cols), BF16),
-            pltpu.VMEM((cols, span), BF16),
-        ],
-        flops=span * span * cols * 2,
-        moved=span * cols * 10,
-    )
-
-
-def attend_back_body(
-    docs, sc, p0, p1, p2, p3, kv, acc_in, top_in, total_in, mixed, out, log_total, q_all, k_all, v_flip, acc
-):
-    block = pl.program_id(0)
-    cols = q_all.shape[1]
-    span = q_all.shape[0]
-
-    @pl.when(block == 0)
-    def _():
-        spread(sc, (p0, p1, p2, p3), 0, cols, straight=q_all)
-        spread(sc, (kv,) * GROUP, 0, cols, straight=k_all)
-        spread(sc, (kv,) * GROUP, cols, cols, flipped=v_flip)
-
-    position, start, lowest = query_rows(sc, docs, block)
-    queries = head_stack(q_all[block_at(block, QB), :], HEAD_DIM**-0.5)
-    acc[...] = acc_in[...]
-    before = sc[1] - span
-    least = jnp.maximum(lowest - before, 0) // KB
-
-    def step(at, carry):
-        return flash_step(k_all, v_flip, queries, at, before + at * KB, position, start, acc, carry)
-
-    top, total = lax.fori_loop(
-        least,
-        span // KB,
-        step,
-        (
-            jnp.concatenate([top_in[h : h + 1, :] for h in range(2)], 1),
-            jnp.concatenate([total_in[h : h + 1, :] for h in range(2)], 1),
-        ),
+        jnp.minimum(jnp.maximum(lowest - before, 0), span) // KB, span // KB, step_back, carry
     )
     sums = top + jnp.log(total)
     share = 1.0 / total
@@ -671,35 +983,25 @@
     return pl.BlockSpec((1, QB, cols), lambda j, sc: ((j // per) ^ sc[0], j % per, 0))
 
 
-def attend_back(sc, docs, pieces, kv, acc, top, total):
-    rows, cols = pieces[1].shape[0], pieces[1].shape[1] // 3
+def attend(sc, docs, pieces, kv):
+    rows, cols = pieces.shape[1], pieces.shape[2] // 3
     span = GROUP * rows
-    stat = pl.BlockSpec((8, QB), lambda j, sc: (0, j))
-    ins = piece_specs(pieces) + [
-        (whole(kv.shape), kv),
-        (pl.BlockSpec((cols, QB), lambda j, sc: (0, j)), acc),
-        (stat, top),
-        (stat, total),
-    ]
-    outs = [
-        (slot_spec(rows, cols), shape((GROUP, rows, cols), BF16)),
-        (pl.BlockSpec((QB, cols), lambda j, sc: (j, 0)), shape((span, cols), F32)),
-        (stat, shape((8, span), F32)),
-    ]
+    stat = (pl.BlockSpec((8, QB), lambda j, sc: (0, j)), shape((8, span), F32))
+    low = pltpu.VMEM((span, cols), BF16)
+    low_flip = pltpu.VMEM((cols, span), BF16)
     return run_kernel(
-        functools.partial(attend_back_body, docs),
+        functools.partial(attend_body, docs),
         (span // QB,),
         sc,
-        ins,
-        outs,
-        scratch=[
-            pltpu.VMEM((span, cols), BF16),
-            pltpu.VMEM((span, cols), BF16),
-            pltpu.VMEM((cols, span), BF16),
-            pltpu.VMEM((cols, QB), F32),
+        [(whole(pieces.shape), pieces), (whole(kv.shape), kv)],
+        [
+            (slot_spec(rows, cols), shape((GROUP, rows, cols), BF16)),
+            (pl.BlockSpec((QB, cols), lambda j, sc: (j, 0)), shape((span, cols), F32)),
+            stat,
         ],
-        flops=span * span * cols * 2,
-        moved=span * cols * 16,
+        scratch=[low, low, low_flip, low, low_flip, pltpu.VMEM((cols, QB), F32)],
+        flops=span * span * cols * 4,
+        moved=span * cols * 20,
     )
 
 
@@ -733,9 +1035,9 @@
     return queries, grads, log_rows, delta
 
 
-def pull_back_body(
-    docs, sc, p0, p1, p2, p3, g0, g1, g2, g3, kv, out, log_total, grad_q, grad_kv,
-    q_all, g_all, k_all, v_all, k_flip, grad_k, grad_v
+def pull_body(
+    docs, sc, p0, g0, kv, out, log_total, grad_q_out, grad_kv, grad_kv_back,
+    q_all, g_all, k_all, v_all, k_flip, grad_k, grad_v, k_back, v_back, k_back_flip, grad_k_back, grad_v_back, grad_q
 ):
     block = pl.program_id(0)
     span, cols = q_all.shape
@@ -743,35 +1045,37 @@
 
     @pl.when(block == 0)
     def _():
-        spread(sc, (p0, p1, p2, p3), 0, cols, straight=q_all)
-        spread(sc, (g0, g1, g2, g3), 0, cols, straight=g_all)
-        spread(sc, (kv,) * GROUP, 0, cols, straight=k_all, flipped=k_flip)
-        spread(sc, (kv,) * GROUP, cols, cols, straight=v_all)
-        grad_k[...] = jnp.zeros_like(grad_k)
-        grad_v[...] = jnp.zeros_like(grad_v)
+        pieces = (p0,) * GROUP
+        spread(sc, pieces, 0, cols, straight=q_all)
+        spread(sc, (g0,) * GROUP, 0, cols, straight=g_all)
+        spread(sc, pieces, cols, cols, straight=k_all, flipped=k_flip)
+        spread(sc, pieces, 2 * cols, cols, straight=v_all)
+        spread(sc, (kv,) * GROUP, 0, cols, straight=k_back, flipped=k_back_flip)
+        spread(sc, (kv,) * GROUP, cols, cols, straight=v_back)
+        for total in (grad_k, grad_v, grad_k_back, grad_v_back):
+            total[...] = jnp.zeros_like(total)
 
     grad_q[...] = jnp.zeros_like(grad_q)
     position, start, lowest = query_rows(sc, docs, block)
-
-    @pl.when(lowest < sc[1])
-    def _():
-        queries, grads, log_rows, delta = pull_rows(block, q_all, g_all, out, log_total)
-
-        def step(at, carry):
-            pull_step(
-                at,
-                before + at * KB,
-                position,
-                start,
-                queries,
-                grads,
-                log_rows,
-                delta,
-                (k_all, v_all, k_flip, grad_k, grad_v, grad_q),
-            )
-            return carry
-
-        lax.fori_loop(jnp.maximum(lowest - before, 0) // KB, span // KB, step, 0)
+    queries, grads, log_rows, delta = pull_rows(block, q_all, g_all, out, log_total)
+
+    def step(first, refs, at, carry):
+        pull_step(at, first + at * KB, position, start, queries, grads, log_rows, delta, refs)
+        return carry
+
+    own_refs = (k_all, v_all, k_flip, grad_k, grad_v, grad_q)
+    back_refs = (k_back, v_back, k_back_flip, grad_k_back, grad_v_back, grad_q)
+    last = ((block + 1) * QB - 1) // KB
+    lax.fori_loop(
+        jnp.maximum(lowest - sc[1], 0) // KB, last + 1, functools.partial(step, sc[1], own_refs), 0
+    )
+    lax.fori_loop(
+        jnp.minimum(jnp.maximum(lowest - before, 0), span) // KB,
+        span // KB,
+        functools.partial(step, before, back_refs),
+        0,
+    )
+    grad_q_out[0] = (grad_q[...] * HEAD_DIM**-0.5).T.astype(BF16)
 
     @pl.when(block == pl.num_programs(0) - 1)
     def _():
@@ -779,119 +1083,34 @@
             at = place_rows(sc, s, span // GROUP)
             grad_kv[s, :, :cols] = grad_k[at, :].astype(BF16)
             grad_kv[s, :, cols:] = grad_v[at, :].astype(BF16)
-
-
-def pull_back(sc, docs, pieces, grads, kv, out, log_total):
-    rows, cols = pieces[1].shape[0], pieces[1].shape[1] // 3
+            grad_kv_back[s, :, :cols] = grad_k_back[at, :].astype(BF16)
+            grad_kv_back[s, :, cols:] = grad_v_back[at, :].astype(BF16)
+
+
+def attend_pull(sc, docs, pieces, grads, kv, out, log_total):
+    rows, cols = pieces.shape[1], pieces.shape[2] // 3
     span = GROUP * rows
-    ins = piece_specs(pieces) + piece_specs(grads) + [
+    ins = [
+        (whole(pieces.shape), pieces),
+        (whole(grads.shape), grads),
         (whole(kv.shape), kv),
         (pl.BlockSpec((QB, cols), lambda j, sc: (j, 0)), out),
         (pl.BlockSpec((8, QB), lambda j, sc: (0, j)), log_total),
     ]
-    outs = [
-        (pl.BlockSpec((cols, QB), lambda j, sc: (0, j)), shape((cols, span), F32)),
-        (whole((GROUP, rows, 2 * cols)), shape((GROUP, rows, 2 * cols), BF16)),
-    ]
+    both = (whole((GROUP, rows, 2 * cols)), shape((GROUP, rows, 2 * cols), BF16))
     low = pltpu.VMEM((span, cols), BF16)
+    low_flip = pltpu.VMEM((cols, span), BF16)
+    high = pltpu.VMEM((span, cols), F32)
     return run_kernel(
-        functools.partial(pull_back_body, docs),
+        functools.partial(pull_body, docs),
         (span // QB,),
         sc,
         ins,
-        outs,
-        scratch=[
-            low,
-            low,
-            low,
-            low,
-            pltpu.VMEM((cols, span), BF16),
-            pltpu.VMEM((span, cols), F32),
-            pltpu.VMEM((span, cols), F32),
-        ],
-        flops=span * span * cols * 4,
-        moved=span * cols * 20,
-    )
-
-
-def pull_own_body(
-    docs, sc, p0, p1, p2, p3, g0, g1, g2, g3, out, log_total, grad_q_in, grad_q_out, grad_kv,
-    q_all, g_all, k_all, v_all, k_flip, grad_k, grad_v, grad_q
-):
-    block = pl.program_id(0)
-    span, cols = q_all.shape
-
-    @pl.when(block == 0)
-    def _():
-        pieces = (p0, p1, p2, p3)
-        spread(sc, pieces, 0, cols, straight=q_all)
-        spread(sc, (g0, g1, g2, g3), 0, cols, straight=g_all)
-        spread(sc, pieces, cols, cols, straight=k_all, flipped=k_flip)
-        spread(sc, pieces, 2 * cols, cols, straight=v_all)
-        grad_k[...] = jnp.zeros_like(grad_k)
-        grad_v[...] = jnp.zeros_like(grad_v)
-
-    grad_q[...] = grad_q_in[...]
-    position, start, lowest = query_rows(sc, docs, block)
-    queries, grads, log_rows, delta = pull_rows(block, q_all, g_all, out, log_total)
-
-    def step(at, carry):
-        pull_step(
-            at,
-            sc[1] + at * KB,
-            position,
-            start,
-            queries,
-            grads,
-            log_rows,
-            delta,
-            (k_all, v_all, k_flip, grad_k, grad_v, grad_q),
-        )
-        return carry
-
-    last = ((block + 1) * QB - 1) // KB
-    lax.fori_loop(jnp.maximum(lowest - sc[1], 0) // KB, last + 1, step, 0)
-    grad_q_out[0] = (grad_q[...] * HEAD_DIM**-0.5).T.astype(BF16)
-
-    @pl.when(block == pl.num_programs(0) - 1)
-    def _():
-        for s in range(GROUP):
-            at = place_rows(sc, s, span // GROUP)
-            grad_kv[s, :, :cols] = grad_k[at, :]
-            grad_kv[s, :, cols:] = grad_v[at, :]
-
-
-def pull_own(sc, docs, pieces, grads, out, log_total, grad_q):
-    rows, cols = pieces[1].shape[0], pieces[1].shape[1] // 3
-    span = GROUP * rows
-    ins = piece_specs(pieces) + piece_specs(grads) + [
-        (pl.BlockSpec((QB, cols), lambda j, sc: (j, 0)), out),
-        (pl.BlockSpec((8, QB), lambda j, sc: (0, j)), log_total),
-        (pl.BlockSpec((cols, QB), lambda j, sc: (0, j)), grad_q),
-    ]
-    outs = [
-        (slot_spec(rows, cols), shape((GROUP, rows, cols), BF16)),
-        (whole((GROUP, rows, 2 * cols)), shape((GROUP, rows, 2 * cols), F32)),
-    ]
-    low = pltpu.VMEM((span, cols), BF16)
-    return run_kernel(
-        functools.partial(pull_own_body, docs),
-        (span // QB,),
-        sc,
-        ins,
-        outs,
-        scratch=[
-            low,
-            low,
-            low,
-            low,
-            pltpu.VMEM((cols, span), BF16),
-            pltpu.VMEM((span, cols), F32),
-            pltpu.VMEM((span, cols), F32),
-            pltpu.VMEM((cols, QB), F32),
-        ],
-        flops=span * span * cols * 5,
-        moved=span * cols * 24,
+        [(slot_spec(rows, cols), shape((GROUP, rows, cols), BF16)), both, both],
+        scratch=[low, low, low, low, low_flip, high, high, low, low, low_flip, high, high]
+        + [pltpu.VMEM((cols, QB), F32)],
+        flops=span * span * cols * 9,
+        moved=span * cols * 30,
     )
 
 
@@ -924,8 +1143,43 @@
     return lax.all_gather(shard, "fsdp", axis=0, tiled=True)
 
 
-def scatter_sum(full):
-    return lax.psum_scatter(full, "fsdp", scatter_dimension=0, tiled=True)
+def tie(*values):
+    return lax.optimization_barrier(values)
+
+
+class SlotSum:
+    def __init__(self, halves):
+        self.keep, self.send = halves
+        self.groups = lax.axis_size("fsdp") // GROUP
+
+    def add(self, rows):
+        total = self.keep[rows].astype(F32)
+        for part in self.parts:
+            total = total + part[rows].astype(F32)
+        return total
+
+    def to_core(self):
+        self.parts = [swap_fsdp(self.send, 1)]
+
+    def to_x(self):
+        half = self.keep.shape[0] // 2
+        self.parts.append(swap_fsdp(self.add(slice(half, None)).astype(BF16), 2))
+
+    def to_groups(self):
+        rows = self.keep.shape[0] // 2 // self.groups
+        size = lax.axis_size("fsdp")
+        self.near = self.add(slice(0, rows))
+        self.far = []
+        for onward in range(1, self.groups):
+            part = self.add(slice(onward * rows, (onward + 1) * rows)).astype(BF16)
+            pairs = [(i, (i + GROUP * onward) % size) for i in range(size)]
+            self.far.append(lax.ppermute(part, "fsdp", pairs))
+
+    def result(self):
+        total = self.near
+        for part in self.far:
+            total = total + part.astype(F32)
+        return total
 
 
 def shards(
@@ -989,37 +1243,45 @@
     def row(vector):
         return vector.reshape(1, vector.shape[0])
 
-    stream, sums = tokens, None
     stored = []
+    stream, low_one, pieces, kv_back = first_segment(
+        tokens, row(ln1_gain[0]), row(ln1_bias[0]), full_a, bias_qkv(0)
+    )
     for l in range(LAYERS):
-        weights, first = qkv_of[l]
-        stream, low_one, pieces = norm_qkv(
-            sc, stream, sums, row(ln1_gain[l]), row(ln1_bias[l]), weights, first // (3 * cols), bias_qkv(l)
-        )
-        pieces = trade(pieces)
-        kv = jnp.stack([pieces[0][0, :, cols:]] + [piece[:, cols:] for piece in pieces[1:]])
-        kv_back = shift_fsdp(kv, GROUP)
-        acc, top, total = attend_own(sc, docs, pieces)
-        mixed, out, log_total = attend_back(sc, docs, pieces, kv_back, acc, top, total)
-        mixed = trade(mixed)
-        mixed_full, part = out_proj(sc, mixed[0], mixed[1:], rest_of[l])
-        middle, low_two, hidden, act, part_two = feed(
-            sc,
-            stream,
-            part,
-            swap_tp(part),
-            row(b_out[l]),
-            row(ln2_gain[l]),
-            row(ln2_bias[l]),
-            rest_of[l],
-            fc_at,
-            proj_at,
-            row(b_fc[l]),
-        )
-        stored.append(
-            (stream, low_one, pieces, kv_back, out, log_total, mixed_full, middle, low_two, hidden, act)
-        )
-        stream, sums = middle, (part_two, swap_tp(part_two), row(b_proj[l]))
+        mixed, out, log_total = attend(sc, docs, pieces, kv_back)
+        if l + 1 < LAYERS:
+            vectors = (b_out[l], ln2_gain[l], ln2_bias[l], b_fc[l], b_proj[l], ln1_gain[l + 1], ln1_bias[l + 1])
+            mixed_full, middle, low_two, hidden, act, *later = between_segment(
+                mixed,
+                stream,
+                [row(vector) for vector in vectors],
+                bias_qkv(l + 1),
+                rest_of[l],
+                fc_at,
+                proj_at,
+                *qkv_of[l + 1],
+            )
+            kept = (stream, low_one, pieces, kv_back)
+            stream, low_one, pieces, kv_back = later
+        else:
+            kept = (stream, low_one, pieces, kv_back)
+            mixed = trade(mixed)
+            mixed_full, part = out_proj(sc, mixed[0], mixed[1:], rest_of[l])
+            middle, low_two, hidden, act, part_two = feed(
+                sc,
+                stream,
+                part,
+                swap_tp(part),
+                row(b_out[l]),
+                row(ln2_gain[l]),
+                row(ln2_bias[l]),
+                rest_of[l],
+                fc_at,
+                proj_at,
+                row(b_fc[l]),
+            )
+            stream, sums = middle, (part_two, swap_tp(part_two), row(b_proj[l]))
+        stored.append(kept + (out, log_total, mixed_full, middle, low_two, hidden, act))
     own, got, badd = sums
     outputs = (stream + (own.astype(F32) + got.astype(F32)) + badd).astype(BF16)
 
@@ -1032,26 +1294,42 @@
             sc, grad, hidden, rest_of[l], fc_at, proj_at
         )
         got = swap_tp(part)
-        feed_grads = scatter_sum(weight_pull(sc, low_two, grad_hidden, low_proj, act))
+        halves = weight_pull(sc, low_two, grad_hidden, low_proj, act)
+        got, *halves = tie(got, *halves)
+        feed_sum = SlotSum(halves)
+        feed_sum.to_core()
+        if l + 1 < LAYERS:
+            attn_sum.to_groups()
         grad, low_out, grad_mixed, sum_gain_two, sum_bias_two, sum_bout = mid_pull(
             sc, grad, part, got, middle, row(ln2_gain[l]), rest_of[l], out_cols
         )
-        grad_mixed = trade(grad_mixed)
-        grad_q, grad_kv_back = pull_back(sc, docs, pieces, grad_mixed, kv_back, out, log_total)
+        grad_mixed, feed_sum.parts[0] = tie(grad_mixed, feed_sum.parts[0])
+        feed_sum.to_x()
+        grad_mixed = jnp.stack([piece if piece.ndim == 2 else piece[0] for piece in trade(grad_mixed)])
+        grad_q, grad_kv, grad_kv_back = attend_pull(sc, docs, pieces, grad_mixed, kv_back, out, log_total)
         grad_kv_got = shift_fsdp(grad_kv_back, -GROUP)
-        grad_q, grad_kv = pull_own(sc, docs, pieces, grad_mixed, out, log_total, grad_q)
-        grad_pieces = jnp.concatenate([grad_q, (grad_kv + grad_kv_got.astype(F32)).astype(BF16)], 2)
+        grad_q, feed_sum.parts[1] = tie(grad_q, feed_sum.parts[1])
+        feed_sum.to_groups()
+        grad_kv = (grad_kv.astype(F32) + grad_kv_got.astype(F32)).astype(BF16)
+        grad_pieces = jnp.concatenate([grad_q, grad_kv], 2)
         grad_pieces = trade(grad_pieces)
         weights, first = qkv_of[l]
         grad_qkv, part, sum_bqkv = qkv_pull(
             sc, grad_pieces[0], grad_pieces[1:], weights, first // (3 * out_cols)
         )
         got = swap_tp(part)
-        attn_grads = scatter_sum(weight_pull(sc, low_one, grad_qkv, low_out, mixed_full))
+        halves = weight_pull(sc, low_one, grad_qkv, low_out, mixed_full)
+        got, *halves = tie(got, *halves)
+        attn_sum = SlotSum(halves)
+        attn_sum.to_core()
         grad, sum_gain_one, sum_bias_one = first_pull(sc, grad, part, got, stream, row(ln1_gain[l]))
+        grad, attn_sum.parts[0] = tie(grad, attn_sum.parts[0])
+        attn_sum.to_x()
         sums = [sum_gain_one, sum_bias_one, sum_bqkv, sum_bout, sum_gain_two, sum_bias_two, sum_bfc, sum_bproj]
         small[l] = butterfly(jnp.concatenate([jnp.sum(value, 0) for value in sums]))
-        large[l] = (feed_grads, attn_grads)
+        large[l] = (feed_sum, attn_sum)
+    attn_sum.to_groups()
+    large = [[one.result() for one in pair] for pair in large]
 
     def small_parts(vector):
         ends, at = [], 0

time: 1010 us -> 922 us (0.913)
  waiting for transfers between devices: 537 us -> 378 us
  Pallas kernels: 310 us -> 366 us
  other arithmetic: 28.8 us -> 50.9 us
  local copies, waits for them, and re-layouts: 38.6 us -> 17.6 us
  starting transfers between devices: 59.5 us -> 76.2 us
    reduce_scatter x4 -> x0, waiting for transfers between devices: 198 us -> none  [scatter_sum(): return lax.psum_scatter(full, 'fsdp', scatter_dimension=0, tiled=True)]
    pallas_call x0 -> x2, Pallas kernels: none -> 140 us  [run_links(): pl.pallas_call(body, in_specs=[spec for spec, _ in ins], out_specs=[spec...]
    pallas_call x26 -> x18, Pallas kernels: 310 us -> 226 us  [run_kernel(): pl.pallas_call(body, grid_spec=pltpu.PrefetchScalarGridSpec(num_scalar_pr...]
    ppermute x8 -> x6, waiting for transfers between devices: 155 us -> 88.4 us  [swap_tp(): return lax.ppermute(value, 'tp', [(0, 1), (1, 0)])]
    ppermute x0 -> x12, waiting for transfers between devices: none -> 44.9 us  [to_groups(): self.far.append(lax.ppermute(part, 'fsdp', pairs))]
    ppermute x36 -> x35, waiting for transfers between devices: 104 us -> 141 us  [swap_fsdp(): lax.ppermute(value, 'fsdp', [(i, i ^ s) for i in range(lax.axis_size('fsd...]
    all_gather x3, waiting for transfers between devices: 47.4 us -> 77.7 us  [gather(): return lax.all_gather(shard, 'fsdp', axis=0, tiled=True)]
    ppermute x36 -> x35, starting transfers between devices: 34.7 us -> 53.1 us  [swap_fsdp(): lax.ppermute(value, 'fsdp', [(i, i ^ s) for i in range(lax.axis_size('fsd...]
  transfers between devices with their start and end apart: 55 -> 58, of which waited for: 38 -> 31; matrix products, arithmetic and copies ran while one was open for 4% -> 6% of each run, Pallas kernels for 24% -> 34%
where the time goes in v2:
time: 922 us; the launch traced here: 904 us
  waiting for transfers between devices  378 us (41%)
  Pallas kernels  366 us (40%)
  starting transfers between devices  76.2 us (8%)
  other arithmetic  50.9 us (6%)
  local copies, waits for them, and re-layouts  17.6 us (2%)
  between operations  15.3 us (2%)
    pallas_call x18, Pallas kernels, run_kernel(): pl.pallas_call(body, grid_spec=pltpu.PrefetchScalarGridSpec(num_scalar_pr...  226 us
    ppermute x35, waiting for transfers between devices, swap_fsdp(): lax.ppermute(value, 'fsdp', [(i, i ^ s) for i in range(lax.axis_size('fsd...  141 us
    pallas_call x2, Pallas kernels, run_links(): pl.pallas_call(body, in_specs=[spec for spec, _ in ins], out_specs=[spec...  140 us
    ppermute x6, waiting for transfers between devices, swap_tp(): return lax.ppermute(value, 'tp', [(0, 1), (1, 0)])  88.4 us
    all_gather x3, waiting for transfers between devices, gather(): return lax.all_gather(shard, 'fsdp', axis=0, tiled=True)  77.7 us
    ppermute x35, starting transfers between devices, swap_fsdp(): lax.ppermute(value, 'fsdp', [(i, i ^ s) for i in range(lax.axis_size('fsd...  53.1 us
    ppermute x12, waiting for transfers between devices, to_groups(): self.far.append(lax.ppermute(part, 'fsdp', pairs))  44.9 us
    ppermute x2, waiting for transfers between devices, shift_fsdp(): lax.ppermute(value, 'fsdp', [(i, i + by) for i in range(size) if 0 <= i +...  26.4 us
  transfers between devices with their start and end apart: 58, of which 31 were waited for; matrix products, arithmetic and copies ran while one was open for 6% of the time, Pallas kernels for 34%

profile of v2, /device:TPU:0, one launch (start us, length us, event | category | flops | bytes accessed | tf_op | source)
XLA Modules:
  0.0 904.0 jit_solution(11685116388735500639)
XLA Ops:
  30.3 28.5 %all-gather.4.cloned.1.call-done.w_all.w = bf16[1024,1536]{1,0:T(8,128)(2,1)} async-done(((bf16[64,1536]{1,0:T(8,128)(2,1)}), bf16[1024,1536]{1,0:T(8,128)(2,1)}) %all-gather.4.cloned.1.call-update) | async-done | bytes 3145744 | tf_op jit(solution)/shard_map/all_gather | solution.py:1143
  58.8 46.3 %shard_map.263 = (f32[512,1024]{1,0:T(8,128)}, bf16[512,1024]{1,0:T(8,128)(2,1)}, bf16[4,512,384]{2,1,0:T(8,128)(2,1)}, bf16[4,512,256]{2,1,0:T(8,128)(2,1)}) custom-call(bf16[512,1024]{1,0:T(8,128)(2,1)} %base.1, f32[1,1024]{1,0:T(1,128)} %get-tuple-element.280.gain, f32[1,1024]{1,0:T(1,128)} %get-tuple-element.283.bias, ...), custom_call_target="tpu_custom_call" | custom-call | flops 1610612736 | bytes 7340032 | tf_op jit(solution)/shard_map/pallas_call | solution.py:684
  105.1 22.2 %shard_map.264 = (bf16[4,512,128]{2,1,0:T(8,128)(2,1)}, f32[2048,128]{1,0:T(8,128)}, f32[8,2048]{1,0:T(8,128)}) custom-call(s32[10]{0:T(128)} %pad_add_fusion.sc, bf16[4,512,384]{2,1,0:T(8,128)(2,1)} %get-tuple-element.112.p0, bf16[4,512,256]{2,1,0:T(8,128)(2,1)} %get-tuple-element.113.kv), custom_call_target="tpu_custom_call" | custom-call | flops 2147483648 | bytes 5242880 | tf_op jit(solution)/shard_map/pallas_call | solution.py:46
  127.3 49.2 %all-gather.6.cloned.1.call-done.rest.qkv.w.proj.fc = bf16[1024,6144]{1,0:T(8,128)(2,1)} async-done(((bf16[64,6144]{1,0:T(8,128)(2,1)}), bf16[1024,6144]{1,0:T(8,128)(2,1)}) %all-gather.6.cloned.1.call-update) | async-done | bytes 12582928 | tf_op jit(solution)/shard_map/all_gather | solution.py:1143
  176.5 93.6 %shard_map.265 = (bf16[512,512]{1,0:T(8,128)(2,1)}, f32[512,1024]{1,0:T(8,128)}, bf16[512,1024]{1,0:T(8,128)(2,1)}, f32[512,2048]{1,0:T(8,128)}, bf16[512,2048]{...) custom-call(bf16[4,512,128]{2,1,0:T(8,128)(2,1)} %get-tuple-element., ...), custom_call_target="tpu_custom_call" | custom-call | flops 6442450944 | bytes 29360128 | tf_op jit(solution)/shard_map/pallas_call | solution.py:684
  270.1 22.6 %shard_map.266 = (bf16[4,512,128]{2,1,0:T(8,128)(2,1)}, f32[2048,128]{1,0:T(8,128)}, f32[8,2048]{1,0:T(8,128)}) custom-call(s32[10]{0:T(128)} %pad_add_fusion.sc, bf16[4,512,384]{2,1,0:T(8,128)(2,1)} %get-tuple-element.117.p0, bf16[4,512,256]{2,1,0:T(8,128)(2,1)} %get-tuple-element.118.kv), custom_call_target="tpu_custom_call" | custom-call | flops 2147483648 | bytes 5242880 | tf_op jit(solution)/shard_map/pallas_call | solution.py:46
  311.6 23.1 %collective-permute-done.7.got = bf16[512,1024]{1,0:T(8,128)(2,1)S(1)} collective-permute-done((bf16[512,1024]{1,0:T(8,128)(2,1)}, bf16[512,1024]{1,0:T(8,128)(2,1)S(1)}, u32[]{:S(2)}, u32[]{:S(2)}) %collective-permute-start.7) | collective-permute-done | bytes 1048608 | tf_op jit(solution)/shard_map/ppermute | solution.py:1118
  335.6 15.4 %shard_map.268 = (f32[512,1024]{1,0:T(8,128)}, bf16[512,1024]{1,0:T(8,128)(2,1)}, f32[512,2048]{1,0:T(8,128)}, bf16[512,2048]{1,0:T(8,128)(2,1)}, bf16[512,1024]{1,0:T(8,128)(2,1)}) custom-call(s32[10]{0:T(128)} %pad_add_fusion.sc, f32[512,1024]{1,0:T(8,128)} %get-tuple-element.116.base.inputs, bf16[512,1024]{1,0:T(8,128)(2,1)} %get-tuple-element.120.own, ...), custom_call_target="tpu_custom_call" | custom-call | flops 4294967296 | bytes 23068672 | tf_op jit(solution)/shard_map/pallas_call | solution.py:46
  351.1 15.1 %shard_map.269 = (bf16[512,1024]{1,0:T(8,128)(2,1)}, f32[8,1024]{1,0:T(8,128)}, bf16[512,2048]{1,0:T(8,128)(2,1)}, f32[8,2048]{1,0:T(8,128)}, bf16[512,1024]{1,0:T(8,128)(2,1)}) custom-call(s32[10]{0:T(128)} %pad_add_fusion.sc, f32[512,1024]{1,0:T(8,128)} %convert_multiply_fusion.grad, f32[512,2048]{1,0:T(8,128)} %get-tuple-element.123.hidden, ...), custom_call_target="tpu_custom_call" | custom-call | flops 4294967296 | bytes 18874368 | tf_op jit(solution)/shard_map/pallas_call | solution.py:46
  366.7 12.0 %shard_map.270 = (bf16[512,4096]{1,0:T(8,128)(2,1)}, bf16[512,4096]{1,0:T(8,128)(2,1)}) custom-call(s32[10]{0:T(128)} %pad_add_fusion.sc, bf16[512,1024]{1,0:T(8,128)(2,1)} %get-tuple-element.125.x0, bf16[512,2048]{1,0:T(8,128)(2,1)} %get-tuple-element.126.g0, bf16[512,1024]{1,0:T(8,128)(2,1)} %get-tuple-element.127.x1, bf16[512,2048]{1,0:T(8,128)(2,1)} %get-tuple-element.128.g1), custom_call_target="tpu_custom_call" | custom-call | flops 4294967296 | bytes 14680064 | tf_op jit(solution)/shard_map/pallas_call | solution.py:46
  378.7 12.1 %collective-permute-done.9.got = bf16[512,1024]{1,0:T(8,128)(2,1)S(1)} collective-permute-done((bf16[512,1024]{1,0:T(8,128)(2,1)}, bf16[512,1024]{1,0:T(8,128)(2,1)S(1)}, u32[]{:S(2)}, u32[]{:S(2)}) %collective-permute-start.9) | collective-permute-done | bytes 1048608 | tf_op jit(solution)/shard_map/ppermute | solution.py:1118
  406.4 47.5 %collective-permute-done.12 = bf16[512,128]{1,0:T(8,128)(2,1)S(1)} collective-permute-done((bf16[512,128]{1,0:T(8,128)(2,1)S(1)}, bf16[512,128]{1,0:T(8,128)(2,1)S(1)}, u32[]{:S(2)}, u32[]{:S(2)}) %collective-permute-start.12) | collective-permute-done | bytes 131104 | tf_op jit(solution)/shard_map/ppermute | solution.py:1122
  455.5 24.6 %shard_map.272 = (bf16[4,512,128]{2,1,0:T(8,128)(2,1)}, bf16[4,512,256]{2,1,0:T(8,128)(2,1)}, bf16[4,512,256]{2,1,0:T(8,128)(2,1)}) custom-call(s32[10]{0:T(128)} %pad_add_fusion.sc, bf16[4,512,384]{2,1,0:T(8,128)(2,1)} %get-tuple-element.117.p0, bf16[4,512,128]{2,1,0:T(8,128)(2,1)} %pad_maximum_fusion.7.g0, bf16[4,512,256]{2,1,0:T(8,128)(2,1)} %get-tuple-element.118.kv, ...), custom_call_target="tpu_custom_call" | custom-call | flops 4831838208 | bytes 7864320 | tf_op jit(solution)/shard_map/pallas_call | solution.py:46
  481.6 26.4 %collective-permute-done.15 = bf16[4,512,256]{2,1,0:T(8,128)(2,1)S(1)} collective-permute-done((bf16[4,512,256]{2,1,0:T(8,128)(2,1)}, bf16[4,512,256]{2,1,0:T(8,128)(2,1)S(1)}, u32[]{:S(2)}, u32[]{:S(2)}) %collective-permute-start.15) | collective-permute-done | bytes 1048608 | tf_op jit(solution)/shard_map/ppermute | solution.py:1127
  544.7 17.1 %collective-permute-done.19.got = bf16[512,1024]{1,0:T(8,128)(2,1)S(1)} collective-permute-done((bf16[512,1024]{1,0:T(8,128)(2,1)}, bf16[512,1024]{1,0:T(8,128)(2,1)S(1)}, u32[]{:S(2)}, u32[]{:S(2)}) %collective-permute-start.19) | collective-permute-done | bytes 1048608 | tf_op jit(solution)/shard_map/ppermute | solution.py:1118
  569.4 15.1 %shard_map.276 = (bf16[512,1024]{1,0:T(8,128)(2,1)}, f32[8,1024]{1,0:T(8,128)}, bf16[512,2048]{1,0:T(8,128)(2,1)}, f32[8,2048]{1,0:T(8,128)}, bf16[512,1024]{1,0:T(8,128)(2,1)}) custom-call(s32[10]{0:T(128)} %pad_add_fusion.sc, f32[512,1024]{1,0:T(8,128)} %get-tuple-element.154.grad, f32[512,2048]{1,0:T(8,128)} %get-tuple-element.155.hidden, ...), custom_call_target="tpu_custom_call" | custom-call | flops 4294967296 | bytes 18874368 | tf_op jit(solution)/shard_map/pallas_call | solution.py:46
  585.0 12.1 %shard_map.277 = (bf16[512,4096]{1,0:T(8,128)(2,1)}, bf16[512,4096]{1,0:T(8,128)(2,1)}) custom-call(s32[10]{0:T(128)} %pad_add_fusion.sc, bf16[512,1024]{1,0:T(8,128)(2,1)} %get-tuple-element.157.x0, bf16[512,2048]{1,0:T(8,128)(2,1)} %get-tuple-element.158.g0, bf16[512,1024]{1,0:T(8,128)(2,1)} %get-tuple-element.159.x1, bf16[512,2048]{1,0:T(8,128)(2,1)} %get-tuple-element.160.g1), custom_call_target="tpu_custom_call" | custom-call | flops 4294967296 | bytes 14680064 | tf_op jit(solution)/shard_map/pallas_call | solution.py:46
  597.2 12.3 %collective-permute-done.21.got = bf16[512,1024]{1,0:T(8,128)(2,1)} collective-permute-done((bf16[512,1024]{1,0:T(8,128)(2,1)}, bf16[512,1024]{1,0:T(8,128)(2,1)}, u32[]{:S(2)}, u32[]{:S(2)}) %collective-permute-start.21) | collective-permute-done | bytes 1048608 | tf_op jit(solution)/shard_map/ppermute | solution.py:1118
  617.5 18.0 %collective-permute-done.8 = bf16[512,1024]{1,0:T(8,128)(2,1)} collective-permute-done((bf16[512,1024]{1,0:T(8,128)(2,1)}, bf16[512,1024]{1,0:T(8,128)(2,1)}, u32[]{:S(2)}, u32[]{:S(2)}) %collective-permute-start.8) | collective-permute-done | bytes 1048608 | tf_op jit(solution)/shard_map/ppermute | solution.py:1118
  639.6 12.2 %collective-permute-done.53 = bf16[64,4096]{1,0:T(8,128)(2,1)S(1)} collective-permute-done((bf16[64,4096]{1,0:T(8,128)(2,1)S(1)}, bf16[64,4096]{1,0:T(8,128)(2,1)S(1)}, u32[]{:S(2)}, u32[]{:S(2)}) %collective-permute-start.53) | collective-permute-done | bytes 524320 | tf_op jit(solution)/shard_map/ppermute | solution.py:1176
  682.2 24.6 %shard_map.279 = (bf16[4,512,128]{2,1,0:T(8,128)(2,1)}, bf16[4,512,256]{2,1,0:T(8,128)(2,1)}, bf16[4,512,256]{2,1,0:T(8,128)(2,1)}) custom-call(s32[10]{0:T(128)} %pad_add_fusion.sc, bf16[4,512,384]{2,1,0:T(8,128)(2,1)} %get-tuple-element.112.p0, bf16[4,512,128]{2,1,0:T(8,128)(2,1)} %pad_maximum_fusion.8.g0, bf16[4,512,256]{2,1,0:T(8,128)(2,1)} %get-tuple-element.113.kv, ...), custom_call_target="tpu_custom_call" | custom-call | flops 4831838208 | bytes 7864320 | tf_op jit(solution)/shard_map/pallas_call | solution.py:46
  709.6 39.7 %collective-permute-done.45 = bf16[256,2048]{1,0:T(8,128)(2,1)} collective-permute-done((bf16[256,2048]{1,0:T(8,128)(2,1)}, bf16[256,2048]{1,0:T(8,128)(2,1)}, u32[]{:S(2)}, u32[]{:S(2)}) %collective-permute-start.45) | collective-permute-done | bytes 1048608 | tf_op jit(solution)/shard_map/ppermute | solution.py:1122
  833.6 11.7 %collective-permute-start.35 = (f32[9728]{0:T(1024)S(1)}, f32[9728]{0:T(1024)S(1)}, u32[]{:S(2)}, u32[]{:S(2)}) collective-permute-start(f32[9728]{0:T(1024)S(1)} %add.222), channel_id=1, source_target_pairs={{0,8},{2,10},{4,12},{6,14},{8,0},{10,2},{12,4},{14,6},{16,24},{18,... | collective-permute-start | bytes 116744 | tf_op jit(solution)/shard_map/ppermute | solution.py:1122
  857.8 16.4 %collective-permute-done.41 = bf16[256,2048]{1,0:T(8,128)(2,1)} collective-permute-done((bf16[256,2048]{1,0:T(8,128)(2,1)}, bf16[256,2048]{1,0:T(8,128)(2,1)}, u32[]{:S(2)}, u32[]{:S(2)}) %collective-permute-start.41) | collective-permute-done | bytes 1048608 | tf_op jit(solution)/shard_map/ppermute | solution.py:1122
  (358 shorter events, 270.8 us)
Async XLA Ops:
  7.2 51.6 %all-gather.4.cloned.1.call-start = ((), (), s32[]{:S(2)}) async-start(), calls=%async_computation | async-start | bytes 3342336 | tf_op jit(solution)/shard_map/all_gather | solution.py:1143
  9.5 167.0 %all-gather.6.cloned.1.call-start = ((), (), s32[]{:S(2)}) async-start(), calls=%async_computation.1 | async-start | bytes 13369344 | tf_op jit(solution)/shard_map/all_gather | solution.py:1143
  11.1 287.0 %all-gather.8.cloned.1.call-start = ((), (), s32[]{:S(2)}) async-start(), calls=%async_computation.2 | async-start | bytes 10027008 | tf_op jit(solution)/shard_map/all_gather | solution.py:1143
  309.3 25.4 %collective-permute-start.7 = (bf16[512,1024]{1,0:T(8,128)(2,1)}, bf16[512,1024]{1,0:T(8,128)(2,1)S(1)}, u32[]{:S(2)}, u32[]{:S(2)}) collective-permute-start(bf16[512,1024]{1,0:T(8,128)(2,1)} %get-tuple-element.120.own), channel_id=1, source_target_pairs={{0,1},{1,0},{2,3},{3,2},{4,5},{5,4},{6,7},{7,6},{8,9},{9,8},{10,11... | collective-permute-start | bytes 3145736 | tf_op jit(solution)/shard_map/ppermute | solution.py:1118
  402.4 107.1 %collective-permute-start.14 = (bf16[256,4096]{1,0:T(8,128)(2,1)S(1)}, bf16[256,4096]{1,0:T(8,128)(2,1)S(1)}, u32[]{:S(2)}, u32[]{:S(2)}) collective-permute-start(bf16[256,4096]{1,0:T(8,128)(2,1)S(1)} %add_convert_fusion.1), channel_id=1, source_target_pairs={{0,4},{2,6},{4,0},{6,2},{8,12},{10,14},{12,8},{14,10},{16,20},{18,... | collective-permute-start | bytes 6291464 | tf_op jit(solution)/shard_map/ppermute | solution.py:1122
  404.5 49.3 %collective-permute-start.12 = (bf16[512,128]{1,0:T(8,128)(2,1)S(1)}, bf16[512,128]{1,0:T(8,128)(2,1)S(1)}, u32[]{:S(2)}, u32[]{:S(2)}) collective-permute-start(bf16[512,128]{1,0:T(8,128)(2,1)S(1)} %get-tuple-element.238), channel_id=1, source_target_pairs={{0,4},{2,6},{4,0},{6,2},{8,12},{10,14},{12,8},{14,10},{16,20},{18,... | collective-permute-start | bytes 393224 | tf_op jit(solution)/shard_map/ppermute | solution.py:1122
  404.7 49.9 %collective-permute-start.13 = (bf16[512,128]{1,0:T(8,128)(2,1)S(1)}, bf16[512,128]{1,0:T(8,128)(2,1)S(1)}, u32[]{:S(2)}, u32[]{:S(2)}) collective-permute-start(bf16[512,128]{1,0:T(8,128)(2,1)S(1)} %get-tuple-element.237), channel_id=1, source_target_pairs={{0,6},{2,4},{4,2},{6,0},{8,14},{10,12},{12,10},{14,8},{16,22},{18,... | collective-permute-start | bytes 393224 | tf_op jit(solution)/shard_map/ppermute | solution.py:1122
  480.1 27.9 %collective-permute-start.15 = (bf16[4,512,256]{2,1,0:T(8,128)(2,1)}, bf16[4,512,256]{2,1,0:T(8,128)(2,1)S(1)}, u32[]{:S(2)}, u32[]{:S(2)}) collective-permute-start(bf16[4,512,256]{2,1,0:T(8,128)(2,1)} %get-tuple-element.143), channel_id=1, source_target_pairs={{8,0},{10,2},{12,4},{14,6},{16,8},{18,10},{20,12},{22,14},{24,16},... | collective-permute-start | bytes 3145736 | tf_op jit(solution)/shard_map/ppermute | solution.py:1127
  536.2 25.6 %collective-permute-start.19 = (bf16[512,1024]{1,0:T(8,128)(2,1)}, bf16[512,1024]{1,0:T(8,128)(2,1)S(1)}, u32[]{:S(2)}, u32[]{:S(2)}) collective-permute-start(bf16[512,1024]{1,0:T(8,128)(2,1)} %get-tuple-element.144.own), channel_id=1, source_target_pairs={{0,1},{1,0},{2,3},{3,2},{4,5},{5,4},{6,7},{7,6},{8,9},{9,8},{10,11... | collective-permute-start | bytes 3145736 | tf_op jit(solution)/shard_map/ppermute | solution.py:1118
  584.5 25.0 %collective-permute-start.21 = (bf16[512,1024]{1,0:T(8,128)(2,1)}, bf16[512,1024]{1,0:T(8,128)(2,1)}, u32[]{:S(2)}, u32[]{:S(2)}) collective-permute-start(bf16[512,1024]{1,0:T(8,128)(2,1)} %get-tuple-element.156.own), channel_id=1, source_target_pairs={{0,1},{1,0},{2,3},{3,2},{4,5},{5,4},{6,7},{7,6},{8,9},{9,8},{10,11... | collective-permute-start | bytes 3145736 | tf_op jit(solution)/shard_map/ppermute | solution.py:1118
  609.5 62.4 %collective-permute-start.22 = (bf16[512,4096]{1,0:T(8,128)(2,1)}, bf16[512,4096]{1,0:T(8,128)(2,1)}, u32[]{:S(2)}, u32[]{:S(2)}) collective-permute-start(bf16[512,4096]{1,0:T(8,128)(2,1)} %get-tuple-element.167), channel_id=1, source_target_pairs={{0,2},{2,0},{4,6},{6,4},{8,10},{10,8},{12,14},{14,12},{16,18},{18,... | collective-permute-start | bytes 12582920 | tf_op jit(solution)/shard_map/ppermute | solution.py:1122
  609.5 26.0 %collective-permute-start.8 = (bf16[512,1024]{1,0:T(8,128)(2,1)}, bf16[512,1024]{1,0:T(8,128)(2,1)}, u32[]{:S(2)}, u32[]{:S(2)}) collective-permute-start(bf16[512,1024]{1,0:T(8,128)(2,1)} %get-tuple-element.122), channel_id=1, source_target_pairs={{0,1},{1,0},{2,3},{3,2},{4,5},{5,4},{6,7},{7,6},{8,9},{9,8},{10,11... | collective-permute-start | bytes 3145736 | tf_op jit(solution)/shard_map/ppermute | solution.py:1118
  613.4 26.1 %collective-permute-start.52 = (bf16[64,4096]{1,0:T(8,128)(2,1)S(1)}, bf16[64,4096]{1,0:T(8,128)(2,1)S(1)}, u32[]{:S(2)}, u32[]{:S(2)}) collective-permute-start(bf16[64,4096]{1,0:T(8,128)(2,1)S(1)} %get-tuple-element.213), channel_id=1, source_target_pairs={{0,8},{2,10},{4,12},{6,14},{8,16},{10,18},{12,20},{14,22},{16,24},... | collective-permute-start | bytes 1572872 | tf_op jit(solution)/shard_map/ppermute | solution.py:1176
  613.5 38.3 %collective-permute-start.53 = (bf16[64,4096]{1,0:T(8,128)(2,1)S(1)}, bf16[64,4096]{1,0:T(8,128)(2,1)S(1)}, u32[]{:S(2)}, u32[]{:S(2)}) collective-permute-start(bf16[64,4096]{1,0:T(8,128)(2,1)S(1)} %get-tuple-element.215), channel_id=1, source_target_pairs={{0,16},{2,18},{4,20},{6,22},{8,24},{10,26},{12,28},{14,30},{16,0},... | collective-permute-start | bytes 1572872 | tf_op jit(solution)/shard_map/ppermute | solution.py:1176
  616.7 35.1 %collective-permute-start.54 = (bf16[64,4096]{1,0:T(8,128)(2,1)S(1)}, bf16[64,4096]{1,0:T(8,128)(2,1)S(1)}, u32[]{:S(2)}, u32[]{:S(2)}) collective-permute-start(bf16[64,4096]{1,0:T(8,128)(2,1)S(1)} %get-tuple-element.214), channel_id=1, source_target_pairs={{0,24},{2,26},{4,28},{6,30},{8,0},{10,2},{12,4},{14,6},{16,8},{18,... | collective-permute-start | bytes 1572872 | tf_op jit(solution)/shard_map/ppermute | solution.py:1176
  653.4 56.0 %collective-permute-start.40 = (f32[9728]{0:T(1024)S(1)}, f32[9728]{0:T(1024)S(1)}, u32[]{:S(2)}, u32[]{:S(2)}) collective-permute-start(f32[9728]{0:T(1024)S(1)} %add.227), channel_id=1, source_target_pairs={{0,16},{2,18},{4,20},{6,22},{8,24},{10,26},{12,28},{14,30},{16,0},... | collective-permute-start | bytes 116744 | tf_op jit(solution)/shard_map/ppermute | solution.py:1122
  677.6 79.5 %collective-permute-start.26 = (bf16[256,4096]{1,0:T(8,128)(2,1)S(1)}, bf16[256,4096]{1,0:T(8,128)(2,1)}, u32[]{:S(2)}, u32[]{:S(2)}) collective-permute-start(bf16[256,4096]{1,0:T(8,128)(2,1)S(1)} %add_convert_fusion), channel_id=1, source_target_pairs={{0,4},{2,6},{4,0},{6,2},{8,12},{10,14},{12,8},{14,10},{16,20},{18,... | collective-permute-start | bytes 6291464 | tf_op jit(solution)/shard_map/ppermute | solution.py:1122
  680.2 69.0 %collective-permute-start.45 = (bf16[256,2048]{1,0:T(8,128)(2,1)}, bf16[256,2048]{1,0:T(8,128)(2,1)}, u32[]{:S(2)}, u32[]{:S(2)}) collective-permute-start(bf16[256,2048]{1,0:T(8,128)(2,1)} %add_convert_fusion.2), channel_id=1, source_target_pairs={{0,4},{2,6},{4,0},{6,2},{8,12},{10,14},{12,8},{14,10},{16,20},{18,... | collective-permute-start | bytes 3145736 | tf_op jit(solution)/shard_map/ppermute | solution.py:1122
  706.9 48.4 %collective-permute-start.27 = (bf16[4,512,256]{2,1,0:T(8,128)(2,1)}, bf16[4,512,256]{2,1,0:T(8,128)(2,1)}, u32[]{:S(2)}, u32[]{:S(2)}) collective-permute-start(bf16[4,512,256]{2,1,0:T(8,128)(2,1)} %get-tuple-element.176), channel_id=1, source_target_pairs={{8,0},{10,2},{12,4},{14,6},{16,8},{18,10},{20,12},{22,14},{24,16},... | collective-permute-start | bytes 3145736 | tf_op jit(solution)/shard_map/ppermute | solution.py:1127
  784.3 25.5 %collective-permute-start.31 = (bf16[512,1024]{1,0:T(8,128)(2,1)}, bf16[512,1024]{1,0:T(8,128)(2,1)S(1)}, u32[]{:S(2)}, u32[]{:S(2)}) collective-permute-start(bf16[512,1024]{1,0:T(8,128)(2,1)} %get-tuple-element.177.own), channel_id=1, source_target_pairs={{0,1},{1,0},{2,3},{3,2},{4,5},{5,4},{6,7},{7,6},{8,9},{9,8},{10,11... | collective-permute-start | bytes 3145736 | tf_op jit(solution)/shard_map/ppermute | solution.py:1118
  788.9 30.7 %collective-permute-start.49 = (bf16[64,4096]{1,0:T(8,128)(2,1)S(1)}, bf16[64,4096]{1,0:T(8,128)(2,1)}, u32[]{:S(2)}, u32[]{:S(2)}) collective-permute-start(bf16[64,4096]{1,0:T(8,128)(2,1)S(1)} %get-tuple-element.210), channel_id=1, source_target_pairs={{0,8},{2,10},{4,12},{6,14},{8,16},{10,18},{12,20},{14,22},{16,24},... | collective-permute-start | bytes 1572872 | tf_op jit(solution)/shard_map/ppermute | solution.py:1176
  793.1 34.1 %collective-permute-start.50 = (bf16[64,4096]{1,0:T(8,128)(2,1)S(1)}, bf16[64,4096]{1,0:T(8,128)(2,1)}, u32[]{:S(2)}, u32[]{:S(2)}) collective-permute-start(bf16[64,4096]{1,0:T(8,128)(2,1)S(1)} %get-tuple-element.212), channel_id=1, source_target_pairs={{0,16},{2,18},{4,20},{6,22},{8,24},{10,26},{12,28},{14,30},{16,0},... | collective-permute-start | bytes 1572872 | tf_op jit(solution)/shard_map/ppermute | solution.py:1176
  793.1 34.1 %collective-permute-start.51 = (bf16[64,4096]{1,0:T(8,128)(2,1)S(1)}, bf16[64,4096]{1,0:T(8,128)(2,1)}, u32[]{:S(2)}, u32[]{:S(2)}) collective-permute-start(bf16[64,4096]{1,0:T(8,128)(2,1)S(1)} %get-tuple-element.211), channel_id=1, source_target_pairs={{0,24},{2,26},{4,28},{6,30},{8,0},{10,2},{12,4},{14,6},{16,8},{18,... | collective-permute-start | bytes 1572872 | tf_op jit(solution)/shard_map/ppermute | solution.py:1176
  818.9 31.2 %collective-permute-start.32 = (bf16[512,2048]{1,0:T(8,128)(2,1)}, bf16[512,2048]{1,0:T(8,128)(2,1)S(1)}, u32[]{:S(2)}, u32[]{:S(2)}) collective-permute-start(bf16[512,2048]{1,0:T(8,128)(2,1)} %get-tuple-element.186), channel_id=1, source_target_pairs={{0,2},{2,0},{4,6},{6,4},{8,10},{10,8},{12,14},{14,12},{16,18},{18,... | collective-permute-start | bytes 6291464 | tf_op jit(solution)/shard_map/ppermute | solution.py:1122
  (89 other events, 907.2 us)
Sparse Core Ops, SparseCore 0:
  10.9 47.8 all-gather.3
  61.7 114.7 all-gather.5
  179.3 107.7 all-gather.7

commit v3 on v2

--- a/solution.py
+++ b/solution.py
@@ -21,7 +21,7 @@
 NEG = -1e30
 F32 = jnp.float32
 BF16 = jnp.bfloat16
-VMEM_BYTES = 56 * 1024 * 1024
+VMEM_BYTES = 62 * 1024 * 1024
 LAST = (((1,), (1,)), ((), ()))
 FIRST = (((0,), (0,)), ((), ()))
 
@@ -87,87 +87,6 @@
     return jnp.sum(rows.reshape(rows.shape[0] // 8, 8, rows.shape[1]), 0)
 
 
-def norm_qkv_body(summed, sc, *refs):
-    if summed:
-        base, own, got, badd, gain, bias, w, bq, stream, low, piece = refs
-    else:
-        base, gain, bias, w, bq, stream, low, piece = refs
-
-    @pl.when(pl.program_id(0) == 0)
-    def _():
-        def rows(at):
-            value = base[at, :].astype(F32)
-            if summed:
-                value = value + (own[at, :].astype(F32) + got[at, :].astype(F32)) + badd[...]
-            stream[at, :] = value
-            unit, _ = norm_parts(value)
-            low[at, :] = (unit * gain[...] + bias[...]).astype(BF16)
-
-        each_rows(base.shape[0], LN_ROWS, rows)
-
-    piece[0] = (dot(low[...], w[...]) + bq[...]).astype(BF16)
-
-
-def norm_qkv(sc, base, sums, gain, bias, weights, first_block, bq):
-    rows, width = base.shape
-    cols = bq.shape[1] // GROUP
-    ins = [(whole(base.shape), base)]
-    if sums is not None:
-        own, got, badd = sums
-        ins += [(whole(own.shape), own), (whole(got.shape), got), (whole(badd.shape), badd)]
-    ins += [
-        (whole(gain.shape), gain),
-        (whole(bias.shape), bias),
-        (pl.BlockSpec((width, cols), lambda s, sc: (0, first_block + (sc[0] ^ s))), weights),
-        (pl.BlockSpec((1, cols), lambda s, sc: (0, sc[0] ^ s)), bq),
-    ]
-    outs = [
-        (whole((rows, width)), shape((rows, width), F32)),
-        (whole((rows, width)), shape((rows, width), BF16)),
-        (pl.BlockSpec((1, rows, cols), lambda s, sc: (s, 0, 0)), shape((GROUP, rows, cols), BF16)),
-    ]
-    return run_kernel(
-        functools.partial(norm_qkv_body, sums is not None),
-        (GROUP,),
-        sc,
-        ins,
-        outs,
-        flops=2 * rows * width * cols * GROUP,
-        moved=rows * width * 12 + width * cols * GROUP * 2,
-    )
-
-
-def out_proj_body(sc, p0, p1, p2, p3, w, full, partial):
-    cols = p1.shape[1]
-    for s, piece in enumerate((p0, p1, p2, p3)):
-        value = piece[0] if s == 0 else piece[...]
-        full[:, pl.ds(pl.multiple_of((sc[0] ^ s) * cols, cols), cols)] = value
-    tile = 256
-    for at in range(0, partial.shape[1], tile):
-        partial[:, at : at + tile] = dot_last(full[...], w[at : at + tile, :]).astype(BF16)
-
-
-def out_proj(sc, mixed_all, got, weights):
-    rows, cols = got[0].shape
-    width = weights.shape[0]
-    ins = [(whole((1, rows, cols)), mixed_all)]
-    ins += [(whole((rows, cols)), piece) for piece in got]
-    ins += [(whole((width, GROUP * cols)), weights)]
-    outs = [
-        (whole((rows, GROUP * cols)), shape((rows, GROUP * cols), BF16)),
-        (whole((rows, width)), shape((rows, width), BF16)),
-    ]
-    return run_kernel(
-        out_proj_body,
-        (1,),
-        sc,
-        ins,
-        outs,
-        flops=2 * rows * width * GROUP * cols,
-        moved=rows * width * 4 + width * GROUP * cols * 2,
-    )
-
-
 def gelu_rows(value):
     return 0.5 * value * (1.0 + jnp.tanh(0.7978845608028654 * (value + 0.044715 * value * value * value)))
 
@@ -177,141 +96,6 @@
     top = jnp.tanh(0.7978845608028654 * (value + 0.044715 * square * value))
     inner = 0.7978845608028654 * (1.0 + 3.0 * 0.044715 * square)
     return 0.5 * (1.0 + top) + 0.5 * value * (1.0 - top * top) * inner
-
-
-def feed_body(
-    sc, base, own, got, badd, gain, bias, fc, bfc, proj, middle, low, hidden, act, partial, total
-):
-    at_chunk = pl.program_id(0)
-
-    @pl.when(at_chunk == 0)
-    def _():
-        def rows(at):
-            value = base[at, :] + (own[at, :].astype(F32) + got[at, :].astype(F32)) + badd[...]
-            middle[at, :] = value
-            unit, _ = norm_parts(value)
-            low[at, :] = (unit * gain[...] + bias[...]).astype(BF16)
-
-        each_rows(base.shape[0], LN_ROWS, rows)
-
-    hidden[...] = dot(low[...], fc[...]) + bfc[...]
-
-    def rows_act(at):
-        act[at, :] = gelu_rows(hidden[at, :]).astype(BF16)
-
-    each_rows(hidden.shape[0], ACT_ROWS, rows_act)
-    part = dot_last(act[...], proj[...])
-
-    @pl.when(at_chunk == 0)
-    def _():
-        total[...] = part
-
-    @pl.when(at_chunk > 0)
-    def _():
-        total[...] += part
-
-    @pl.when(at_chunk == pl.num_programs(0) - 1)
-    def _():
-        partial[...] = total[...].astype(BF16)
-
-
-def feed(sc, base, own, got, badd, gain, bias, weights, fc_at, proj_at, bfc):
-    rows, width = base.shape
-    units, chunk = bfc.shape[1], 512
-    ins = [
-        (whole(base.shape), base),
-        (whole(own.shape), own),
-        (whole(got.shape), got),
-        (whole(badd.shape), badd),
-        (whole(gain.shape), gain),
-        (whole(bias.shape), bias),
-        (pl.BlockSpec((width, chunk), lambda j, sc: (0, fc_at // chunk + j)), weights),
-        (pl.BlockSpec((1, chunk), lambda j, sc: (0, j)), bfc),
-        (pl.BlockSpec((width, chunk), lambda j, sc: (0, proj_at // chunk + j)), weights),
-    ]
-    outs = [
-        (whole((rows, width)), shape((rows, width), F32)),
-        (whole((rows, width)), shape((rows, width), BF16)),
-        (pl.BlockSpec((rows, chunk), lambda j, sc: (0, j)), shape((rows, units), F32)),
-        (pl.BlockSpec((rows, chunk), lambda j, sc: (0, j)), shape((rows, units), BF16)),
-        (whole((rows, width)), shape((rows, width), BF16)),
-    ]
-    return run_kernel(
-        feed_body,
-        (units // chunk,),
-        sc,
-        ins,
-        outs,
-        scratch=[pltpu.VMEM((rows, width), F32)],
-        flops=4 * rows * width * units,
-        moved=rows * width * 16 + width * units * 4 + rows * units * 6,
-    )
-
-
-def feed_pull_body(sc, grad, hidden, proj, fc, low, sum_low, slope_grad, sum_hidden, partial, total, grad_act):
-    at_chunk = pl.program_id(0)
-
-    @pl.when(at_chunk == 0)
-    def _():
-        sum_low[...] = jnp.zeros_like(sum_low)
-
-        def rows(at):
-            value = grad[at, :].astype(BF16)
-            low[at, :] = value
-            sum_low[...] += eight_rows(value.astype(F32))
-
-        each_rows(grad.shape[0], LN_ROWS, rows)
-
-    grad_act[...] = dot(low[...], proj[...])
-    sum_hidden[...] = jnp.zeros_like(sum_hidden)
-
-    def rows_slope(at):
-        value = (grad_act[at, :] * gelu_slope(hidden[at, :])).astype(BF16)
-        slope_grad[at, :] = value
-        sum_hidden[...] += eight_rows(value.astype(F32))
-
-    each_rows(grad.shape[0], ACT_ROWS, rows_slope)
-    part = dot_last(slope_grad[...], fc[...])
-
-    @pl.when(at_chunk == 0)
-    def _():
-        total[...] = part
-
-    @pl.when(at_chunk > 0)
-    def _():
-        total[...] += part
-
-    @pl.when(at_chunk == pl.num_programs(0) - 1)
-    def _():
-        partial[...] = total[...].astype(BF16)
-
-
-def feed_pull(sc, grad, hidden, weights, fc_at, proj_at):
-    rows, width = grad.shape
-    units, chunk = hidden.shape[1], 512
-    ins = [
-        (whole(grad.shape), grad),
-        (pl.BlockSpec((rows, chunk), lambda j, sc: (0, j)), hidden),
-        (pl.BlockSpec((width, chunk), lambda j, sc: (0, proj_at // chunk + j)), weights),
-        (pl.BlockSpec((width, chunk), lambda j, sc: (0, fc_at // chunk + j)), weights),
-    ]
-    outs = [
-        (whole((rows, width)), shape((rows, width), BF16)),
-        (whole((8, width)), shape((8, width), F32)),
-        (pl.BlockSpec((rows, chunk), lambda j, sc: (0, j)), shape((rows, units), BF16)),
-        (pl.BlockSpec((8, chunk), lambda j, sc: (0, j)), shape((8, units), F32)),
-        (whole((rows, width)), shape((rows, width), BF16)),
-    ]
-    return run_kernel(
-        feed_pull_body,
-        (units // chunk,),
-        sc,
-        ins,
-        outs,
-        scratch=[pltpu.VMEM((rows, width), F32), pltpu.VMEM((rows, chunk), F32)],
-        flops=4 * rows * width * units,
-        moved=rows * width * 8 + width * units * 4 + rows * units * 6,
-    )
 
 
 def norm_pull_rows(at, grad, own, got, inputs, gain, grad_new, sum_gain, sum_bias):
@@ -322,183 +106,6 @@
     sum_gain[...] += eight_rows(grad_rows * unit)
     sum_bias[...] += eight_rows(grad_rows)
     return value
-
-
-def mid_pull_body(sc, grad, own, got, inputs, gain, w, grad_new, low, pieces, sum_gain, sum_bias, sum_low, mixed):
-    for total in (sum_gain, sum_bias, sum_low):
-        total[...] = jnp.zeros_like(total)
-
-    def rows(at):
-        value = norm_pull_rows(at, grad, own, got, inputs, gain, grad_new, sum_gain, sum_bias)
-        value = value.astype(BF16)
-        low[at, :] = value
-        sum_low[...] += eight_rows(value.astype(F32))
-
-    each_rows(grad.shape[0], LN_ROWS, rows)
-    mixed[...] = dot(low[...], w[...]).astype(BF16)
-    cols = pieces.shape[2]
-    for s in range(GROUP):
-        pieces[s] = mixed[:, pl.ds(pl.multiple_of((sc[0] ^ s) * cols, cols), cols)]
-
-
-def mid_pull(sc, grad, own, got, inputs, gain, weights, out_cols):
-    rows, width = grad.shape
-    cols = out_cols // GROUP
-    ins = [
-        (whole(grad.shape), grad),
-        (whole(own.shape), own),
-        (whole(got.shape), got),
-        (whole(inputs.shape), inputs),
-        (whole(gain.shape), gain),
-        (whole((width, out_cols)), weights),
-    ]
-    sums = (whole((8, width)), shape((8, width), F32))
-    outs = [
-        (whole((rows, width)), shape((rows, width), F32)),
-        (whole((rows, width)), shape((rows, width), BF16)),
-        (whole((GROUP, rows, cols)), shape((GROUP, rows, cols), BF16)),
-        sums,
-        sums,
-        sums,
-    ]
-    return run_kernel(
-        mid_pull_body,
-        (1,),
-        sc,
-        ins,
-        outs,
-        scratch=[pltpu.VMEM((rows, out_cols), BF16)],
-        flops=2 * rows * width * out_cols,
-        moved=rows * width * 18 + width * out_cols * 2,
-    )
-
-
-def qkv_pull_body(sc, p0, p1, p2, p3, w, full, partial, sums):
-    cols = p1.shape[1]
-    for s, piece in enumerate((p0, p1, p2, p3)):
-        value = piece[0] if s == 0 else piece[...]
-        full[:, pl.ds(pl.multiple_of((sc[0] ^ s) * cols, cols), cols)] = value
-    sums[...] = jnp.zeros_like(sums)
-
-    def rows(at):
-        sums[...] += eight_rows(full[at, :].astype(F32))
-
-    each_rows(full.shape[0], LN_ROWS, rows)
-    tile = 256
-    for at in range(0, partial.shape[1], tile):
-        partial[:, at : at + tile] = dot_last(full[...], w[at : at + tile, :]).astype(BF16)
-
-
-def qkv_pull(sc, own, got, weights, block_at):
-    rows, cols = got[0].shape
-    width, total = weights.shape[0], GROUP * cols
-    ins = [(whole((1, rows, cols)), own)]
-    ins += [(whole((rows, cols)), piece) for piece in got]
-    ins += [(pl.BlockSpec((width, total), lambda j, sc: (0, block_at)), weights)]
-    outs = [
-        (whole((rows, total)), shape((rows, total), BF16)),
-        (whole((rows, width)), shape((rows, width), BF16)),
-        (whole((8, total)), shape((8, total), F32)),
-    ]
-    return run_kernel(
-        qkv_pull_body,
-        (1,),
-        sc,
-        ins,
-        outs,
-        flops=2 * rows * width * total,
-        moved=rows * width * 6 + width * total * 2,
-    )
-
-
-def first_pull_body(sc, grad, own, got, inputs, gain, grad_new, sum_gain, sum_bias):
-    for total in (sum_gain, sum_bias):
-        total[...] = jnp.zeros_like(total)
-
-    def rows(at):
-        norm_pull_rows(at, grad, own, got, inputs, gain, grad_new, sum_gain, sum_bias)
-
-    each_rows(grad.shape[0], LN_ROWS, rows)
-
-
-def first_pull(sc, grad, own, got, inputs, gain):
-    rows, width = grad.shape
-    arrays = (grad, own, got, inputs, gain)
-    sums = (whole((8, width)), shape((8, width), F32))
-    return run_kernel(
-        first_pull_body,
-        (1,),
-        sc,
-        [(whole(array.shape), array) for array in arrays],
-        [(whole((rows, width)), shape((rows, width), F32)), sums, sums],
-        moved=rows * width * 16,
-    )
-
-
-def flip_slots(sc, span, source, plain, flipped):
-    plain[...] = source[...].T
-    width = plain.shape[0]
-    groups = lax.axis_size("fsdp") // GROUP
-    depth = width // (GROUP * groups)
-    mine = sc[1] // span
-    slot = 0
-    for s in (0, 2, 1, 3):
-        for onward in range(groups):
-            owner = lax.rem(mine + onward, groups) * GROUP + (sc[0] ^ s)
-            flipped[slot * depth : (slot + 1) * depth, :] = plain[
-                pl.ds(pl.multiple_of(owner * depth, depth), depth), :
-            ]
-            slot += 1
-
-
-def weight_pull_body(first_steps, sc, x0, g0, x1, g1, keep, send, plain, flipped):
-    at = pl.program_id(0)
-    half = keep.shape[0]
-    span = GROUP * x0.shape[0]
-
-    @pl.when(at == 0)
-    def _():
-        flip_slots(sc, span, x0, plain, flipped)
-
-    @pl.when(at == first_steps)
-    def _():
-        flip_slots(sc, span, x1, plain, flipped)
-
-    @pl.when(at < first_steps)
-    def _():
-        keep[...] = dot(flipped[:half, :], g0[...]).astype(BF16)
-        send[...] = dot(flipped[half:, :], g0[...]).astype(BF16)
-
-    @pl.when(at >= first_steps)
-    def _():
-        keep[...] = dot(flipped[:half, :], g1[...]).astype(BF16)
-        send[...] = dot(flipped[half:, :], g1[...]).astype(BF16)
-
-
-def weight_pull(sc, x0, g0, x1, g1):
-    rows, width = x0.shape
-    chunk = 512
-    n0, n1 = g0.shape[1] // chunk, g1.shape[1] // chunk
-    ins = [
-        (whole(x0.shape), x0),
-        (pl.BlockSpec((rows, chunk), lambda j, sc: (0, jnp.minimum(j, n0 - 1))), g0),
-        (whole(x1.shape), x1),
-        (pl.BlockSpec((rows, chunk), lambda j, sc: (0, jnp.maximum(j - n0, 0))), g1),
-    ]
-    half = (
-        pl.BlockSpec((width // 2, chunk), lambda j, sc: (0, j)),
-        shape((width // 2, (n0 + n1) * chunk), BF16),
-    )
-    return run_kernel(
-        functools.partial(weight_pull_body, n0),
-        (n0 + n1,),
-        sc,
-        ins,
-        [half, half],
-        scratch=[pltpu.VMEM((width, rows), BF16), pltpu.VMEM((width, rows), BF16)],
-        flops=2 * rows * width * (n0 + n1) * chunk,
-        moved=rows * width * 4 + (rows + width) * (n0 + n1) * chunk * 2,
-    )
 
 
 ROWS = 256
@@ -850,6 +457,734 @@
     )
 
 
+def pull_qkv_rows(first, back, links, full, back_got, w, target, sums):
+    cols = full.shape[1] // GROUP
+    rows = pl.ds(first, ROWS)
+
+    @pl.when(links.group < links.groups - 1)
+    def _():
+        for s in range(GROUP):
+            at = pl.ds(
+                pl.multiple_of((links.place ^ s) * cols + cols // 3, cols // 3), 2 * cols // 3
+            )
+            full[rows, at] = (full[rows, at].astype(F32) + back_got[s, rows].astype(F32)).astype(BF16)
+
+    def tile(at):
+        target[rows, at] = dot_last(full[rows, :], w[at, :]).astype(BF16)
+
+    tiles(w.shape[0], 256, tile)
+
+    def body(at):
+        sums[...] += eight_rows(full[at, :].astype(F32))
+
+    rows_within(first, body)
+
+
+def trade_pulls(links, grad_q, grad_kv, grad_kv_back, full, back_got):
+    part = grad_q.shape[2]
+    copies = []
+    for c in range(full.shape[0] // ROWS):
+        rows = pl.ds(c * ROWS, ROWS)
+        across, back = [], []
+        for s in (2, 3, 1):
+            for source, start, size in ((grad_kv, part, 2 * part), (grad_q, 0, part)):
+                at = pl.ds(pl.multiple_of(links.place * 3 * part + start, part), size)
+                across.append(
+                    links.copy(source.at[s, rows], full.at[rows, at], links.peer(s))
+                )
+        for s in (2, 3, 1, 0):
+            back.append(
+                links.copy(
+                    grad_kv_back.at[s, rows],
+                    back_got.at[s, rows],
+                    links.beyond(links.groups - 1, s),
+                )
+            )
+        copies.append((across, back))
+
+    def start():
+        for across, back in copies:
+            for one in across:
+                one.start()
+
+            @pl.when(links.group > 0)
+            def _():
+                for one in back:
+                    one.start()
+
+        first = pl.multiple_of(links.place * 3 * part, part)
+        full[:, pl.ds(first, part)] = grad_q[0]
+        full[:, pl.ds(pl.multiple_of(first + part, part), 2 * part)] = grad_kv[0]
+
+    def wait(c):
+        across, back = copies[c]
+        for one in across:
+            one.wait_recv()
+
+        @pl.when(links.group < links.groups - 1)
+        def _():
+            for one in back:
+                one.wait_recv()
+
+    def finish():
+        for across, back in copies:
+            for one in across:
+                one.wait_send()
+
+            @pl.when(links.group > 0)
+            def _():
+                for one in back:
+                    one.wait_send()
+
+    return start, wait, finish
+
+
+def pull_copies(rows):
+    return rows // ROWS * (2 * (GROUP - 1) + GROUP)
+
+
+def pull_norm_rows(first, grad, own, got, inputs, gain, grad_new, sums, low=None):
+    def body(at):
+        value = norm_pull_rows(at, grad, own, got, inputs, gain, grad_new, sums[0], sums[1])
+        if low is not None:
+            value = value.astype(BF16)
+            low[at, :] = value
+            sums[2][...] += eight_rows(value.astype(F32))
+
+    rows_within(first, body)
+
+
+def round_rows(first, grad, low, sums):
+    def body(at):
+        value = grad[at, :].astype(BF16)
+        low[at, :] = value
+        sums[...] += eight_rows(value.astype(F32))
+
+    rows_within(first, body)
+
+
+def pull_feed_rows(rows, low, proj, hidden, grad_hidden, sums, fc, target):
+    def tile(at):
+        value = dot(low[rows, :], proj[:, at]) * gelu_slope(hidden[rows, at])
+        value = value.astype(BF16)
+        grad_hidden[rows, at] = value
+        sums[:, at] += eight_rows(value.astype(F32))
+
+    tiles(proj.shape[1], 512, tile)
+
+    def tile_out(at):
+        target[rows, at] = dot_last(grad_hidden[rows, :], fc[at, :]).astype(BF16)
+
+    tiles(fc.shape[0], 256, tile_out)
+
+
+def send_mixed_pull(links, low, w, ready, pieces, kept):
+    cols = ready.shape[2]
+    copies = []
+    for c in range(low.shape[0] // ROWS):
+        rows = pl.ds(c * ROWS, ROWS)
+        across = {
+            s: links.copy(ready.at[s, rows], pieces.at[s, rows], links.peer(s))
+            for s in range(1, GROUP)
+        }
+        copies.append((across, pltpu.make_async_copy(ready.at[0, rows], pieces.at[0, rows], kept.at[c])))
+
+    def start(c):
+        rows = pl.ds(c * ROWS, ROWS)
+        across, own = copies[c]
+        for s in (2, 3, 1, 0):
+            at = columns(links.place ^ s, cols)
+            ready[s, rows, :] = dot(low[rows, :], w[:, at]).astype(BF16)
+            (across[s] if s else own).start()
+
+    def finish():
+        for across, own in copies:
+            own.wait()
+            for one in across.values():
+                one.wait()
+
+    return start, finish
+
+
+def load_columns(plan, load):
+    copies = []
+    for i, (source, start, target) in enumerate(plan):
+        if start is not None:
+            source = source.at[:, pl.ds(start, target.shape[1])]
+        copies.append(pltpu.make_async_copy(source, target, load.at[i]))
+    for one in copies:
+        one.start()
+    return copies
+
+
+def turn_body(
+    at, mixed_all, base_in, grad_in, bout, gain_two, bias_two, bfc, rest,
+    mixed, middle, low_two, act, part_two, low_proj, sum_proj, grad_hidden, sum_fc, grad_new, low_out,
+    sum_gain, sum_bias, sum_out, pieces, stay0, go0, stay1, go1,
+    w_out, w_fc, w_proj, base, grad, hidden, part, got, part_three, got_three, ready,
+    plain, flipped, away0, away1, met0, met1, send, recv, load, kept
+):
+    fc_at, proj_at = at
+    links = Links(send, recv)
+    loads = load_columns(
+        (
+            (rest, 0, w_out),
+            (base_in, None, base),
+            (grad_in, None, grad),
+            (rest, fc_at, w_fc),
+            (rest, proj_at, w_proj),
+        ),
+        load,
+    )
+    links.greet([links.peer(s) for s in range(1, GROUP)] + [{"tp": links.other}])
+    chunks = [pl.ds(c * ROWS, ROWS) for c in range(base.shape[0] // ROWS)]
+    start_mixed, wait_mixed, finish_mixed = trade_mixed(links, mixed_all, mixed)
+    swaps = [links.swap(part.at[rows], got.at[rows]) for rows in chunks]
+    swaps_three = [links.swap(part_three.at[rows], got_three.at[rows]) for rows in chunks]
+    start_pull, finish_pull = send_mixed_pull(links, low_out, w_out, ready, pieces, kept)
+    core_sums = (
+        CoreSum(links, stay0, go0, away0, met0),
+        CoreSum(links, stay1, go1, away1, met1),
+    )
+    start_mixed()
+    for total in (sum_proj, sum_fc, sum_gain, sum_bias, sum_out):
+        total[...] = jnp.zeros_like(total)
+    loads[0].wait()
+    for c, rows in enumerate(chunks):
+        wait_mixed(c)
+        out_rows(rows, mixed, w_out, part)
+        swaps[c].start()
+    for one in loads[1:]:
+        one.wait()
+    for c in range(len(chunks)):
+        round_rows(c * ROWS, grad, low_proj, sum_proj)
+    for c, rows in enumerate(chunks):
+        swaps[c].wait()
+        norm_rows(c * ROWS, base, (part, got, bout), gain_two, bias_two, middle, low_two)
+
+        def tile(at):
+            value = dot(low_two[rows, :], w_fc[:, at]) + bfc[:, at]
+            hidden[rows, at] = value
+            act[rows, at] = gelu_rows(value).astype(BF16)
+
+        tiles(w_fc.shape[1], 512, tile)
+        pull_feed_rows(rows, low_proj, w_proj, hidden, grad_hidden, sum_fc, w_fc, part_three)
+        swaps_three[c].start()
+    core_sums[0].multiply(low_two, grad_hidden, plain, flipped)
+    core_sums[1].multiply(low_proj, act, plain, flipped)
+    for rows in chunks:
+
+        def tile_out(at):
+            part_two[rows, at] = dot_last(act[rows, :], w_proj[at, :]).astype(BF16)
+
+        tiles(w_proj.shape[0], 256, tile_out)
+    for c, rows in enumerate(chunks):
+        swaps_three[c].wait()
+        pull_norm_rows(
+            c * ROWS, grad, part_three, got_three, middle, gain_two, grad_new, (sum_gain, sum_bias, sum_out), low_out
+        )
+        start_pull(c)
+    for one in core_sums:
+        one.add()
+    finish_mixed()
+    finish_pull()
+
+
+def turn_segment(mixed_all, base, grad, vectors, rest, fc_at, proj_at):
+    rows, width = base.shape
+    out_cols, units = fc_at, proj_at - fc_at
+    cols = out_cols // GROUP
+    chunks = rows // ROWS
+    copies = pltpu.SemaphoreType.DMA((2 * chunks * (GROUP - 1) + 2 * chunks + 2,))
+    high = (VMEM, shape((rows, width), F32))
+    low = (VMEM, shape((rows, width), BF16))
+    sums = (VMEM, shape((8, width), F32))
+    return run_links(
+        functools.partial(turn_body, (fc_at, proj_at)),
+        2,
+        [(VMEM, mixed_all), (ANY, base), (ANY, grad)]
+        + [(VMEM, vector) for vector in vectors]
+        + [(ANY, rest)],
+        [
+            (VMEM, shape((rows, out_cols), BF16)),
+            high,
+            low,
+            (VMEM, shape((rows, units), BF16)),
+            low,
+            low,
+            sums,
+            (VMEM, shape((rows, units), BF16)),
+            (VMEM, shape((8, units), F32)),
+            high,
+            low,
+            sums,
+            sums,
+            sums,
+            (ANY, shape((GROUP, rows, cols), BF16)),
+        ]
+        + [(VMEM, shape((width // 4, units), BF16))] * 4,
+        [
+            pltpu.VMEM((width, out_cols), BF16),
+            pltpu.VMEM((width, units), BF16),
+            pltpu.VMEM((width, units), BF16),
+            pltpu.VMEM((rows, width), F32),
+            pltpu.VMEM((rows, width), F32),
+            pltpu.VMEM((rows, units), F32),
+        ]
+        + [pltpu.VMEM((rows, width), BF16)] * 4
+        + [
+            pltpu.VMEM((GROUP, rows, cols), BF16),
+        ]
+        + [pltpu.VMEM((width, rows), BF16)] * 2
+        + [pltpu.VMEM((width // 2, units), BF16)] * 4
+        + [
+            copies,
+            copies,
+            pltpu.SemaphoreType.DMA((5,)),
+            pltpu.SemaphoreType.DMA((chunks,)),
+        ],
+        flops=2 * rows * width * (2 * out_cols + 4 * units),
+        moved=rows * width * 22 + rows * units * 4 + width * (out_cols + 2 * units) * 2,
+    )
+
+
+def pull_both_body(
+    at, grad_q, grad_kv, grad_kv_back, gain, gain_two, qkv, rest, grad_in, stream_in, hidden_in, middle_in,
+    stay0_in, met0_in, stay1_in, go1,
+    full, sum_qkv, sum_gain_one, sum_bias_one, low_proj, sum_proj, grad_hidden, sum_fc, grad_new, low_out,
+    sum_gain, sum_bias, sum_out, pieces, total0, total1,
+    w_qkv, w_out, w_fc, w_proj, grad, stream, hidden, middle, grad_mid, back_got,
+    part, got, part_two, got_two, ready,
+    stay0, met0, far0, came0, stay1, met1, far1, came1, send, recv, load, kept
+):
+    first, fc_at, proj_at = at
+    links = Links(send, recv)
+    loads = load_columns(
+        (
+            (qkv, first, w_qkv),
+            (grad_in, None, grad),
+            (stream_in, None, stream),
+            (rest, proj_at, w_proj),
+            (hidden_in, None, hidden),
+            (rest, fc_at, w_fc),
+            (middle_in, None, middle),
+            (rest, 0, w_out),
+            (stay0_in, None, stay0),
+            (met0_in, None, met0),
+            (stay1_in, None, stay1),
+        ),
+        load,
+    )
+    links.greet(
+        [links.peer(s) for s in range(1, GROUP)]
+        + [links.beyond(1, s) for s in range(GROUP)]
+        + [links.beyond(links.groups - 1, s) for s in range(GROUP)]
+        + [{"tp": links.other}]
+        + group_greets(links)
+    )
+    chunks = [pl.ds(c * ROWS, ROWS) for c in range(grad.shape[0] // ROWS)]
+    start_pulls, wait_pulls, finish_pulls = trade_pulls(
+        links, grad_q, grad_kv, grad_kv_back, full, back_got
+    )
+    swaps = [links.swap(part.at[rows], got.at[rows]) for rows in chunks]
+    swaps_two = [links.swap(part_two.at[rows], got_two.at[rows]) for rows in chunks]
+    start_pull, finish_pull = send_mixed_pull(links, low_out, w_out, ready, pieces, kept)
+    late_x = links.copy(go1, met1, links.peer(2))
+    group_sums = (
+        GroupSum(links, stay0, met0, far0, came0, total0),
+        GroupSum(links, stay1, met1, far1, came1, total1),
+    )
+    start_pulls()
+    for total in (sum_qkv, sum_gain_one, sum_bias_one, sum_proj, sum_fc, sum_gain, sum_bias, sum_out):
+        total[...] = jnp.zeros_like(total)
+    for one in loads:
+        one.wait()
+    group_sums[0].add()
+    for c, rows in enumerate(chunks):
+        wait_pulls(c)
+        if c == len(chunks) - 1:
+            late_x.start()
+            group_sums[0].start()
+        pull_qkv_rows(c * ROWS, None, links, full, back_got, w_qkv, part, sum_qkv)
+        swaps[c].start()
+    for c, rows in enumerate(chunks):
+        swaps[c].wait()
+        pull_norm_rows(
+            c * ROWS, grad, part, got, stream, gain, grad_mid, (sum_gain_one, sum_bias_one)
+        )
+        round_rows(c * ROWS, grad_mid, low_proj, sum_proj)
+        pull_feed_rows(rows, low_proj, w_proj, hidden, grad_hidden, sum_fc, w_fc, part_two)
+        swaps_two[c].start()
+    late_x.wait()
+    group_sums[1].add()
+    group_sums[1].start()
+    for c, rows in enumerate(chunks):
+        swaps_two[c].wait()
+        pull_norm_rows(
+            c * ROWS, grad_mid, part_two, got_two, middle, gain_two, grad_new, (sum_gain, sum_bias, sum_out), low_out
+        )
+        start_pull(c)
+    finish_pulls()
+    finish_pull()
+    for one in group_sums:
+        one.finish()
+
+
+def pull_both_segment(pulls, gain, gain_two, qkv, first, rest, fc_at, proj_at, grad, stream, hidden, middle, sums_in):
+    rows, width = grad.shape
+    out_cols, units = fc_at, proj_at - fc_at
+    cols = out_cols // GROUP
+    total = 3 * out_cols
+    chunks = rows // ROWS
+    groups = lax.axis_size("fsdp") // GROUP
+    stay = sums_in[0]
+    copies = pltpu.SemaphoreType.DMA((pull_copies(rows) + chunks * (GROUP - 1) + 2 * chunks + 2 * groups - 1,))
+    high = (VMEM, shape((rows, width), F32))
+    low = (VMEM, shape((rows, width), BF16))
+    sums = (VMEM, shape((8, width), F32))
+    return run_links(
+        functools.partial(pull_both_body, (first, fc_at, proj_at)),
+        3,
+        [(VMEM, pull) for pull in pulls]
+        + [(VMEM, gain), (VMEM, gain_two)]
+        + [(ANY, array) for array in (qkv, rest, grad, stream, hidden, middle)]
+        + [(ANY, array) for array in sums_in],
+        [
+            (VMEM, shape((rows, total), BF16)),
+            (VMEM, shape((8, total), F32)),
+            sums,
+            sums,
+            low,
+            sums,
+            (VMEM, shape((rows, units), BF16)),
+            (VMEM, shape((8, units), F32)),
+            high,
+            low,
+            sums,
+            sums,
+            sums,
+            (ANY, shape((GROUP, rows, cols), BF16)),
+        ]
+        + [(VMEM, shape((stay.shape[0] // groups, stay.shape[1]), F32))] * 2,
+        [
+            pltpu.VMEM((width, total), BF16),
+            pltpu.VMEM((width, out_cols), BF16),
+            pltpu.VMEM((width, units), BF16),
+            pltpu.VMEM((width, units), BF16),
+            pltpu.VMEM((rows, width), F32),
+            pltpu.VMEM((rows, width), F32),
+            pltpu.VMEM((rows, units), F32),
+            pltpu.VMEM((rows, width), F32),
+            pltpu.VMEM((rows, width), F32),
+            pltpu.VMEM((GROUP, rows, 2 * cols), BF16),
+        ]
+        + [pltpu.VMEM((rows, width), BF16)] * 4
+        + [
+            pltpu.VMEM((GROUP, rows, cols), BF16),
+        ]
+        + ([pltpu.VMEM(stay.shape, BF16)] + group_scratch(stay, groups, True)) * 2
+        + [
+            copies,
+            copies,
+            pltpu.SemaphoreType.DMA((11,)),
+            pltpu.SemaphoreType.DMA((chunks,)),
+        ],
+        flops=2 * rows * width * (total + out_cols + 2 * units),
+        moved=rows * width * 22 + rows * units * 6 + width * (total + out_cols + 2 * units) * 2,
+    )
+
+
+def pull_last_body(
+    first, grad_q, grad_kv, grad_kv_back, gain, qkv, grad_in, stream_in,
+    low_two_in, grad_hidden_in, low_proj_in, act_in, low_one_in, low_out_in, mixed_in, stay0_in, met0_in, stay1_in, met1_in,
+    full, sum_qkv, sum_gain, sum_bias, grad_new, total0, total1, total2, total3, total4, total5,
+    w_qkv, grad, stream, back_got, part, got, left, right, wide, narrow, plain, flipped,
+    stay0, met0, far0, came0, stay1, met1, far1, came1,
+    away2, gone2, stay2, go2, met2, far2, came2,
+    away3, gone3, stay3, go3, met3, far3, came3,
+    away4, gone4, stay4, go4, met4, far4, came4,
+    away5, gone5, stay5, go5, met5, far5, came5,
+    send, recv, load
+):
+    links = Links(send, recv)
+    loads = load_columns(
+        (
+            (low_two_in, None, left),
+            (grad_hidden_in, None, wide),
+            (stay0_in, None, stay0),
+            (met0_in, None, met0),
+            (stay1_in, None, stay1),
+            (met1_in, None, met1),
+            (low_proj_in, None, right),
+            (qkv, first, w_qkv),
+            (grad_in, None, grad),
+            (stream_in, None, stream),
+            (mixed_in, None, narrow),
+        ),
+        load,
+    )
+    again = [
+        pltpu.make_async_copy(source, target, load.at[len(loads) + i])
+        for i, (source, target) in enumerate(((act_in, wide), (low_one_in, left), (low_out_in, right)))
+    ]
+    links.greet(
+        [links.peer(s) for s in range(1, GROUP)]
+        + [links.beyond(1, s) for s in range(GROUP)]
+        + [links.beyond(links.groups - 1, s) for s in range(GROUP)]
+        + [{"tp": links.other}]
+        + group_greets(links)
+    )
+    chunks = [pl.ds(c * ROWS, ROWS) for c in range(grad.shape[0] // ROWS)]
+    start_pulls, wait_pulls, finish_pulls = trade_pulls(
+        links, grad_q, grad_kv, grad_kv_back, full, back_got
+    )
+    swaps = [links.swap(part.at[rows], got.at[rows]) for rows in chunks]
+    parts = (
+        (away2, gone2, stay2, go2, met2),
+        (away3, gone3, stay3, go3, met3),
+        (away4, gone4, stay4, go4, met4),
+        (away5, gone5, stay5, go5, met5),
+    )
+    core_sums = [CoreSum(links, stay, go, away, gone) for away, gone, stay, go, _ in parts]
+    over_x = [links.copy(go, met, links.peer(2)) for _, _, _, go, met in parts]
+    group_sums = [
+        GroupSum(links, *refs)
+        for refs in (
+            (stay0, met0, far0, came0, total0),
+            (stay1, met1, far1, came1, total1),
+            (stay2, met2, far2, came2, total2),
+            (stay3, met3, far3, came3, total3),
+            (stay4, met4, far4, came4, total4),
+            (stay5, met5, far5, came5, total5),
+        )
+    ]
+    start_pulls()
+    for total in (sum_qkv, sum_gain, sum_bias):
+        total[...] = jnp.zeros_like(total)
+    loads[0].wait()
+    loads[1].wait()
+    core_sums[0].multiply(left, wide, plain, flipped)
+    again[0].start()
+    again[1].start()
+    for one in loads[2:]:
+        one.wait()
+    group_sums[0].add()
+    group_sums[1].add()
+    again[0].wait()
+    core_sums[1].multiply(right, wide, plain, flipped)
+    again[2].start()
+    core_sums[0].add()
+    core_sums[1].add()
+    for c, rows in enumerate(chunks):
+        wait_pulls(c)
+        if c == len(chunks) - 1:
+            over_x[0].start()
+            group_sums[0].start()
+            group_sums[1].start()
+            over_x[1].start()
+        pull_qkv_rows(c * ROWS, None, links, full, back_got, w_qkv, part, sum_qkv)
+        swaps[c].start()
+    again[1].wait()
+    again[2].wait()
+    core_sums[2].multiply(left, full, plain, flipped)
+    core_sums[3].multiply(right, narrow, plain, flipped)
+    for c, rows in enumerate(chunks):
+        swaps[c].wait()
+        pull_norm_rows(c * ROWS, grad, part, got, stream, gain, grad_new, (sum_gain, sum_bias))
+    for at in (2, 3):
+        core_sums[at].add()
+        over_x[at].start()
+    for at in range(4):
+        over_x[at].wait()
+        group_sums[2 + at].add()
+        group_sums[2 + at].start()
+    finish_pulls()
+    for one in group_sums:
+        one.finish()
+
+
+def pull_last_segment(pulls, gain, qkv, first, grad, stream, factors, sums_in):
+    rows, width = grad.shape
+    cols = pulls[0].shape[2]
+    total = 3 * GROUP * cols
+    units = factors[1].shape[1]
+    chunks = rows // ROWS
+    groups = lax.axis_size("fsdp") // GROUP
+    copies = pltpu.SemaphoreType.DMA((pull_copies(rows) + chunks + 8 + 6 * (groups - 1),))
+    sums = (VMEM, shape((8, width), F32))
+    sizes = [sums_in[0].shape[1], sums_in[2].shape[1], units, units, total, GROUP * cols]
+    quarter = width // 4
+    scratch = []
+    for at, size in enumerate(sizes):
+        stay = shape((quarter, size), BF16)
+        if at >= 2:
+            scratch += [pltpu.VMEM((2 * quarter, size), BF16)] * 2
+            scratch += [pltpu.VMEM(stay.shape, BF16)]
+        scratch += [pltpu.VMEM(stay.shape, BF16)] + group_scratch(stay, groups, True)
+    return run_links(
+        functools.partial(pull_last_body, first),
+        4,
+        [(VMEM, pull) for pull in pulls]
+        + [(VMEM, gain)]
+        + [(ANY, array) for array in (qkv, grad, stream, *factors, *sums_in)],
+        [
+            (VMEM, shape((rows, total), BF16)),
+            (VMEM, shape((8, total), F32)),
+            sums,
+            sums,
+            (VMEM, shape((rows, width), F32)),
+        ]
+        + [(VMEM, shape((quarter // groups, size), F32)) for size in sizes],
+        [
+            pltpu.VMEM((width, total), BF16),
+            pltpu.VMEM((rows, width), F32),
+            pltpu.VMEM((rows, width), F32),
+            pltpu.VMEM((GROUP, rows, 2 * cols), BF16),
+            pltpu.VMEM((rows, width), BF16),
+            pltpu.VMEM((rows, width), BF16),
+            pltpu.VMEM((rows, width), BF16),
+            pltpu.VMEM((rows, width), BF16),
+            pltpu.VMEM((rows, units), BF16),
+            pltpu.VMEM((rows, GROUP * cols), BF16),
+            pltpu.VMEM((width, rows), BF16),
+            pltpu.VMEM((width, rows), BF16),
+        ]
+        + scratch
+        + [copies, copies, pltpu.SemaphoreType.DMA((14,))],
+        flops=2 * rows * width * total * 2 + 4 * rows * width * units,
+        moved=rows * width * 24 + rows * units * 4 + width * total * 2,
+    )
+
+
+def flip_slots(links, source, plain, flipped):
+    plain[...] = source[...].T
+    depth = plain.shape[0] // (GROUP * links.groups)
+    slot = 0
+    for s in (0, 2, 1, 3):
+        for onward in range(links.groups):
+            owner = lax.rem(links.group + onward, links.groups) * GROUP + (links.place ^ s)
+            flipped[slot * depth : (slot + 1) * depth, :] = plain[
+                pl.ds(pl.multiple_of(owner * depth, depth), depth), :
+            ]
+            slot += 1
+
+
+class CoreSum:
+    def __init__(self, links, stay, go, away, got):
+        self.links, self.stay, self.go, self.away, self.got = links, stay, go, away, got
+        self.copy = links.copy(away, got, links.peer(1))
+
+    def multiply(self, x, g, plain, flipped):
+        flip_slots(self.links, x, plain, flipped)
+        quarter = self.stay.shape[0]
+
+        def far(at):
+            self.away[:, at] = dot(flipped[2 * quarter :, :], g[:, at]).astype(BF16)
+
+        def near(at):
+            self.stay[:, at] = dot(flipped[:quarter, :], g[:, at]).astype(BF16)
+            self.go[:, at] = dot(flipped[quarter : 2 * quarter, :], g[:, at]).astype(BF16)
+
+        tiles(g.shape[1], 512, far)
+        self.copy.start()
+        tiles(g.shape[1], 512, near)
+
+    def add(self):
+        self.copy.wait()
+        quarter = self.stay.shape[0]
+        chunk = 16
+        for target, first in ((self.go, quarter), (self.stay, 0)):
+
+            def body(at):
+                from_row = pl.ds(pl.multiple_of(at.start + first, chunk), chunk)
+                total = target[at, :].astype(F32) + self.got[from_row, :].astype(F32)
+                target[at, :] = total.astype(BF16)
+
+            each_rows(quarter, chunk, body)
+
+
+def weight_pull_body(x0, g0, x1, g1, stay0, go0, stay1, go1, plain, flipped, away0, got0, away1, got1, send, recv):
+    links = Links(send, recv)
+    links.greet([links.peer(1)])
+    first = CoreSum(links, stay0, go0, away0, got0)
+    second = CoreSum(links, stay1, go1, away1, got1)
+    first.multiply(x0, g0, plain, flipped)
+    second.multiply(x1, g1, plain, flipped)
+    first.add()
+    second.add()
+
+
+def weight_pull(name, x0, g0, x1, g1):
+    rows, width = x0.shape
+    sizes = (g0.shape[1], g1.shape[1])
+    quarter = [(VMEM, shape((width // 4, size), BF16)) for size in sizes]
+    half = [pltpu.VMEM((width // 2, size), BF16) for size in sizes]
+    return run_links(
+        weight_pull_body,
+        name,
+        [(VMEM, array) for array in (x0, g0, x1, g1)],
+        [quarter[0], quarter[0], quarter[1], quarter[1]],
+        [pltpu.VMEM((width, rows), BF16), pltpu.VMEM((width, rows), BF16)]
+        + [half[0], half[0], half[1], half[1]]
+        + [pltpu.SemaphoreType.DMA((2,)), pltpu.SemaphoreType.DMA((2,))],
+        flops=2 * rows * width * sum(sizes),
+        moved=rows * width * 4 + (rows + width) * sum(sizes) * 2,
+    )
+
+
+class GroupSum:
+    def __init__(self, links, stay, met, far, came, result):
+        self.stay, self.met, self.far, self.came, self.result = stay, met, far, came, result
+        self.depth = result.shape[0]
+        self.copies = []
+        for onward in range(1, links.groups):
+            rows = pl.ds((onward - 1) * self.depth, self.depth)
+            self.copies.append(links.copy(far.at[rows], came.at[rows], links.beyond(onward, 0)))
+
+    def add(self):
+        chunk = 16
+
+        def near(at):
+            self.result[at, :] = self.stay[at, :].astype(F32) + self.met[at, :].astype(F32)
+
+        each_rows(self.depth, chunk, near)
+
+        def far(at):
+            from_row = pl.ds(pl.multiple_of(at.start + self.depth, chunk), chunk)
+            total = self.stay[from_row, :].astype(F32) + self.met[from_row, :].astype(F32)
+            self.far[at, :] = total.astype(BF16)
+
+        each_rows(self.far.shape[0], chunk, far)
+
+    def start(self):
+        for one in self.copies:
+            one.start()
+
+    def finish(self):
+        for one in self.copies:
+            one.wait()
+        chunk = 16
+
+        def body(at):
+            total = self.result[at, :]
+            for onward in range(len(self.copies)):
+                from_row = pl.ds(pl.multiple_of(at.start + onward * self.depth, chunk), chunk)
+                total = total + self.came[from_row, :].astype(F32)
+            self.result[at, :] = total
+
+        each_rows(self.depth, chunk, body)
+
+
+def group_scratch(stay, groups, met):
+    rows, size = stay.shape
+    far = pltpu.VMEM((rows - rows // groups, size), BF16)
+    return ([pltpu.VMEM((rows, size), BF16)] if met else []) + [far, far]
+
+
+def group_greets(links):
+    return [links.beyond(onward, 0) for onward in range(2, links.groups - 1)]
+
+
 def doc_start_rows(sc, docs, positions):
     start = jnp.zeros_like(positions)
     for d in range(docs):
@@ -1145,41 +1480,6 @@
 
 def tie(*values):
     return lax.optimization_barrier(values)
-
-
-class SlotSum:
-    def __init__(self, halves):
-        self.keep, self.send = halves
-        self.groups = lax.axis_size("fsdp") // GROUP
-
-    def add(self, rows):
-        total = self.keep[rows].astype(F32)
-        for part in self.parts:
-            total = total + part[rows].astype(F32)
-        return total
-
-    def to_core(self):
-        self.parts = [swap_fsdp(self.send, 1)]
-
-    def to_x(self):
-        half = self.keep.shape[0] // 2
-        self.parts.append(swap_fsdp(self.add(slice(half, None)).astype(BF16), 2))
-
-    def to_groups(self):
-        rows = self.keep.shape[0] // 2 // self.groups
-        size = lax.axis_size("fsdp")
-        self.near = self.add(slice(0, rows))
-        self.far = []
-        for onward in range(1, self.groups):
-            part = self.add(slice(onward * rows, (onward + 1) * rows)).astype(BF16)
-            pairs = [(i, (i + GROUP * onward) % size) for i in range(size)]
-            self.far.append(lax.ppermute(part, "fsdp", pairs))
-
-    def result(self):
-        total = self.near
-        for part in self.far:
-            total = total + part.astype(F32)
-        return total
 
 
 def shards(
@@ -1247,89 +1547,121 @@
     stream, low_one, pieces, kv_back = first_segment(
         tokens, row(ln1_gain[0]), row(ln1_bias[0]), full_a, bias_qkv(0)
     )
-    for l in range(LAYERS):
+    for l in range(LAYERS - 1):
         mixed, out, log_total = attend(sc, docs, pieces, kv_back)
-        if l + 1 < LAYERS:
-            vectors = (b_out[l], ln2_gain[l], ln2_bias[l], b_fc[l], b_proj[l], ln1_gain[l + 1], ln1_bias[l + 1])
-            mixed_full, middle, low_two, hidden, act, *later = between_segment(
-                mixed,
-                stream,
-                [row(vector) for vector in vectors],
-                bias_qkv(l + 1),
-                rest_of[l],
-                fc_at,
-                proj_at,
-                *qkv_of[l + 1],
-            )
-            kept = (stream, low_one, pieces, kv_back)
-            stream, low_one, pieces, kv_back = later
-        else:
-            kept = (stream, low_one, pieces, kv_back)
-            mixed = trade(mixed)
-            mixed_full, part = out_proj(sc, mixed[0], mixed[1:], rest_of[l])
-            middle, low_two, hidden, act, part_two = feed(
-                sc,
-                stream,
-                part,
-                swap_tp(part),
-                row(b_out[l]),
-                row(ln2_gain[l]),
-                row(ln2_bias[l]),
-                rest_of[l],
-                fc_at,
-                proj_at,
-                row(b_fc[l]),
-            )
-            stream, sums = middle, (part_two, swap_tp(part_two), row(b_proj[l]))
-        stored.append(kept + (out, log_total, mixed_full, middle, low_two, hidden, act))
-    own, got, badd = sums
-    outputs = (stream + (own.astype(F32) + got.astype(F32)) + badd).astype(BF16)
-
+        vectors = (b_out[l], ln2_gain[l], ln2_bias[l], b_fc[l], b_proj[l], ln1_gain[l + 1], ln1_bias[l + 1])
+        mixed_full, middle, low_two, hidden, act, *later = between_segment(
+            mixed,
+            stream,
+            [row(vector) for vector in vectors],
+            bias_qkv(l + 1),
+            rest_of[l],
+            fc_at,
+            proj_at,
+            *qkv_of[l + 1],
+        )
+        stored.append(
+            (stream, low_one, pieces, kv_back, out, log_total, mixed_full, middle, low_two, hidden, act)
+        )
+        stream, low_one, pieces, kv_back = later
+
+    l = LAYERS - 1
+    mixed, out, log_total = attend(sc, docs, pieces, kv_back)
     grad = cotangent.astype(F32) * row_weight[:, None]
-    small = [None] * LAYERS
-    large = [None] * LAYERS
-    for l in range(LAYERS - 1, -1, -1):
-        stream, low_one, pieces, kv_back, out, log_total, mixed_full, middle, low_two, hidden, act = stored[l]
-        low_proj, sum_bproj, grad_hidden, sum_bfc, part = feed_pull(
-            sc, grad, hidden, rest_of[l], fc_at, proj_at
-        )
-        got = swap_tp(part)
-        halves = weight_pull(sc, low_two, grad_hidden, low_proj, act)
-        got, *halves = tie(got, *halves)
-        feed_sum = SlotSum(halves)
-        feed_sum.to_core()
-        if l + 1 < LAYERS:
-            attn_sum.to_groups()
-        grad, low_out, grad_mixed, sum_gain_two, sum_bias_two, sum_bout = mid_pull(
-            sc, grad, part, got, middle, row(ln2_gain[l]), rest_of[l], out_cols
-        )
-        grad_mixed, feed_sum.parts[0] = tie(grad_mixed, feed_sum.parts[0])
-        feed_sum.to_x()
-        grad_mixed = jnp.stack([piece if piece.ndim == 2 else piece[0] for piece in trade(grad_mixed)])
-        grad_q, grad_kv, grad_kv_back = attend_pull(sc, docs, pieces, grad_mixed, kv_back, out, log_total)
-        grad_kv_got = shift_fsdp(grad_kv_back, -GROUP)
-        grad_q, feed_sum.parts[1] = tie(grad_q, feed_sum.parts[1])
-        feed_sum.to_groups()
-        grad_kv = (grad_kv.astype(F32) + grad_kv_got.astype(F32)).astype(BF16)
-        grad_pieces = jnp.concatenate([grad_q, grad_kv], 2)
-        grad_pieces = trade(grad_pieces)
-        weights, first = qkv_of[l]
-        grad_qkv, part, sum_bqkv = qkv_pull(
-            sc, grad_pieces[0], grad_pieces[1:], weights, first // (3 * out_cols)
-        )
-        got = swap_tp(part)
-        halves = weight_pull(sc, low_one, grad_qkv, low_out, mixed_full)
-        got, *halves = tie(got, *halves)
-        attn_sum = SlotSum(halves)
-        attn_sum.to_core()
-        grad, sum_gain_one, sum_bias_one = first_pull(sc, grad, part, got, stream, row(ln1_gain[l]))
-        grad, attn_sum.parts[0] = tie(grad, attn_sum.parts[0])
-        attn_sum.to_x()
-        sums = [sum_gain_one, sum_bias_one, sum_bqkv, sum_bout, sum_gain_two, sum_bias_two, sum_bfc, sum_bproj]
-        small[l] = butterfly(jnp.concatenate([jnp.sum(value, 0) for value in sums]))
-        large[l] = (feed_sum, attn_sum)
-    attn_sum.to_groups()
-    large = [[one.result() for one in pair] for pair in large]
+    (
+        mixed_full,
+        middle,
+        low_two,
+        act,
+        part_two,
+        low_proj,
+        sum_bproj,
+        grad_hidden,
+        sum_bfc,
+        grad,
+        low_out,
+        sum_gain_two,
+        sum_bias_two,
+        sum_bout,
+        grad_mixed,
+        *feed_parts,
+    ) = turn_segment(
+        mixed,
+        stream,
+        grad,
+        [row(vector) for vector in (b_out[l], ln2_gain[l], ln2_bias[l], b_fc[l])],
+        rest_of[l],
+        fc_at,
+        proj_at,
+    )
+    other_two = swap_tp(part_two)
+    outputs = (middle + (part_two.astype(F32) + other_two.astype(F32)) + b_proj[l][None]).astype(BF16)
+
+    stay0, go0, stay1, go1 = feed_parts
+    met0 = swap_fsdp(go0, 2)
+    grad_mixed, stay0 = tie(grad_mixed, stay0)
+    pulls = attend_pull(sc, docs, pieces, grad_mixed, kv_back, out, log_total)
+    *pulls, met0 = tie(*pulls, met0)
+    sums_one = [sum_bout, sum_gain_two, sum_bias_two, sum_bfc, sum_bproj]
+    low_one_kept, low_out_kept, mixed_kept = low_one, low_out, mixed_full
+    (stream_below, low_one, pieces, kv_back, out, log_total, mixed_full, middle, low_two, hidden, act) = stored[0]
+    weights, first = qkv_of[1]
+    (
+        grad_qkv,
+        sum_bqkv,
+        sum_gain_one,
+        sum_bias_one,
+        low_proj,
+        sum_bproj,
+        grad_hidden,
+        sum_bfc,
+        grad,
+        low_out,
+        sum_gain_two,
+        sum_bias_two,
+        sum_bout,
+        grad_mixed,
+        *feed_totals,
+    ) = pull_both_segment(
+        pulls,
+        row(ln1_gain[1]),
+        row(ln2_gain[0]),
+        weights,
+        first,
+        rest_of[0],
+        fc_at,
+        proj_at,
+        grad,
+        stream,
+        hidden,
+        middle,
+        [stay0, met0, stay1, go1],
+    )
+    stay0, go0, stay1, go1 = weight_pull(5, low_one_kept, grad_qkv, low_out_kept, mixed_kept)
+    met0, met1 = swap_fsdp(go0, 2), swap_fsdp(go1, 2)
+
+    def join_small(sums):
+        return butterfly(jnp.concatenate([jnp.sum(value, 0) for value in sums]))
+
+    small_one = join_small([sum_gain_one, sum_bias_one, sum_bqkv] + sums_one)
+    grad_mixed, stay0 = tie(grad_mixed, stay0)
+    pulls = attend_pull(sc, docs, pieces, grad_mixed, kv_back, out, log_total)
+    *pulls, met0, met1 = tie(*pulls, met0, met1)
+    sums_zero = [sum_bout, sum_gain_two, sum_bias_two, sum_bfc, sum_bproj]
+    weights, first = qkv_of[0]
+    grad_qkv, sum_bqkv, sum_gain_one, sum_bias_one, grad, *totals = pull_last_segment(
+        pulls,
+        row(ln1_gain[0]),
+        weights,
+        first,
+        grad,
+        stream_below,
+        [low_two, grad_hidden, low_proj, act, low_one, low_out, mixed_full],
+        [stay0, met0, stay1, met1],
+    )
+    small_zero = join_small([sum_gain_one, sum_bias_one, sum_bqkv] + sums_zero)
+    small = [small_zero, small_one]
+    large = [totals[2:], feed_totals + totals[:2]]
 
     def small_parts(vector):
         ends, at = [], 0
@@ -1347,16 +1679,16 @@
 
     grad_wqkv = jnp.stack(
         [
-            large[l][1][:, : 3 * out_cols]
+            large[l][2]
             .reshape(depth, GROUP, 3, cols)
             .transpose(0, 2, 1, 3)
             .reshape(depth, 3, out_cols)
             for l in range(LAYERS)
         ]
-    ).astype(F32)
-    grad_wout = jnp.stack([large[l][1][:, 3 * out_cols :].T for l in range(LAYERS)]).astype(F32)
-    grad_wfc = jnp.stack([large[l][0][:, :units] for l in range(LAYERS)]).astype(F32)
-    grad_wproj = jnp.stack([large[l][0][:, units:].T for l in range(LAYERS)]).astype(F32)
+    )
+    grad_wout = jnp.stack([large[l][3].T for l in range(LAYERS)])
+    grad_wfc = jnp.stack([large[l][0] for l in range(LAYERS)])
+    grad_wproj = jnp.stack([large[l][1].T for l in range(LAYERS)])
 
     return (
         outputs,

time: 922 us -> 703 us (0.76); the launches traced: 904 us -> 701 us
  waiting for transfers between devices: 378 us -> 92.5 us
  Pallas kernels: 366 us -> 515 us
  starting transfers between devices: 76.2 us -> 38.8 us
  other arithmetic: 50.9 us -> 27.6 us
    pallas_call x2 -> x6, Pallas kernels: 140 us -> 450 us  [run_links(): pl.pallas_call(body, in_specs=[spec for spec, _ in ins], out_specs=[spec...]
    pallas_call x18 -> x4, Pallas kernels: 226 us -> 66 us  [run_kernel(): pl.pallas_call(body, grid_spec=pltpu.PrefetchScalarGridSpec(num_scalar_pr...]
    ppermute x35 -> x15, waiting for transfers between devices: 141 us -> 8.98 us  [swap_fsdp(): lax.ppermute(value, 'fsdp', [(i, i ^ s) for i in range(lax.axis_size('fsd...]
    ppermute x6 -> x1, waiting for transfers between devices: 88.4 us -> 0.01 us  [swap_tp(): return lax.ppermute(value, 'tp', [(0, 1), (1, 0)])]
    ppermute x14 -> x0, waiting for transfers between devices: 71.3 us -> none  [the longest x12 44.9 us: to_groups(): self.far.append(lax.ppermute(part, 'fsdp', pairs))]
    convert_element_type x11 -> x1, other arithmetic: 23.8 us -> 3.41 us  [shards(): (middle + (part_two.astype(F32) + other_two.astype(F32)) + b_proj[l][None...]
    ppermute x14 -> x0, starting transfers between devices: 18.9 us -> none  [the longest x12 16 us: to_groups(): self.far.append(lax.ppermute(part, 'fsdp', pairs))]
    ppermute x35 -> x15, starting transfers between devices: 53.1 us -> 38.2 us  [swap_fsdp(): lax.ppermute(value, 'fsdp', [(i, i ^ s) for i in range(lax.axis_size('fsd...]
  transfers between devices with their start and end apart: 58 -> 19, of which waited for: 31 -> 11; matrix products, arithmetic and copies ran while one was open for 6% -> 4% of each run, Pallas kernels for 34% -> 46%
where the time goes in v3:
time: 703 us; the launch traced here: 701 us
  Pallas kernels  515 us (73%)
  waiting for transfers between devices  92.5 us (13%)
  starting transfers between devices  38.8 us (6%)
  other arithmetic  27.6 us (4%)
  between operations  14.7 us (2%)
  local copies, waits for them, and re-layouts  11.6 us (2%)
    pallas_call x6, Pallas kernels, run_links(): pl.pallas_call(body, in_specs=[spec for spec, _ in ins], out_specs=[spec...  450 us
    all_gather x3, waiting for transfers between devices, gather(): return lax.all_gather(shard, 'fsdp', axis=0, tiled=True)  83.4 us
    pallas_call x4, Pallas kernels, run_kernel(): pl.pallas_call(body, grid_spec=pltpu.PrefetchScalarGridSpec(num_scalar_pr...  66 us
    ppermute x15, starting transfers between devices, swap_fsdp(): lax.ppermute(value, 'fsdp', [(i, i ^ s) for i in range(lax.axis_size('fsd...  38.2 us
  transfers between devices with their start and end apart: 19, of which 11 were waited for; matrix products, arithmetic and copies ran while one was open for 4% of the time, Pallas kernels for 46%

profile of v3, /device:TPU:0, one launch (start us, length us, event | category | flops | bytes accessed | tf_op | source)
XLA Modules:
  0.0 700.7 jit_solution(5118966738958751410)
XLA Ops:
  17.2 2.6 collective-permute-start.1
  21.3 2.1 collective-permute-start.2
  24.9 3.0 collective-permute-start.3
  32.2 26.6 %all-gather.4.cloned.1.call-done.w_all.qkv = bf16[1024,1536]{1,0:T(8,128)(2,1)} async-done(((bf16[64,1536]{1,0:T(8,128)(2,1)}), bf16[1024,1536]{1,0:T(8,128)(2,1)}) %all-gather.4.cloned.1.call-update) | async-done | bytes 3145744 | tf_op jit(solution)/shard_map/all_gather | solution.py:1478
  58.8 46.8 %shard_map.263 = (f32[512,1024]{1,0:T(8,128)}, bf16[512,1024]{1,0:T(8,128)(2,1)}, bf16[4,512,384]{2,1,0:T(8,128)(2,1)}, bf16[4,512,256]{2,1,0:T(8,128)(2,1)}) custom-call(bf16[512,1024]{1,0:T(8,128)(2,1)} %base.1, f32[1,1024]{1,0:T(1,128)} %get-tuple-element.217.gain, f32[1,1024]{1,0:T(1,128)} %get-tuple-element.220.bias, ...), custom_call_target="tpu_custom_call" | custom-call | flops 1610612736 | bytes 7340032 | tf_op jit(solution)/shard_map/pallas_call | solution.py:291
  105.6 15.1 %shard_map.264 = (bf16[4,512,128]{2,1,0:T(8,128)(2,1)}, f32[2048,128]{1,0:T(8,128)}, f32[8,2048]{1,0:T(8,128)}) custom-call(s32[10]{0:T(128)} %pad_add_fusion.sc, bf16[4,512,384]{2,1,0:T(8,128)(2,1)} %get-tuple-element.97.p0, bf16[4,512,256]{2,1,0:T(8,128)(2,1)} %get-tuple-element.98.kv), custom_call_target="tpu_custom_call" | custom-call | flops 2147483648 | bytes 5242880 | tf_op jit(solution)/shard_map/pallas_call | solution.py:46
  120.7 55.7 %all-gather.6.cloned.1.call-done.rest.qkv = bf16[1024,6144]{1,0:T(8,128)(2,1)} async-done(((bf16[64,6144]{1,0:T(8,128)(2,1)}), bf16[1024,6144]{1,0:T(8,128)(2,1)}) %all-gather.6.cloned.1.call-update) | async-done | bytes 12582928 | tf_op jit(solution)/shard_map/all_gather | solution.py:1478
  176.4 93.8 %shard_map.265 = (bf16[512,512]{1,0:T(8,128)(2,1)}, f32[512,1024]{1,0:T(8,128)}, bf16[512,1024]{1,0:T(8,128)(2,1)}, f32[512,2048]{1,0:T(8,128)}, bf16[512,2048]{...) custom-call(bf16[4,512,128]{2,1,0:T(8,128)(2,1)} %get-tuple-element., ...), custom_call_target="tpu_custom_call" | custom-call | flops 6442450944 | bytes 29360128 | tf_op jit(solution)/shard_map/pallas_call | solution.py:291
  270.2 15.6 %shard_map.266 = (bf16[4,512,128]{2,1,0:T(8,128)(2,1)}, f32[2048,128]{1,0:T(8,128)}, f32[8,2048]{1,0:T(8,128)}) custom-call(s32[10]{0:T(128)} %pad_add_fusion.sc, bf16[4,512,384]{2,1,0:T(8,128)(2,1)} %get-tuple-element.101.p0, bf16[4,512,256]{2,1,0:T(8,128)(2,1)} %get-tuple-element.102.kv), custom_call_target="tpu_custom_call" | custom-call | flops 2147483648 | bytes 5242880 | tf_op jit(solution)/shard_map/pallas_call | solution.py:46
  287.0 68.0 %shard_map.267 = (bf16[512,512]{1,0:T(8,128)(2,1)}, f32[512,1024]{1,0:T(8,128)}, bf16[512,1024]{1,0:T(8,128)(2,1)}, bf16[512,2048]{1,0:T(8,128)(2,1)}, bf16[512,...) custom-call(bf16[4,512,128]{2,1,0:T(8,128)(2,1)} %get-tuple-element., ...), custom_call_target="tpu_custom_call" | custom-call | flops 9663676416 | bytes 25165824 | tf_op jit(solution)/shard_map/pallas_call | solution.py:291
  355.0 2.1 collective-permute-start.5
  361.5 17.6 %shard_map.268 = (bf16[4,512,128]{2,1,0:T(8,128)(2,1)}, bf16[4,512,256]{2,1,0:T(8,128)(2,1)}, bf16[4,512,256]{2,1,0:T(8,128)(2,1)}) custom-call(s32[10]{0:T(128)} %pad_add_fusion.sc, bf16[4,512,384]{2,1,0:T(8,128)(2,1)} %get-tuple-element.101.p0, bf16[4,512,128]{2,1,0:T(8,128)(2,1)} %get-tuple-element.109.g0, bf16[4,512,256]{2,1,0:T(8,128)(2,1)} %get-tuple-element.102.kv, ...), custom_call_target="tpu_custom_call" | custom-call | flops 4831838208 | bytes 7864320 | tf_op jit(solution)/shard_map/pallas_call | solution.py:46
  379.1 1.6 collective-permute-done.5.met0_in
  381.6 106.0 %shard_map.269 = (bf16[512,1536]{1,0:T(8,128)(2,1)}, f32[8,1536]{1,0:T(8,128)}, f32[8,1024]{1,0:T(8,128)}, f32[8,1024]{1,0:T(8,128)}, bf16[512,1024]{1,0:T(8,128...) custom-call(bf16[4,512,128]{2,1,0:T(8,128)(2,1)} %get-tuple-element., ...), custom_call_target="tpu_custom_call" | custom-call | flops 6442450944 | bytes 30408704 | tf_op jit(solution)/shard_map/pallas_call | solution.py:291
  492.5 9.7 %shard_map.270 = (bf16[256,1536]{1,0:T(8,128)(2,1)}, bf16[256,1536]{1,0:T(8,128)(2,1)}, bf16[256,512]{1,0:T(8,128)(2,1)}, bf16[256,512]{1,0:T(8,128)(2,1)}) custom-call(bf16[512,1024]{1,0:T(8,128)(2,1)} %get-tuple-element.127.x0, bf16[512,1536]{1,0:T(8,128)(2,1)} %get-tuple-element.128.g0, bf16[512,1024]{1,0:T(8,128)(2,1)} %get-tuple-element.129.x1, ...), custom_call_target="tpu_custom_call" | custom-call | flops 2147483648 | bytes 8388608 | tf_op jit(solution)/shard_map/pallas_call | solution.py:291
  504.3 2.1 collective-permute-start.14
  506.4 17.7 %shard_map.271 = (bf16[4,512,128]{2,1,0:T(8,128)(2,1)}, bf16[4,512,256]{2,1,0:T(8,128)(2,1)}, bf16[4,512,256]{2,1,0:T(8,128)(2,1)}) custom-call(s32[10]{0:T(128)} %pad_add_fusion.sc, bf16[4,512,384]{2,1,0:T(8,128)(2,1)} %get-tuple-element.97.p0, bf16[4,512,128]{2,1,0:T(8,128)(2,1)} %get-tuple-element.132.g0, bf16[4,512,256]{2,1,0:T(8,128)(2,1)} %get-tuple-element.98.kv, ...), custom_call_target="tpu_custom_call" | custom-call | flops 4831838208 | bytes 7864320 | tf_op jit(solution)/shard_map/pallas_call | solution.py:46
  524.1 9.7 %collective-permute-start.15 = (f32[9728]{0:T(1024)S(1)}, f32[9728]{0:T(1024)S(1)}, u32[]{:S(2)}, u32[]{:S(2)}) collective-permute-start(f32[9728]{0:T(1024)S(1)} %add.73), channel_id=1, source_target_pairs={{0,16},{2,18},{4,20},{6,22},{8,24},{10,26},{12,28},{14,30},{16,0},... | collective-permute-start | bytes 116744 | tf_op jit(solution)/shard_map/ppermute | solution.py:1457
  533.8 3.4 add_convert_fusion
  538.4 125.2 %shard_map.272 = (bf16[512,1536]{1,0:T(8,128)(2,1)}, f32[8,1536]{1,0:T(8,128)}, f32[8,1024]{1,0:T(8,128)}, f32[8,1024]{1,0:T(8,128)}, f32[512,1024]{1,0:T(8,128)...) custom-call(bf16[4,512,128]{2,1,0:T(8,128)(2,1)} %get-tuple-element., ...), custom_call_target="tpu_custom_call" | custom-call | flops 7516192768 | bytes 19922944 | tf_op jit(solution)/shard_map/pallas_call | solution.py:291
  666.3 2.2 pad_maximum_fusion
  672.5 7.8 %collective-permute-start.10 = (f32[9728]{0:T(1024)S(1)}, f32[9728]{0:T(1024)S(1)}, u32[]{:S(2)}, u32[]{:S(2)}) collective-permute-start(f32[9728]{0:T(1024)S(1)} %add.68), channel_id=1, source_target_pairs={{0,8},{2,10},{4,12},{6,14},{8,0},{10,2},{12,4},{14,6},{16,24},{18,... | collective-permute-start | bytes 116744 | tf_op jit(solution)/shard_map/ppermute | solution.py:1457
  682.3 3.4 collective-permute-start.11
  685.7 1.7 pad_maximum_fusion.5
  (188 shorter events, 46.6 us)
Async XLA Ops:
  7.2 51.6 %all-gather.4.cloned.1.call-start = ((), (), s32[]{:S(2)}) async-start(), calls=%async_computation | async-start | bytes 3342336 | tf_op jit(solution)/shard_map/all_gather | solution.py:1478
  9.5 166.9 %all-gather.6.cloned.1.call-start = ((), (), s32[]{:S(2)}) async-start(), calls=%async_computation.1 | async-start | bytes 13369344 | tf_op jit(solution)/shard_map/all_gather | solution.py:1478
  10.2 20.2 %copy-start.27 = (s32[8]{0:T(128)S(1)}, s32[8]{0:T(128)}, u32[]{:S(2)}) copy-start(s32[8]{0:T(128)} %param.19) | copy-start | bytes 100
  10.2 20.5 %copy-start.2 = (bf16[512,1024]{1,0:T(8,128)(2,1)S(1)}, bf16[512,1024]{1,0:T(8,128)(2,1)}, u32[]{:S(2)}) copy-start(bf16[512,1024]{1,0:T(8,128)(2,1)} %param.17) | copy-start | bytes 3145732
  11.2 275.8 %all-gather.8.cloned.1.call-start = ((), (), s32[]{:S(2)}) async-start(), calls=%async_computation.2 | async-start | bytes 10027008 | tf_op jit(solution)/shard_map/all_gather | solution.py:1478
  12.2 5.0 collective-permute-start
  17.2 4.1 collective-permute-start.1
  21.3 3.6 collective-permute-start.2
  24.9 4.6 collective-permute-start.3
  355.0 25.7 %collective-permute-start.5 = (bf16[256,2048]{1,0:T(8,128)(2,1)}, bf16[256,2048]{1,0:T(8,128)(2,1)S(1)}, u32[]{:S(2)}, u32[]{:S(2)}) collective-permute-start(bf16[256,2048]{1,0:T(8,128)(2,1)} %get-tuple-element.115), channel_id=1, source_target_pairs={{0,4},{2,6},{4,0},{6,2},{8,12},{10,14},{12,8},{14,10},{16,20},{18,... | collective-permute-start | bytes 3145736 | tf_op jit(solution)/shard_map/ppermute | solution.py:1457
  361.1 172.7 %collective-permute-start.4 = (bf16[512,1024]{1,0:T(8,128)(2,1)}, bf16[512,1024]{1,0:T(8,128)(2,1)}, u32[]{:S(2)}, u32[]{:S(2)}) collective-permute-start(bf16[512,1024]{1,0:T(8,128)(2,1)} %get-tuple-element.106), channel_id=1, source_target_pairs={{0,1},{1,0},{2,3},{3,2},{4,5},{5,4},{6,7},{7,6},{8,9},{9,8},{10,11... | collective-permute-start | bytes 3145736 | tf_op jit(solution)/shard_map/ppermute | solution.py:1453
  490.1 1.5 collective-permute-start.12
  491.6 12.7 %collective-permute-start.13 = (f32[9728]{0:T(1024)S(1)}, f32[9728]{0:T(1024)S(1)}, u32[]{:S(2)}, u32[]{:S(2)}) collective-permute-start(f32[9728]{0:T(1024)S(1)} %add.71), channel_id=1, source_target_pairs={{0,4},{2,6},{4,0},{6,2},{8,12},{10,14},{12,8},{14,10},{16,20},{18,... | collective-permute-start | bytes 116744 | tf_op jit(solution)/shard_map/ppermute | solution.py:1457
  502.2 35.3 %collective-permute-start.7 = (bf16[256,512]{1,0:T(8,128)(2,1)}, bf16[256,512]{1,0:T(8,128)(2,1)}, u32[]{:S(2)}, u32[]{:S(2)}) collective-permute-start(bf16[256,512]{1,0:T(8,128)(2,1)} %get-tuple-element.139), channel_id=1, source_target_pairs={{0,4},{2,6},{4,0},{6,2},{8,12},{10,14},{12,8},{14,10},{16,20},{18,... | collective-permute-start | bytes 786440 | tf_op jit(solution)/shard_map/ppermute | solution.py:1457
  503.4 34.1 %collective-permute-start.6 = (bf16[256,1536]{1,0:T(8,128)(2,1)}, bf16[256,1536]{1,0:T(8,128)(2,1)S(1)}, u32[]{:S(2)}, u32[]{:S(2)}) collective-permute-start(bf16[256,1536]{1,0:T(8,128)(2,1)} %get-tuple-element.138), channel_id=1, source_target_pairs={{0,4},{2,6},{4,0},{6,2},{8,12},{10,14},{12,8},{14,10},{16,20},{18,... | collective-permute-start | bytes 2359304 | tf_op jit(solution)/shard_map/ppermute | solution.py:1457
  504.3 19.9 %collective-permute-start.14 = (f32[9728]{0:T(1024)S(1)}, f32[9728]{0:T(1024)S(1)}, u32[]{:S(2)}, u32[]{:S(2)}) collective-permute-start(f32[9728]{0:T(1024)S(1)} %add.72), channel_id=1, source_target_pairs={{0,8},{2,10},{4,12},{6,14},{8,0},{10,2},{12,4},{14,6},{16,24},{18,... | collective-permute-start | bytes 116744 | tf_op jit(solution)/shard_map/ppermute | solution.py:1457
  506.4 27.4 %copy-start.3 = (bf16[512,1024]{1,0:T(8,128)(2,1)S(1)}, bf16[512,1024]{1,0:T(8,128)(2,1)}, u32[]{:S(2)}) copy-start(bf16[512,1024]{1,0:T(8,128)(2,1)} %get-tuple-element.106) | copy-start | bytes 3145732
  524.1 13.3 %collective-permute-start.15 = (f32[9728]{0:T(1024)S(1)}, f32[9728]{0:T(1024)S(1)}, u32[]{:S(2)}, u32[]{:S(2)}) collective-permute-start(f32[9728]{0:T(1024)S(1)} %add.73), channel_id=1, source_target_pairs={{0,16},{2,18},{4,20},{6,22},{8,24},{10,26},{12,28},{14,30},{16,0},... | collective-permute-start | bytes 116744 | tf_op jit(solution)/shard_map/ppermute | solution.py:1457
  538.4 127.9 %copy-start.7 = (f32[64,2048]{1,0:T(8,128)S(1)}, f32[64,2048]{1,0:T(8,128)}, u32[]{:S(2)}) copy-start(f32[64,2048]{1,0:T(8,128)} %get-tuple-element.177) | copy-start | bytes 1572868
  666.1 2.3 collective-permute-start.8
  668.5 4.1 collective-permute-start.9
  671.7 20.9 %copy-start = (f32[512,1024]{1,0:T(8,128)S(1)}, f32[512,1024]{1,0:T(8,128)}, u32[]{:S(2)}) copy-start(f32[512,1024]{1,0:T(8,128)} %get-tuple-element.239) | copy-start | bytes 6291460
  672.5 9.8 %collective-permute-start.10 = (f32[9728]{0:T(1024)S(1)}, f32[9728]{0:T(1024)S(1)}, u32[]{:S(2)}, u32[]{:S(2)}) collective-permute-start(f32[9728]{0:T(1024)S(1)} %add.68), channel_id=1, source_target_pairs={{0,8},{2,10},{4,12},{6,14},{8,0},{10,2},{12,4},{14,6},{16,24},{18,... | collective-permute-start | bytes 116744 | tf_op jit(solution)/shard_map/ppermute | solution.py:1457
  682.3 5.4 collective-permute-start.11
  (23 other events, 86.9 us)
Sparse Core Ops, SparseCore 0:
  10.9 47.8 all-gather.3
  61.7 114.6 all-gather.5
  179.2 107.6 all-gather.7

commit v4 on v3

--- a/solution.py
+++ b/solution.py
@@ -14,10 +14,12 @@
 
 EPS = 1e-05
 GROUP = REACH
-QB = 256
+QB = 512
+PULL_QB = 256
 LN_ROWS = 128
 ACT_ROWS = 128
-KB = 256
+KB = 512
+PULL_KB = 256
 NEG = -1e30
 F32 = jnp.float32
 BF16 = jnp.bfloat16
@@ -211,17 +213,17 @@
     for c in range(chunks):
         rows = pl.ds(c * ROWS, ROWS)
         across = {
-            s: links.copy(ready.at[s, rows], pieces.at[s, rows], links.peer(s)) for s in order if s
+            s: links.copy(ready.at[s, rows], pieces.at[links.place, rows], links.peer(s)) for s in order if s
         }
         onward = {
             s: links.copy(
                 ready.at[s, rows, pl.ds(cols // 3, 2 * cols // 3)],
-                kv_back.at[s, rows],
+                kv_back.at[links.place, rows],
                 links.beyond(1, s),
             )
             for s in order
         }
-        own = pltpu.make_async_copy(ready.at[0, rows], pieces.at[0, rows], kept.at[c])
+        own = pltpu.make_async_copy(ready.at[0, rows], pieces.at[links.place, rows], kept.at[c])
         copies.append((across, onward, own))
     last = links.group == links.groups - 1
 
@@ -262,24 +264,127 @@
     return rows // ROWS * (2 * GROUP - 1)
 
 
+class ShardGather:
+    def __init__(self, links, shard, full):
+        self.depth = shard.shape[0]
+        self.links, self.shard, self.full = links, shard, full
+        groups = range(links.groups)
+        self.along = [
+            links.copy(shard, full.at[self.rows(0, 0)], links.beyond(onward, 0)) for onward in groups[1:]
+        ]
+        self.over_x = [self.relay(onward, 0, links.peer(2)) for onward in groups]
+        self.over_core = [
+            [self.relay(onward, s, links.peer(1)) for onward in groups] for s in (0, 2)
+        ]
+
+    def rows(self, back, s):
+        links = self.links
+        group = lax.rem(links.group + links.groups - back, links.groups)
+        owner = group * GROUP + (links.place ^ s)
+        return pl.ds(pl.multiple_of(owner * self.depth, self.depth), self.depth)
+
+    def relay(self, back, s, device):
+        rows = self.rows(back, s)
+        own = back == 0 and s == 0
+        return self.links.copy(self.shard if own else self.full.at[rows], self.full.at[rows], device)
+
+    def start(self):
+        for one in self.along:
+            one.start()
+        self.over_x[0].start()
+        self.over_core[0][0].start()
+        self.full[self.rows(0, 0), :] = self.shard[...]
+
+    def pass_x(self):
+        for onward, one in enumerate(self.along, 1):
+            one.wait_recv()
+            self.over_x[onward].start()
+            self.over_core[0][onward].start()
+
+    def pass_core(self):
+        for one, last in zip(self.over_x, self.over_core[1]):
+            one.wait_recv()
+            last.start()
+
+    def arrive(self):
+        for one in self.over_core[0] + self.over_core[1]:
+            one.wait_recv()
+
+    def finish(self):
+        for one in self.along + self.over_x + self.over_core[0] + self.over_core[1]:
+            one.wait_send()
+
+
+def gather_copies():
+    groups = lax.axis_size("fsdp") // GROUP
+    return 4 * groups - 1
+
+
+class RowSum:
+    def __init__(self, links, held, came, far):
+        self.held, self.came, self.far = held, came, far
+        self.near = [links.copy(held.at[i], came.at[i], links.peer(i + 1)) for i in range(2)]
+        self.along = [
+            links.copy(held.at[2], far.at[onward - 1], links.beyond(onward, 0))
+            for onward in range(1, links.groups)
+        ]
+
+    def step(self, i):
+        self.near[i].wait()
+        self.held[i + 1] = self.held[i] + self.came[i]
+
+    def finish(self):
+        total = self.held[2]
+        for at, one in enumerate(self.along):
+            one.wait()
+            total = total + self.far[at]
+        return total
+
+
+def count_docs(segments, counts):
+    for d in range(counts.shape[0]):
+        found = jnp.where(segments[...] == d, 1.0, 0.0).astype(F32)
+        total = jnp.sum(jnp.sum(found, 0, keepdims=True), 1, keepdims=True)
+        counts[d : d + 1, :] = jnp.broadcast_to(total, (1, counts.shape[1]))
+
+
 def first_body(
-    base, gain, bias, w_all, bq, stream, low, pieces, kv_back, w, ready, send, recv, load, kept
+    base, gain, bias, shard, bq, segments, stream, low, w, tokens, first, pieces, kv_back,
+    ready, held, came, far, send, recv, kept
 ):
     links = Links(send, recv)
-    loaded = pltpu.make_async_copy(w_all, w, load.at[0])
-    loaded.start()
+    gathered = ShardGather(links, shard, w)
+    counted = RowSum(links, held, came, far)
+    start, finish = send_qkv(links, low, w, bq, ready, pieces, kv_back, kept)
+    count_docs(segments, held.at[0])
     links.greet(
         [links.peer(s) for s in range(1, GROUP)]
         + [links.beyond(1, s) for s in range(GROUP)]
         + [links.beyond(links.groups - 1, s) for s in range(GROUP)]
-    )
-    start, finish = send_qkv(links, low, w, bq, ready, pieces, kv_back, kept)
+        + group_greets(links)
+    )
+    gathered.start()
+    counted.near[0].start()
     chunks = base.shape[0] // ROWS
     for c in range(chunks):
         norm_rows(c * ROWS, base, None, gain, bias, stream, low)
-        if c == 0:
-            loaded.wait()
+    counted.step(0)
+    counted.near[1].start()
+    gathered.pass_x()
+    counted.step(1)
+    for one in counted.along:
+        one.start()
+    gathered.pass_core()
+    gathered.arrive()
+    for c in range(chunks):
         start(c)
+    total = counted.finish()
+    tokens[...] = total
+    begin = jnp.zeros((1, total.shape[1]), F32)
+    for d in range(total.shape[0]):
+        first[d : d + 1, :] = begin
+        begin = begin + total[d : d + 1, :]
+    gathered.finish()
     finish()
 
 
@@ -301,27 +406,33 @@
     )(*[array for _, array in ins])
 
 
-def first_segment(base, gain, bias, weights, bq):
+def first_segment(base, gain, bias, shard, bq, segments, docs):
     rows, width = base.shape
     total = bq.shape[1]
     cols = total // GROUP
-    copies = pltpu.SemaphoreType.DMA((qkv_copies(rows),))
+    groups = lax.axis_size("fsdp") // GROUP
+    copies = pltpu.SemaphoreType.DMA((qkv_copies(rows) + gather_copies() + groups + 1,))
+    counts = (VMEM, shape((docs, 128), F32))
     return run_links(
         first_body,
         0,
-        [(VMEM, base), (VMEM, gain), (VMEM, bias), (ANY, weights), (VMEM, bq)],
+        [(VMEM, array) for array in (base, gain, bias, shard, bq, segments)],
         [
             (VMEM, shape((rows, width), F32)),
             (VMEM, shape((rows, width), BF16)),
+            (VMEM, shape((width, total), BF16)),
+            counts,
+            counts,
             (ANY, shape((GROUP, rows, cols), BF16)),
             (ANY, shape((GROUP, rows, 2 * cols // 3), BF16)),
         ],
         [
-            pltpu.VMEM((width, total), BF16),
             pltpu.VMEM((GROUP, rows, cols), BF16),
+            pltpu.VMEM((3, docs, 128), F32),
+            pltpu.VMEM((2, docs, 128), F32),
+            pltpu.VMEM((groups - 1, docs, 128), F32),
             copies,
             copies,
-            pltpu.SemaphoreType.DMA((1,)),
             pltpu.SemaphoreType.DMA((rows // ROWS,)),
         ],
         flops=2 * rows * width * total,
@@ -337,7 +448,7 @@
         copies.append(
             [
                 links.copy(
-                    mixed_all.at[s, rows],
+                    mixed_all.at[links.place ^ s, rows],
                     mixed.at[rows, columns(links.place, cols)],
                     links.peer(s),
                 )
@@ -349,7 +460,7 @@
         for chunk in copies:
             for one in chunk:
                 one.start()
-        mixed[:, columns(links.place, cols)] = mixed_all[0]
+        mixed[:, columns(links.place, cols)] = mixed_all[links.place]
 
     def wait(c):
         for one in copies[c]:
@@ -364,16 +475,16 @@
 
 
 def between_body(
-    at, mixed_all, base, bout, gain_two, bias_two, bfc, bproj, gain, bias, bq, rest, qkv,
-    mixed, middle, low_two, hidden, act, stream, low, pieces, kv_back,
-    w_out, w_fc, w_proj, w_qkv, part, got, part_two, got_two, ready, send, recv, load, kept
+    at, mixed_all, base, bout, gain_two, bias_two, bfc, bproj, gain, bias, bq, rest, shard,
+    mixed, middle, low_two, hidden, act, stream, low, w_qkv, pieces, kv_back,
+    w_out, w_fc, w_proj, part, got, part_two, got_two, ready, send, recv, load, kept
 ):
-    fc_at, proj_at, first = at
+    out_at, fc_at, proj_at = at
     links = Links(send, recv)
     loads = [
         pltpu.make_async_copy(source.at[:, pl.ds(start, target.shape[1])], target, load.at[i])
         for i, (source, start, target) in enumerate(
-            ((rest, 0, w_out), (rest, fc_at, w_fc), (rest, proj_at, w_proj), (qkv, first, w_qkv))
+            ((rest, out_at, w_out), (rest, fc_at, w_fc), (rest, proj_at, w_proj))
         )
     ]
     for one in loads:
@@ -383,13 +494,16 @@
         + [links.beyond(1, s) for s in range(GROUP)]
         + [links.beyond(links.groups - 1, s) for s in range(GROUP)]
         + [{"tp": links.other}]
-    )
+        + group_greets(links)
+    )
+    gathered = ShardGather(links, shard, w_qkv)
     chunks = [pl.ds(c * ROWS, ROWS) for c in range(base.shape[0] // ROWS)]
     start_mixed, wait_mixed, finish_mixed = trade_mixed(links, mixed_all, mixed)
     swaps = [links.swap(part.at[rows], got.at[rows]) for rows in chunks]
     swaps_two = [links.swap(part_two.at[rows], got_two.at[rows]) for rows in chunks]
     start_qkv, finish_qkv = send_qkv(links, low, w_qkv, bq, ready, pieces, kv_back, kept)
     start_mixed()
+    gathered.start()
     loads[0].wait()
     for c, rows in enumerate(chunks):
         wait_mixed(c)
@@ -402,31 +516,32 @@
         norm_rows(c * ROWS, base, (part, got, bout), gain_two, bias_two, middle, low_two)
         feed_rows(rows, low_two, w_fc, bfc, hidden, act, w_proj, part_two)
         swaps_two[c].start()
-    loads[3].wait()
+        (gathered.pass_core if c else gathered.pass_x)()
+    gathered.arrive()
     for c, rows in enumerate(chunks):
         swaps_two[c].wait()
         norm_rows(c * ROWS, middle, (part_two, got_two, bproj), gain, bias, stream, low)
         start_qkv(c)
     finish_mixed()
+    gathered.finish()
     finish_qkv()
 
 
-def between_segment(mixed_all, base, vectors, bq, rest, fc_at, proj_at, qkv, first):
+def between_segment(mixed_all, base, vectors, bq, rest, at, units, shard):
     rows, width = base.shape
     total = bq.shape[1]
     cols = total // GROUP
-    out_cols = fc_at
-    units = proj_at - fc_at
+    out_cols = at[1] - at[0]
     chunks = rows // ROWS
-    copies = pltpu.SemaphoreType.DMA((qkv_copies(rows) + chunks * (GROUP - 1) + 2 * chunks,))
+    copies = pltpu.SemaphoreType.DMA((qkv_copies(rows) + chunks * (GROUP - 1) + 2 * chunks + gather_copies(),))
     whole_f32 = (VMEM, shape((rows, width), F32))
     whole_low = (VMEM, shape((rows, width), BF16))
     return run_links(
-        functools.partial(between_body, (fc_at, proj_at, first)),
+        functools.partial(between_body, at),
         1,
         [(VMEM, mixed_all), (VMEM, base)]
         + [(VMEM, vector) for vector in vectors]
-        + [(VMEM, bq), (ANY, rest), (ANY, qkv)],
+        + [(VMEM, bq), (ANY, rest), (VMEM, shard)],
         [
             (VMEM, shape((rows, out_cols), BF16)),
             whole_f32,
@@ -435,6 +550,7 @@
             (VMEM, shape((rows, units), BF16)),
             whole_f32,
             whole_low,
+            (VMEM, shape((width, total), BF16)),
             (ANY, shape((GROUP, rows, cols), BF16)),
             (ANY, shape((GROUP, rows, 2 * cols // 3), BF16)),
         ],
@@ -442,14 +558,13 @@
             pltpu.VMEM((width, out_cols), BF16),
             pltpu.VMEM((width, units), BF16),
             pltpu.VMEM((width, units), BF16),
-            pltpu.VMEM((width, total), BF16),
         ]
         + [pltpu.VMEM((rows, width), BF16)] * 4
         + [
             pltpu.VMEM((GROUP, rows, cols), BF16),
             copies,
             copies,
-            pltpu.SemaphoreType.DMA((4,)),
+            pltpu.SemaphoreType.DMA((3,)),
             pltpu.SemaphoreType.DMA((chunks,)),
         ],
         flops=2 * rows * width * (total + out_cols + 2 * units),
@@ -490,12 +605,12 @@
             for source, start, size in ((grad_kv, part, 2 * part), (grad_q, 0, part)):
                 at = pl.ds(pl.multiple_of(links.place * 3 * part + start, part), size)
                 across.append(
-                    links.copy(source.at[s, rows], full.at[rows, at], links.peer(s))
+                    links.copy(source.at[links.place ^ s, rows], full.at[rows, at], links.peer(s))
                 )
         for s in (2, 3, 1, 0):
             back.append(
                 links.copy(
-                    grad_kv_back.at[s, rows],
+                    grad_kv_back.at[links.place ^ s, rows],
                     back_got.at[s, rows],
                     links.beyond(links.groups - 1, s),
                 )
@@ -513,8 +628,8 @@
                     one.start()
 
         first = pl.multiple_of(links.place * 3 * part, part)
-        full[:, pl.ds(first, part)] = grad_q[0]
-        full[:, pl.ds(pl.multiple_of(first + part, part), 2 * part)] = grad_kv[0]
+        full[:, pl.ds(first, part)] = grad_q[links.place]
+        full[:, pl.ds(pl.multiple_of(first + part, part), 2 * part)] = grad_kv[links.place]
 
     def wait(c):
         across, back = copies[c]
@@ -563,9 +678,9 @@
     rows_within(first, body)
 
 
-def pull_feed_rows(rows, low, proj, hidden, grad_hidden, sums, fc, target):
+def pull_feed_rows(rows, low, proj, hidden, held, grad_hidden, sums, fc, target):
     def tile(at):
-        value = dot(low[rows, :], proj[:, at]) * gelu_slope(hidden[rows, at])
+        value = dot(low[rows, :], proj[:, at]) * gelu_slope(hidden[held, at])
         value = value.astype(BF16)
         grad_hidden[rows, at] = value
         sums[:, at] += eight_rows(value.astype(F32))
@@ -584,10 +699,11 @@
     for c in range(low.shape[0] // ROWS):
         rows = pl.ds(c * ROWS, ROWS)
         across = {
-            s: links.copy(ready.at[s, rows], pieces.at[s, rows], links.peer(s))
+            s: links.copy(ready.at[s, rows], pieces.at[links.place, rows], links.peer(s))
             for s in range(1, GROUP)
         }
-        copies.append((across, pltpu.make_async_copy(ready.at[0, rows], pieces.at[0, rows], kept.at[c])))
+        own = pltpu.make_async_copy(ready.at[0, rows], pieces.at[links.place, rows], kept.at[c])
+        copies.append((across, own))
 
     def start(c):
         rows = pl.ds(c * ROWS, ROWS)
@@ -624,11 +740,11 @@
     w_out, w_fc, w_proj, base, grad, hidden, part, got, part_three, got_three, ready,
     plain, flipped, away0, away1, met0, met1, send, recv, load, kept
 ):
-    fc_at, proj_at = at
+    out_at, fc_at, proj_at = at
     links = Links(send, recv)
     loads = load_columns(
         (
-            (rest, 0, w_out),
+            (rest, out_at, w_out),
             (base_in, None, base),
             (grad_in, None, grad),
             (rest, fc_at, w_fc),
@@ -668,7 +784,9 @@
             act[rows, at] = gelu_rows(value).astype(BF16)
 
         tiles(w_fc.shape[1], 512, tile)
-        pull_feed_rows(rows, low_proj, w_proj, hidden, grad_hidden, sum_fc, w_fc, part_three)
+        pull_feed_rows(
+            rows, low_proj, w_proj, hidden, rows, grad_hidden, sum_fc, w_fc, part_three
+        )
         swaps_three[c].start()
     core_sums[0].multiply(low_two, grad_hidden, plain, flipped)
     core_sums[1].multiply(low_proj, act, plain, flipped)
@@ -690,9 +808,9 @@
     finish_pull()
 
 
-def turn_segment(mixed_all, base, grad, vectors, rest, fc_at, proj_at):
+def turn_segment(mixed_all, base, grad, vectors, rest, at, units):
     rows, width = base.shape
-    out_cols, units = fc_at, proj_at - fc_at
+    out_cols = at[1] - at[0]
     cols = out_cols // GROUP
     chunks = rows // ROWS
     copies = pltpu.SemaphoreType.DMA((2 * chunks * (GROUP - 1) + 2 * chunks + 2,))
@@ -700,7 +818,7 @@
     low = (VMEM, shape((rows, width), BF16))
     sums = (VMEM, shape((8, width), F32))
     return run_links(
-        functools.partial(turn_body, (fc_at, proj_at)),
+        functools.partial(turn_body, at),
         2,
         [(VMEM, mixed_all), (ANY, base), (ANY, grad)]
         + [(VMEM, vector) for vector in vectors]
@@ -750,31 +868,36 @@
 
 def pull_both_body(
     at, grad_q, grad_kv, grad_kv_back, gain, gain_two, qkv, rest, grad_in, stream_in, hidden_in, middle_in,
-    stay0_in, met0_in, stay1_in, go1,
+    stay0_in, met0_in, stay1_in, go1, low_two_in, act_in,
     full, sum_qkv, sum_gain_one, sum_bias_one, low_proj, sum_proj, grad_hidden, sum_fc, grad_new, low_out,
-    sum_gain, sum_bias, sum_out, pieces, total0, total1,
-    w_qkv, w_out, w_fc, w_proj, grad, stream, hidden, middle, grad_mid, back_got,
-    part, got, part_two, got_two, ready,
-    stay0, met0, far0, came0, stay1, met1, far1, came1, send, recv, load, kept
+    sum_gain, sum_bias, sum_out, pieces, total0, total1, near2, *refs
 ):
-    first, fc_at, proj_at = at
+    groups = lax.axis_size("fsdp") // GROUP
+    far2, (stay3, go3), refs = refs[: groups - 1], refs[groups - 1 : groups + 1], refs[groups + 1 :]
+    (w_qkv, w_out, w_fc, w_proj, grad, stream, hidden, back_got, part, got, part_two, got_two, ready,
+    stay0, met0, far0, came0, stay1, met1, far1, came1,
+    left, wide, plain, flipped, stay2, go2, met2, away, gone2, gone3, send, recv, load, kept) = refs
+    out_at, fc_at, proj_at = at
     links = Links(send, recv)
     loads = load_columns(
         (
-            (qkv, first, w_qkv),
+            (qkv, None, w_qkv),
             (grad_in, None, grad),
             (stream_in, None, stream),
             (rest, proj_at, w_proj),
-            (hidden_in, None, hidden),
+            (hidden_in.at[pl.ds(0, ROWS)], None, hidden),
             (rest, fc_at, w_fc),
-            (middle_in, None, middle),
-            (rest, 0, w_out),
+            (rest, out_at, w_out),
             (stay0_in, None, stay0),
             (met0_in, None, met0),
             (stay1_in, None, stay1),
+            (low_two_in, None, left),
+            (act_in, None, wide),
         ),
         load,
     )
+    middle = stream
+    load_middle = pltpu.make_async_copy(middle_in, middle, load.at[len(loads)])
     links.greet(
         [links.peer(s) for s in range(1, GROUP)]
         + [links.beyond(1, s) for s in range(GROUP)]
@@ -794,61 +917,85 @@
         GroupSum(links, stay0, met0, far0, came0, total0),
         GroupSum(links, stay1, met1, far1, came1, total1),
     )
+    core_sums = (
+        CoreSum(links, stay2, go2, away, gone2),
+        CoreSum(links, stay3, go3, away, gone3),
+    )
+    feed_x = links.copy(go2, met2, links.peer(2))
     start_pulls()
+    late_x.start()
     for total in (sum_qkv, sum_gain_one, sum_bias_one, sum_proj, sum_fc, sum_gain, sum_bias, sum_out):
         total[...] = jnp.zeros_like(total)
     for one in loads:
         one.wait()
     group_sums[0].add()
+    group_sums[0].start()
     for c, rows in enumerate(chunks):
         wait_pulls(c)
-        if c == len(chunks) - 1:
-            late_x.start()
-            group_sums[0].start()
         pull_qkv_rows(c * ROWS, None, links, full, back_got, w_qkv, part, sum_qkv)
         swaps[c].start()
     for c, rows in enumerate(chunks):
         swaps[c].wait()
         pull_norm_rows(
-            c * ROWS, grad, part, got, stream, gain, grad_mid, (sum_gain_one, sum_bias_one)
+            c * ROWS, grad, part, got, stream, gain, grad_new, (sum_gain_one, sum_bias_one)
         )
-        round_rows(c * ROWS, grad_mid, low_proj, sum_proj)
-        pull_feed_rows(rows, low_proj, w_proj, hidden, grad_hidden, sum_fc, w_fc, part_two)
+        if c == len(chunks) - 1:
+            load_middle.start()
+        round_rows(c * ROWS, grad_new, low_proj, sum_proj)
+        if c:
+            load_hidden.wait()
+        pull_feed_rows(
+            rows, low_proj, w_proj, hidden, pl.ds(0, ROWS), grad_hidden, sum_fc, w_fc, part_two
+        )
         swaps_two[c].start()
+        if c + 1 < len(chunks):
+            load_hidden = pltpu.make_async_copy(
+                hidden_in.at[pl.ds((c + 1) * ROWS, ROWS)], hidden, load.at[len(loads) + 1 + c]
+            )
+            load_hidden.start()
+    core_sums[0].multiply(left, grad_hidden, plain, flipped)
+    load_middle.wait()
     late_x.wait()
     group_sums[1].add()
     group_sums[1].start()
     for c, rows in enumerate(chunks):
         swaps_two[c].wait()
         pull_norm_rows(
-            c * ROWS, grad_mid, part_two, got_two, middle, gain_two, grad_new, (sum_gain, sum_bias, sum_out), low_out
+            c * ROWS, grad_new, part_two, got_two, middle, gain_two, grad_new, (sum_gain, sum_bias, sum_out), low_out
         )
         start_pull(c)
+        if c == 0:
+            core_sums[0].add()
+            feed_x.start()
+            core_sums[1].multiply(low_proj, wide, plain, flipped)
+    core_sums[1].add()
+    feed_x.wait()
+    add_slots(stay2, met2, (near2, *far2))
     finish_pulls()
     finish_pull()
     for one in group_sums:
         one.finish()
 
 
-def pull_both_segment(pulls, gain, gain_two, qkv, first, rest, fc_at, proj_at, grad, stream, hidden, middle, sums_in):
+def pull_both_segment(pulls, gain, gain_two, qkv, rest, at, units, grad, stream, hidden, middle, sums_in, factors):
     rows, width = grad.shape
-    out_cols, units = fc_at, proj_at - fc_at
+    out_cols = at[1] - at[0]
     cols = out_cols // GROUP
     total = 3 * out_cols
     chunks = rows // ROWS
     groups = lax.axis_size("fsdp") // GROUP
     stay = sums_in[0]
-    copies = pltpu.SemaphoreType.DMA((pull_copies(rows) + chunks * (GROUP - 1) + 2 * chunks + 2 * groups - 1,))
+    copies = pltpu.SemaphoreType.DMA((pull_copies(rows) + chunks * (GROUP - 1) + 2 * chunks + 2 * groups + 2,))
     high = (VMEM, shape((rows, width), F32))
     low = (VMEM, shape((rows, width), BF16))
     sums = (VMEM, shape((8, width), F32))
     return run_links(
-        functools.partial(pull_both_body, (first, fc_at, proj_at)),
+        functools.partial(pull_both_body, at),
         3,
         [(VMEM, pull) for pull in pulls]
         + [(VMEM, gain), (VMEM, gain_two)]
         + [(ANY, array) for array in (qkv, rest, grad, stream, hidden, middle)]
-        + [(ANY, array) for array in sums_in],
+        + [(ANY, array) for array in (*sums_in, *factors)],
         [
             (VMEM, shape((rows, total), BF16)),
             (VMEM, shape((8, total), F32)),
@@ -865,7 +1012,10 @@
             sums,
             (ANY, shape((GROUP, rows, cols), BF16)),
         ]
-        + [(VMEM, shape((stay.shape[0] // groups, stay.shape[1]), F32))] * 2,
+        + [(VMEM, shape((stay.shape[0] // groups, stay.shape[1]), F32))] * 2
+        + [(VMEM, shape((width // 4 // groups, units), F32))]
+        + [(VMEM, shape((width // 4 // groups, units), BF16))] * (groups - 1)
+        + [(VMEM, shape((width // 4, units), BF16))] * 2,
         [
             pltpu.VMEM((width, total), BF16),
             pltpu.VMEM((width, out_cols), BF16),
@@ -873,9 +1023,7 @@
             pltpu.VMEM((width, units), BF16),
             pltpu.VMEM((rows, width), F32),
             pltpu.VMEM((rows, width), F32),
-            pltpu.VMEM((rows, units), F32),
-            pltpu.VMEM((rows, width), F32),
-            pltpu.VMEM((rows, width), F32),
+            pltpu.VMEM((ROWS, units), F32),
             pltpu.VMEM((GROUP, rows, 2 * cols), BF16),
         ]
         + [pltpu.VMEM((rows, width), BF16)] * 4
@@ -883,10 +1031,14 @@
             pltpu.VMEM((GROUP, rows, cols), BF16),
         ]
         + ([pltpu.VMEM(stay.shape, BF16)] + group_scratch(stay, groups, True)) * 2
+        + [pltpu.VMEM((rows, width), BF16), pltpu.VMEM((rows, units), BF16)]
+        + [pltpu.VMEM((width, rows), BF16)] * 2
+        + [pltpu.VMEM((width // 4, units), BF16)] * 3
+        + [pltpu.VMEM((width // 2, units), BF16)] * 3
         + [
             copies,
             copies,
-            pltpu.SemaphoreType.DMA((11,)),
+            pltpu.SemaphoreType.DMA((12 + chunks,)),
             pltpu.SemaphoreType.DMA((chunks,)),
         ],
         flops=2 * rows * width * (total + out_cols + 2 * units),
@@ -894,39 +1046,103 @@
     )
 
 
+def add_slots(stay, met, slots):
+    chunk = 16
+    depth = slots[0].shape[0]
+    for at, slot in enumerate(slots):
+
+        def body(rows):
+            from_row = pl.ds(pl.multiple_of(rows.start + at * depth, chunk), chunk)
+            total = stay[from_row, :].astype(F32) + met[from_row, :].astype(F32)
+            slot[rows, :] = total.astype(slot.dtype)
+
+        each_rows(depth, chunk, body)
+
+
+def pack_sums(sums, target, first):
+    width = target.shape[1]
+    at = first
+    for one in sums:
+        total = jnp.sum(one[...], 0, keepdims=True)
+        for start in range(0, total.shape[1], width):
+            size = min(width, total.shape[1] - start)
+            target[at : at + 1, :size] = total[:, start : start + size]
+            at += 1
+
+
+def finish_body(small, fc1, proj1, out1, proj0, out0, near, *refs):
+    *came, gain1, bias1, bqv, bout, gain2, bias2, bfc, bproj, wfc, wproj, wout = refs
+    fc0 = near[...]
+    for one in came:
+        fc0 = fc0 + one[...].astype(F32)
+    width = small.shape[1]
+    cols = bqv.shape[2] // GROUP
+    wfc[0] = fc0
+    wfc[1] = fc1[...]
+    for l, proj, out in ((0, proj0, out0), (1, proj1, out1)):
+        at = l * (small.shape[0] // 2)
+        for target, where in ((gain1, 0), (bias1, 1), (bout, 4), (gain2, 5), (bias2, 6), (bproj, 9)):
+            target[l : l + 1, :] = small[at + where : at + where + 1, :]
+        for i in range(bfc.shape[1] // width):
+            bfc[l : l + 1, i * width : (i + 1) * width] = small[at + 7 + i : at + 8 + i, :]
+        for place in range(GROUP):
+            for i in range(2):
+                where = place * 3 * cols + 2 * i * cols
+                line, lane = at + 2 + where // width, where % width
+                bqv[l, i : i + 1, place * cols : (place + 1) * cols] = small[
+                    line : line + 1, lane : lane + cols
+                ]
+        wproj[l] = proj[...].T
+        wout[l] = out[...].T
+
+
+def finish(small, totals, near, came, out_cols, units):
+    depth, width = totals[0].shape[0], small.shape[1]
+    vector = shape((LAYERS, width), F32)
+    outs = [vector, vector, shape((LAYERS, 2, out_cols), F32), vector, vector, vector]
+    outs += [shape((LAYERS, units), F32), vector, shape((LAYERS, depth, units), F32)]
+    outs += [shape((LAYERS, units, depth), F32), shape((LAYERS, out_cols, depth), F32)]
+    return pl.pallas_call(
+        finish_body,
+        in_specs=[VMEM] * (2 + len(totals) + len(came)),
+        out_specs=[VMEM] * len(outs),
+        out_shape=outs,
+        compiler_params=pltpu.CompilerParams(vmem_limit_bytes=VMEM_BYTES),
+    )(small, *totals, near, *came)
+
+
 def pull_last_body(
-    first, grad_q, grad_kv, grad_kv_back, gain, qkv, grad_in, stream_in,
-    low_two_in, grad_hidden_in, low_proj_in, act_in, low_one_in, low_out_in, mixed_in, stay0_in, met0_in, stay1_in, met1_in,
-    full, sum_qkv, sum_gain, sum_bias, grad_new, total0, total1, total2, total3, total4, total5,
-    w_qkv, grad, stream, back_got, part, got, left, right, wide, narrow, plain, flipped,
-    stay0, met0, far0, came0, stay1, met1, far1, came1,
+    grad_q, grad_kv, grad_kv_back, gain, qkv, grad_in, stream_in,
+    low_one1_in, grad_qkv1_in, low_out1_in, mixed1_in, low_one_in, low_out_in, mixed_in, stay0_in, met0_in,
+    gain1, bias1, bqkv1, bout1, gain2_1, bias2_1, bfc1, bproj1, bout0, gain2_0, bias2_0, bfc0, bproj0,
+    grad_new, small, total0, total1, total2, total3, total4,
+    full, sum_qkv, sum_gain, sum_bias, held, came, far, w_qkv, grad, stream, back_got, part, got,
+    left1, wide1, right1, narrow1, left, right, narrow, plain, flipped,
+    stay0, met0, far0, came0,
+    away1, gone1, stay1, go1, met1, far1, came1,
     away2, gone2, stay2, go2, met2, far2, came2,
     away3, gone3, stay3, go3, met3, far3, came3,
     away4, gone4, stay4, go4, met4, far4, came4,
-    away5, gone5, stay5, go5, met5, far5, came5,
     send, recv, load
 ):
     links = Links(send, recv)
     loads = load_columns(
         (
-            (low_two_in, None, left),
-            (grad_hidden_in, None, wide),
+            (low_one1_in, None, left1),
+            (grad_qkv1_in, None, wide1),
+            (low_out1_in, None, right1),
+            (mixed1_in, None, narrow1),
             (stay0_in, None, stay0),
             (met0_in, None, met0),
-            (stay1_in, None, stay1),
-            (met1_in, None, met1),
-            (low_proj_in, None, right),
-            (qkv, first, w_qkv),
+            (qkv, None, w_qkv),
             (grad_in, None, grad),
             (stream_in, None, stream),
+            (low_one_in, None, left),
+            (low_out_in, None, right),
             (mixed_in, None, narrow),
         ),
         load,
     )
-    again = [
-        pltpu.make_async_copy(source, target, load.at[len(loads) + i])
-        for i, (source, target) in enumerate(((act_in, wide), (low_one_in, left), (low_out_in, right)))
-    ]
     links.greet(
         [links.peer(s) for s in range(1, GROUP)]
         + [links.beyond(1, s) for s in range(GROUP)]
@@ -940,119 +1156,138 @@
     )
     swaps = [links.swap(part.at[rows], got.at[rows]) for rows in chunks]
     parts = (
-        (away2, gone2, stay2, go2, met2),
-        (away3, gone3, stay3, go3, met3),
-        (away4, gone4, stay4, go4, met4),
-        (away5, gone5, stay5, go5, met5),
-    )
-    core_sums = [CoreSum(links, stay, go, away, gone) for away, gone, stay, go, _ in parts]
-    over_x = [links.copy(go, met, links.peer(2)) for _, _, _, go, met in parts]
-    group_sums = [
-        GroupSum(links, *refs)
-        for refs in (
-            (stay0, met0, far0, came0, total0),
-            (stay1, met1, far1, came1, total1),
-            (stay2, met2, far2, came2, total2),
-            (stay3, met3, far3, came3, total3),
-            (stay4, met4, far4, came4, total4),
-            (stay5, met5, far5, came5, total5),
-        )
-    ]
+        (away1, gone1, stay1, go1, met1, far1, came1, total1),
+        (away2, gone2, stay2, go2, met2, far2, came2, total2),
+        (away3, gone3, stay3, go3, met3, far3, came3, total3),
+        (away4, gone4, stay4, go4, met4, far4, came4, total4),
+    )
+    core_sums, over_x, group_sums, spans = [], [], [], []
+    for at, (away, gone, stay, go, met, *rest) in enumerate(parts):
+        core_sums.append(CoreSum(links, stay, go, away, gone))
+        size = stay.shape[1]
+        step = size if at % 2 else size // 2
+        spans.append([])
+        for start in range(0, size, step):
+            place = pl.ds(start, step)
+            spans[at].append(len(over_x))
+            over_x.append(links.copy(go.at[:, place], met.at[:, place], links.peer(2)))
+            group_sums.append(GroupSum(links, *[ref.at[:, place] for ref in (stay, met, *rest)]))
+    early_sum = GroupSum(links, stay0, met0, far0, came0, total0)
+    smalls = RowSum(links, held, came, far)
+    sums_one = (gain1, bias1, bqkv1, bout1, gain2_1, bias2_1, bfc1, bproj1)
+    sums_zero = (sum_gain, sum_bias, sum_qkv, bout0, gain2_0, bias2_0, bfc0, bproj0)
     start_pulls()
     for total in (sum_qkv, sum_gain, sum_bias):
         total[...] = jnp.zeros_like(total)
-    loads[0].wait()
-    loads[1].wait()
-    core_sums[0].multiply(left, wide, plain, flipped)
-    again[0].start()
-    again[1].start()
-    for one in loads[2:]:
+    for one in loads:
         one.wait()
-    group_sums[0].add()
-    group_sums[1].add()
-    again[0].wait()
-    core_sums[1].multiply(right, wide, plain, flipped)
-    again[2].start()
+    early_sum.add()
+    early_sum.start()
+    core_sums[0].multiply(left1, wide1, plain, flipped)
+    core_sums[1].multiply(right1, narrow1, plain, flipped)
+    held[0] = jnp.zeros(held.shape[1:], F32)
+    pack_sums(sums_one, held.at[0], held.shape[1] // 2)
     core_sums[0].add()
     core_sums[1].add()
+    for at in spans[0] + spans[1]:
+        over_x[at].start()
     for c, rows in enumerate(chunks):
         wait_pulls(c)
-        if c == len(chunks) - 1:
-            over_x[0].start()
-            group_sums[0].start()
-            group_sums[1].start()
-            over_x[1].start()
         pull_qkv_rows(c * ROWS, None, links, full, back_got, w_qkv, part, sum_qkv)
         swaps[c].start()
-    again[1].wait()
-    again[2].wait()
     core_sums[2].multiply(left, full, plain, flipped)
     core_sums[3].multiply(right, narrow, plain, flipped)
+    core_sums[2].add()
+    for at in spans[2]:
+        over_x[at].start()
+    core_sums[3].add()
+    for at in spans[3]:
+        over_x[at].start()
     for c, rows in enumerate(chunks):
         swaps[c].wait()
         pull_norm_rows(c * ROWS, grad, part, got, stream, gain, grad_new, (sum_gain, sum_bias))
-    for at in (2, 3):
-        core_sums[at].add()
-        over_x[at].start()
-    for at in range(4):
+    pack_sums(sums_zero, held.at[0], 0)
+    smalls.near[0].start()
+    smalls.step(0)
+    smalls.near[1].start()
+    for at, one in enumerate(group_sums):
         over_x[at].wait()
-        group_sums[2 + at].add()
-        group_sums[2 + at].start()
+        one.add()
+        one.start()
+        if at == 3:
+            smalls.step(1)
+            for far_one in smalls.along:
+                far_one.start()
     finish_pulls()
+    small[...] = smalls.finish()
+    early_sum.finish()
     for one in group_sums:
         one.finish()
 
 
-def pull_last_segment(pulls, gain, qkv, first, grad, stream, factors, sums_in):
+def pull_last_segment(pulls, gain, qkv, grad, stream, factors, sums_in, smalls):
     rows, width = grad.shape
     cols = pulls[0].shape[2]
-    total = 3 * GROUP * cols
-    units = factors[1].shape[1]
+    out_cols = GROUP * cols
+    total = 3 * out_cols
+    units = sums_in[0].shape[1]
     chunks = rows // ROWS
     groups = lax.axis_size("fsdp") // GROUP
-    copies = pltpu.SemaphoreType.DMA((pull_copies(rows) + chunks + 8 + 6 * (groups - 1),))
-    sums = (VMEM, shape((8, width), F32))
-    sizes = [sums_in[0].shape[1], sums_in[2].shape[1], units, units, total, GROUP * cols]
+    copies = pltpu.SemaphoreType.DMA(
+        (pull_copies(rows) + chunks + 10 + 7 * (groups - 1) + groups + 1,)
+    )
+    sizes = [total, out_cols, total, out_cols]
     quarter = width // 4
     scratch = []
-    for at, size in enumerate(sizes):
+    for size in sizes:
         stay = shape((quarter, size), BF16)
-        if at >= 2:
-            scratch += [pltpu.VMEM((2 * quarter, size), BF16)] * 2
-            scratch += [pltpu.VMEM(stay.shape, BF16)]
+        scratch += [pltpu.VMEM((2 * quarter, size), BF16)] * 2
+        scratch += [pltpu.VMEM(stay.shape, BF16)]
         scratch += [pltpu.VMEM(stay.shape, BF16)] + group_scratch(stay, groups, True)
+    low = pltpu.VMEM((rows, width), BF16)
+    high = pltpu.VMEM((rows, width), F32)
+    mixed = pltpu.VMEM((rows, out_cols), BF16)
+    flip = pltpu.VMEM((width, rows), BF16)
+    eight = pltpu.VMEM((8, width), F32)
     return run_links(
-        functools.partial(pull_last_body, first),
+        pull_last_body,
         4,
         [(VMEM, pull) for pull in pulls]
         + [(VMEM, gain)]
-        + [(ANY, array) for array in (qkv, grad, stream, *factors, *sums_in)],
+        + [(ANY, array) for array in (qkv, grad, stream, *factors, *sums_in)]
+        + [(VMEM, array) for array in smalls],
+        [(VMEM, shape((rows, width), F32)), (VMEM, shape((24, width), F32))]
+        + [(VMEM, shape((quarter // groups, size), F32)) for size in [units] + sizes],
         [
-            (VMEM, shape((rows, total), BF16)),
-            (VMEM, shape((8, total), F32)),
-            sums,
-            sums,
-            (VMEM, shape((rows, width), F32)),
+            pltpu.VMEM((rows, total), BF16),
+            pltpu.VMEM((8, total), F32),
+            eight,
+            eight,
+            pltpu.VMEM((3, 24, width), F32),
+            pltpu.VMEM((2, 24, width), F32),
+            pltpu.VMEM((groups - 1, 24, width), F32),
+            pltpu.VMEM((width, total), BF16),
+            high,
+            high,
+            pltpu.VMEM((GROUP, rows, 2 * cols), BF16),
+            low,
+            low,
+            low,
+            pltpu.VMEM((rows, total), BF16),
+            low,
+            mixed,
+            low,
+            low,
+            mixed,
+            flip,
+            flip,
+            pltpu.VMEM((quarter, units), BF16),
         ]
-        + [(VMEM, shape((quarter // groups, size), F32)) for size in sizes],
-        [
-            pltpu.VMEM((width, total), BF16),
-            pltpu.VMEM((rows, width), F32),
-            pltpu.VMEM((rows, width), F32),
-            pltpu.VMEM((GROUP, rows, 2 * cols), BF16),
-            pltpu.VMEM((rows, width), BF16),
-            pltpu.VMEM((rows, width), BF16),
-            pltpu.VMEM((rows, width), BF16),
-            pltpu.VMEM((rows, width), BF16),
-            pltpu.VMEM((rows, units), BF16),
-            pltpu.VMEM((rows, GROUP * cols), BF16),
-            pltpu.VMEM((width, rows), BF16),
-            pltpu.VMEM((width, rows), BF16),
-        ]
+        + group_scratch(shape((quarter, units), BF16), groups, True)
         + scratch
-        + [copies, copies, pltpu.SemaphoreType.DMA((14,))],
-        flops=2 * rows * width * total * 2 + 4 * rows * width * units,
-        moved=rows * width * 24 + rows * units * 4 + width * total * 2,
+        + [copies, copies, pltpu.SemaphoreType.DMA((12,))],
+        flops=2 * rows * width * (3 * total + 2 * out_cols),
+        moved=rows * width * 24 + width * total * 2,
     )
 
 
@@ -1073,6 +1308,11 @@
     def __init__(self, links, stay, go, away, got):
         self.links, self.stay, self.go, self.away, self.got = links, stay, go, away, got
         self.copy = links.copy(away, got, links.peer(1))
+        self.sent = False
+
+    def release(self):
+        self.copy.wait_send()
+        self.sent = True
 
     def multiply(self, x, g, plain, flipped):
         flip_slots(self.links, x, plain, flipped)
@@ -1090,7 +1330,9 @@
         tiles(g.shape[1], 512, near)
 
     def add(self):
-        self.copy.wait()
+        if not self.sent:
+            self.release()
+        self.copy.wait_recv()
         quarter = self.stay.shape[0]
         chunk = 16
         for target, first in ((self.go, quarter), (self.stay, 0)):
@@ -1101,35 +1343,6 @@
                 target[at, :] = total.astype(BF16)
 
             each_rows(quarter, chunk, body)
-
-
-def weight_pull_body(x0, g0, x1, g1, stay0, go0, stay1, go1, plain, flipped, away0, got0, away1, got1, send, recv):
-    links = Links(send, recv)
-    links.greet([links.peer(1)])
-    first = CoreSum(links, stay0, go0, away0, got0)
-    second = CoreSum(links, stay1, go1, away1, got1)
-    first.multiply(x0, g0, plain, flipped)
-    second.multiply(x1, g1, plain, flipped)
-    first.add()
-    second.add()
-
-
-def weight_pull(name, x0, g0, x1, g1):
-    rows, width = x0.shape
-    sizes = (g0.shape[1], g1.shape[1])
-    quarter = [(VMEM, shape((width // 4, size), BF16)) for size in sizes]
-    half = [pltpu.VMEM((width // 2, size), BF16) for size in sizes]
-    return run_links(
-        weight_pull_body,
-        name,
-        [(VMEM, array) for array in (x0, g0, x1, g1)],
-        [quarter[0], quarter[0], quarter[1], quarter[1]],
-        [pltpu.VMEM((width, rows), BF16), pltpu.VMEM((width, rows), BF16)]
-        + [half[0], half[0], half[1], half[1]]
-        + [pltpu.SemaphoreType.DMA((2,)), pltpu.SemaphoreType.DMA((2,))],
-        flops=2 * rows * width * sum(sizes),
-        moved=rows * width * 4 + (rows + width) * sum(sizes) * 2,
-    )
 
 
 class GroupSum:
@@ -1201,9 +1414,9 @@
     return start
 
 
-def query_rows(sc, docs, block):
-    first = sc[1] + block * QB
-    position = first + lax.broadcasted_iota(jnp.int32, (1, QB), 1)
+def query_rows(sc, docs, block, size):
+    first = sc[1] + block * size
+    position = first + lax.broadcasted_iota(jnp.int32, (1, size), 1)
     start = doc_start_rows(sc, docs, position)
     return (
         jnp.concatenate([position, position], 1),
@@ -1222,36 +1435,19 @@
     ).astype(BF16)
 
 
-def place_rows(sc, s, rows):
-    return pl.ds(pl.multiple_of((sc[0] ^ s) * rows, rows), rows)
-
-
-def spread(sc, pieces, first_col, cols, straight=None, flipped=None):
-    for s, piece in enumerate(pieces):
-        value = piece[s] if len(piece.shape) == 3 and piece.shape[0] > 1 else None
-        if value is None:
-            value = piece[0] if len(piece.shape) == 3 else piece[...]
-        value = value[:, first_col : first_col + cols]
-        at = place_rows(sc, s, value.shape[0])
-        if straight is not None:
-            straight[at, :] = value
-        if flipped is not None:
-            flipped[:, at] = value.T
-
-
 def block_at(block, size):
     return pl.ds(pl.multiple_of(block * size, size), size)
 
 
 def masked_scores(keys, queries, first_key, position, start):
     scores = dot_last(keys, queries)
-    key_at = first_key + lax.broadcasted_iota(jnp.int32, (KB, 1), 0)
+    key_at = first_key + lax.broadcasted_iota(jnp.int32, (keys.shape[0], 1), 0)
     return jnp.where((key_at >= start) & (key_at <= position), scores, NEG)
 
 
-def flash_step(keys_ref, values_ref, queries, block, first_key, position, start, acc, carry):
+def flash_step(keys, values_ref, queries, at, first_key, position, start, acc, carry):
     top, total = carry
-    scores = masked_scores(keys_ref[block_at(block, KB), :], queries, first_key, position, start)
+    scores = masked_scores(keys, queries, first_key, position, start)
     top_new = jnp.maximum(top, jnp.max(scores, 0, keepdims=True))
     expo = jnp.exp(scores - top_new)
     shrink = jnp.exp(top - top_new)
@@ -1260,40 +1456,38 @@
     for h in range(2):
         lanes = slice(h * QB, (h + 1) * QB)
         rows = slice(h * HEAD_DIM, (h + 1) * HEAD_DIM)
-        values = values_ref[rows, block_at(block, KB)]
-        acc[rows, :] = acc[rows, :] * shrink[:, lanes] + dot(values, expo[:, lanes])
+        acc[rows, :] = acc[rows, :] * shrink[:, lanes] + dot(values_ref[rows, at], expo[:, lanes])
     return top_new, total
 
 
-def attend_body(docs, sc, p0, kv, mixed, out, log_total, q_all, k_all, v_flip, k_back, v_back, acc):
+def attend_body(docs, sc, qkv, kv, mixed, out, log_total, v_flip, v_back, acc):
     block = pl.program_id(0)
-    span, cols = q_all.shape
+    span, cols = out.shape[0] * pl.num_programs(0), out.shape[1]
+    rows = qkv.shape[0]
 
     @pl.when(block == 0)
     def _():
-        pieces = (p0,) * GROUP
-        spread(sc, pieces, 0, cols, straight=q_all)
-        spread(sc, pieces, cols, cols, straight=k_all)
-        spread(sc, pieces, 2 * cols, cols, flipped=v_flip)
-        spread(sc, (kv,) * GROUP, 0, cols, straight=k_back)
-        spread(sc, (kv,) * GROUP, cols, cols, flipped=v_back)
-
-    position, start, lowest = query_rows(sc, docs, block)
-    queries = head_stack(q_all[block_at(block, QB), :], HEAD_DIM**-0.5)
+        for first in range(0, rows, QB):
+            v_flip[:, first : first + QB] = qkv[first : first + QB, 2 * cols :].T
+            v_back[:, first : first + QB] = kv[first : first + QB, cols:].T
+
+    position, start, lowest = query_rows(sc, docs, block, QB)
+    queries = head_stack(qkv[block_at(block, QB), :cols], HEAD_DIM**-0.5)
     acc[...] = jnp.zeros_like(acc)
     least = jnp.maximum(lowest - sc[1], 0) // KB
     last = ((block + 1) * QB - 1) // KB
     before = sc[1] - span
 
     def step(back, carry):
-        at = last - back
+        at = block_at(last - back, KB)
+        keys = qkv[at, cols : 2 * cols]
+        first_key = sc[1] + (last - back) * KB
+        return flash_step(keys, v_flip, queries, at, first_key, position, start, acc, carry)
+
+    def step_back(where, carry):
+        at = block_at(where, KB)
         return flash_step(
-            k_all, v_flip, queries, at, sc[1] + at * KB, position, start, acc, carry
-        )
-
-    def step_back(at, carry):
-        return flash_step(
-            k_back, v_back, queries, at, before + at * KB, position, start, acc, carry
+            kv[at, :cols], v_back, queries, at, before + where * KB, position, start, acc, carry
         )
 
     carry = (jnp.full((1, 2 * QB), NEG, F32), jnp.zeros((1, 2 * QB), F32))
@@ -1310,143 +1504,130 @@
         parts.append(acc[h * HEAD_DIM : (h + 1) * HEAD_DIM, :] * share[:, lanes])
     value = jnp.concatenate(parts, 0).T
     out[...] = value
-    mixed[0] = value.astype(BF16)
-
-
-def slot_spec(rows, cols):
-    per = rows // QB
-    return pl.BlockSpec((1, QB, cols), lambda j, sc: ((j // per) ^ sc[0], j % per, 0))
+    mixed[...] = value.astype(BF16)
 
 
 def attend(sc, docs, pieces, kv):
     rows, cols = pieces.shape[1], pieces.shape[2] // 3
     span = GROUP * rows
-    stat = (pl.BlockSpec((8, QB), lambda j, sc: (0, j)), shape((8, span), F32))
-    low = pltpu.VMEM((span, cols), BF16)
     low_flip = pltpu.VMEM((cols, span), BF16)
-    return run_kernel(
+    block = pl.BlockSpec((QB, cols), lambda j, sc: (j, 0))
+    mixed, out, log_total = run_kernel(
         functools.partial(attend_body, docs),
         (span // QB,),
         sc,
-        [(whole(pieces.shape), pieces), (whole(kv.shape), kv)],
         [
-            (slot_spec(rows, cols), shape((GROUP, rows, cols), BF16)),
-            (pl.BlockSpec((QB, cols), lambda j, sc: (j, 0)), shape((span, cols), F32)),
-            stat,
+            (whole((span, 3 * cols)), pieces.reshape(span, 3 * cols)),
+            (whole((span, 2 * cols)), kv.reshape(span, 2 * cols)),
         ],
-        scratch=[low, low, low_flip, low, low_flip, pltpu.VMEM((cols, QB), F32)],
+        [
+            (block, shape((span, cols), BF16)),
+            (block, shape((span, cols), F32)),
+            (pl.BlockSpec((8, QB), lambda j, sc: (0, j)), shape((8, span), F32)),
+        ],
+        scratch=[low_flip, low_flip, pltpu.VMEM((cols, QB), F32)],
         flops=span * span * cols * 4,
         moved=span * cols * 20,
     )
-
-
-def pull_step(block, first_key, position, start, queries, grads, log_rows, delta, refs):
-    k_all, v_all, k_flip, grad_k, grad_v, grad_q = refs
-    at = block_at(block, KB)
-    scores = masked_scores(k_all[at, :], queries, first_key, position, start)
+    return mixed.reshape(GROUP, rows, cols), out, log_total
+
+
+def pull_step(keys, values, at, first_key, position, start, queries, grads, log_rows, delta, refs):
+    k_flip, grad_k, grad_v, grad_q = refs
+    scores = masked_scores(keys, queries, first_key, position, start)
     probs = jnp.exp(scores - log_rows)
-    grad_probs = dot_last(v_all[at, :], grads)
+    grad_probs = dot_last(values, grads)
     grad_scores = (probs * (grad_probs - delta)).astype(BF16)
     grad_v[at, :] += dot(probs.astype(BF16), grads)
     grad_k[at, :] += dot(grad_scores, queries)
+    size = grad_q.shape[1]
     for h in range(2):
         rows = slice(h * HEAD_DIM, (h + 1) * HEAD_DIM)
-        grad_q[rows, :] += dot(k_flip[rows, at], grad_scores[:, h * QB : (h + 1) * QB])
-
-
-def pull_rows(block, q_all, g_all, out, log_total):
-    queries = head_stack(q_all[block_at(block, QB), :], HEAD_DIM**-0.5)
-    grad_rows = g_all[block_at(block, QB), :]
+        grad_q[rows, :] += dot(k_flip[rows, at], grad_scores[:, h * size : (h + 1) * size])
+
+
+def pull_body(
+    docs, sc, qkv, grad_mixed, kv, out, log_total, grad_q_out, grad_kv, grad_kv_back,
+    k_flip, grad_k, grad_v, k_back_flip, grad_k_back, grad_v_back, grad_q
+):
+    block = pl.program_id(0)
+    span, cols = qkv.shape[0], out.shape[1]
+    size = out.shape[0]
+    before = sc[1] - span
+
+    @pl.when(block == 0)
+    def _():
+        for first in range(0, span, PULL_KB):
+            k_flip[:, first : first + PULL_KB] = qkv[first : first + PULL_KB, cols : 2 * cols].T
+            k_back_flip[:, first : first + PULL_KB] = kv[first : first + PULL_KB, :cols].T
+        for total in (grad_k, grad_v, grad_k_back, grad_v_back):
+            total[...] = jnp.zeros_like(total)
+
+    grad_q[...] = jnp.zeros_like(grad_q)
+    position, start, lowest = query_rows(sc, docs, block, size)
+    queries = head_stack(qkv[block_at(block, size), :cols], HEAD_DIM**-0.5)
+    grad_rows = grad_mixed[block_at(block, size), :]
     grads = head_stack(grad_rows, 1.0)
     flipped = (grad_rows.astype(F32) * out[...]).T
-    delta = jnp.concatenate(
-        [
-            jnp.sum(flipped[h * HEAD_DIM : (h + 1) * HEAD_DIM, :], 0, keepdims=True)
-            for h in range(2)
-        ],
-        1,
-    )
+    heads = [slice(h * HEAD_DIM, (h + 1) * HEAD_DIM) for h in range(2)]
+    delta = jnp.concatenate([jnp.sum(flipped[rows, :], 0, keepdims=True) for rows in heads], 1)
     log_rows = jnp.concatenate([log_total[h : h + 1, :] for h in range(2)], 1)
-    return queries, grads, log_rows, delta
-
-
-def pull_body(
-    docs, sc, p0, g0, kv, out, log_total, grad_q_out, grad_kv, grad_kv_back,
-    q_all, g_all, k_all, v_all, k_flip, grad_k, grad_v, k_back, v_back, k_back_flip, grad_k_back, grad_v_back, grad_q
-):
-    block = pl.program_id(0)
-    span, cols = q_all.shape
-    before = sc[1] - span
-
-    @pl.when(block == 0)
-    def _():
-        pieces = (p0,) * GROUP
-        spread(sc, pieces, 0, cols, straight=q_all)
-        spread(sc, (g0,) * GROUP, 0, cols, straight=g_all)
-        spread(sc, pieces, cols, cols, straight=k_all, flipped=k_flip)
-        spread(sc, pieces, 2 * cols, cols, straight=v_all)
-        spread(sc, (kv,) * GROUP, 0, cols, straight=k_back, flipped=k_back_flip)
-        spread(sc, (kv,) * GROUP, cols, cols, straight=v_back)
-        for total in (grad_k, grad_v, grad_k_back, grad_v_back):
-            total[...] = jnp.zeros_like(total)
-
-    grad_q[...] = jnp.zeros_like(grad_q)
-    position, start, lowest = query_rows(sc, docs, block)
-    queries, grads, log_rows, delta = pull_rows(block, q_all, g_all, out, log_total)
-
-    def step(first, refs, at, carry):
-        pull_step(at, first + at * KB, position, start, queries, grads, log_rows, delta, refs)
+
+    def step(where, carry):
+        at = block_at(where, PULL_KB)
+        pull_step(
+            qkv[at, cols : 2 * cols], qkv[at, 2 * cols :], at, sc[1] + where * PULL_KB,
+            position, start, queries, grads, log_rows, delta, (k_flip, grad_k, grad_v, grad_q),
+        )
         return carry
 
-    own_refs = (k_all, v_all, k_flip, grad_k, grad_v, grad_q)
-    back_refs = (k_back, v_back, k_back_flip, grad_k_back, grad_v_back, grad_q)
-    last = ((block + 1) * QB - 1) // KB
+    def step_back(where, carry):
+        at = block_at(where, PULL_KB)
+        pull_step(
+            kv[at, :cols], kv[at, cols:], at, before + where * PULL_KB,
+            position, start, queries, grads, log_rows, delta, (k_back_flip, grad_k_back, grad_v_back, grad_q),
+        )
+        return carry
+
+    last = ((block + 1) * size - 1) // PULL_KB
+    lax.fori_loop(jnp.maximum(lowest - sc[1], 0) // PULL_KB, last + 1, step, 0)
     lax.fori_loop(
-        jnp.maximum(lowest - sc[1], 0) // KB, last + 1, functools.partial(step, sc[1], own_refs), 0
-    )
-    lax.fori_loop(
-        jnp.minimum(jnp.maximum(lowest - before, 0), span) // KB,
-        span // KB,
-        functools.partial(step, before, back_refs),
-        0,
-    )
-    grad_q_out[0] = (grad_q[...] * HEAD_DIM**-0.5).T.astype(BF16)
+        jnp.minimum(jnp.maximum(lowest - before, 0), span) // PULL_KB, span // PULL_KB, step_back, 0
+    )
+    grad_q_out[...] = (grad_q[...] * HEAD_DIM**-0.5).T.astype(BF16)
 
     @pl.when(block == pl.num_programs(0) - 1)
     def _():
-        for s in range(GROUP):
-            at = place_rows(sc, s, span // GROUP)
-            grad_kv[s, :, :cols] = grad_k[at, :].astype(BF16)
-            grad_kv[s, :, cols:] = grad_v[at, :].astype(BF16)
-            grad_kv_back[s, :, :cols] = grad_k_back[at, :].astype(BF16)
-            grad_kv_back[s, :, cols:] = grad_v_back[at, :].astype(BF16)
+        grad_kv[:, :cols] = grad_k[...].astype(BF16)
+        grad_kv[:, cols:] = grad_v[...].astype(BF16)
+        grad_kv_back[:, :cols] = grad_k_back[...].astype(BF16)
+        grad_kv_back[:, cols:] = grad_v_back[...].astype(BF16)
 
 
 def attend_pull(sc, docs, pieces, grads, kv, out, log_total):
     rows, cols = pieces.shape[1], pieces.shape[2] // 3
     span = GROUP * rows
-    ins = [
-        (whole(pieces.shape), pieces),
-        (whole(grads.shape), grads),
-        (whole(kv.shape), kv),
-        (pl.BlockSpec((QB, cols), lambda j, sc: (j, 0)), out),
-        (pl.BlockSpec((8, QB), lambda j, sc: (0, j)), log_total),
-    ]
-    both = (whole((GROUP, rows, 2 * cols)), shape((GROUP, rows, 2 * cols), BF16))
-    low = pltpu.VMEM((span, cols), BF16)
+    block = pl.BlockSpec((PULL_QB, cols), lambda j, sc: (j, 0))
+    both = (whole((span, 2 * cols)), shape((span, 2 * cols), BF16))
     low_flip = pltpu.VMEM((cols, span), BF16)
     high = pltpu.VMEM((span, cols), F32)
-    return run_kernel(
+    parts = run_kernel(
         functools.partial(pull_body, docs),
-        (span // QB,),
+        (span // PULL_QB,),
         sc,
-        ins,
-        [(slot_spec(rows, cols), shape((GROUP, rows, cols), BF16)), both, both],
-        scratch=[low, low, low, low, low_flip, high, high, low, low, low_flip, high, high]
-        + [pltpu.VMEM((cols, QB), F32)],
+        [
+            (whole((span, 3 * cols)), pieces.reshape(span, 3 * cols)),
+            (whole((span, cols)), grads.reshape(span, cols)),
+            (whole((span, 2 * cols)), kv.reshape(span, 2 * cols)),
+            (block, out),
+            (pl.BlockSpec((8, PULL_QB), lambda j, sc: (0, j)), log_total),
+        ],
+        [(block, shape((span, cols), BF16)), both, both],
+        scratch=[low_flip, high, high, low_flip, high, high, pltpu.VMEM((cols, PULL_QB), F32)],
         flops=span * span * cols * 9,
         moved=span * cols * 30,
     )
+    return [part.reshape(GROUP, rows, part.shape[1]) for part in parts]
 
 
 def swap_tp(value):
@@ -1460,18 +1641,6 @@
 def shift_fsdp(value, by):
     size = lax.axis_size("fsdp")
     return lax.ppermute(value, "fsdp", [(i, i + by) for i in range(size) if 0 <= i + by < size])
-
-
-def butterfly(value):
-    s = 1
-    while s < lax.axis_size("fsdp"):
-        value = value + swap_fsdp(value, s)
-        s *= 2
-    return value
-
-
-def trade(pieces):
-    return [pieces] + [swap_fsdp(pieces[s], s) for s in range(1, GROUP)]
 
 
 def gather(shard):
@@ -1515,38 +1684,41 @@
     def pack_rest(l):
         return [w_out[l].T, w_fc[l], w_proj[l].T]
 
-    fc_at, proj_at = out_cols, out_cols + units
-    rest_cols = out_cols + 2 * units
-    full_a = gather(pack_qkv(0))
-    full_b = gather(jnp.concatenate(pack_rest(0) + [pack_qkv(1)], 1))
-    full_c = gather(jnp.concatenate(pack_rest(1), 1))
-    qkv_of = ((full_a, 0), (full_b, rest_cols))
-    rest_of = (full_b, full_c)
-
+    rest = gather(jnp.concatenate(pack_rest(0) + pack_rest(1), 1))
+
+    def rest_at(l):
+        first = l * (out_cols + 2 * units)
+        return (first, first + out_cols, first + out_cols + units)
+
+    def bias_qkv(l):
+        three = jnp.stack([b_qv[l, 0], jnp.zeros_like(b_qv[l, 0]), b_qv[l, 1]])
+        return three.reshape(3, GROUP, cols).transpose(1, 0, 2).reshape(1, 3 * out_cols)
+
+    def row(vector):
+        return vector.reshape(1, vector.shape[0])
+
+    stored = []
+    stream, low_one, full_qkv, doc_tokens, doc_first, pieces, kv_back = first_segment(
+        tokens,
+        row(ln1_gain[0]),
+        row(ln1_bias[0]),
+        pack_qkv(0),
+        bias_qkv(0),
+        segments.reshape(rows // 128, 128),
+        docs,
+    )
+    qkv_of = [full_qkv]
+    doc_tokens, doc_first = (value[:, 0].astype(jnp.int32) for value in (doc_tokens, doc_first))
+    sc = jnp.concatenate(
+        [jnp.stack([me % GROUP, (me // GROUP) * (GROUP * rows)]).astype(jnp.int32), doc_first]
+    )
     doc_ids = jnp.arange(docs, dtype=jnp.int32)
     is_doc = segments[:, None] == doc_ids[None, :]
-    doc_tokens = butterfly(jnp.sum(is_doc.astype(jnp.int32), 0))
-    doc_first = jnp.cumsum(doc_tokens) - doc_tokens
     in_batch = doc_batch[:, None] == jnp.arange(MB, dtype=jnp.int32)[None, :]
     counts = jnp.sum(jnp.where(in_batch, doc_tokens[:, None], 0), 0)
     doc_count = jnp.sum(jnp.where(in_batch, counts[None, :], 0), 1)
     row_count = jnp.sum(jnp.where(is_doc, doc_count[None, :], 0), 1).astype(F32)
     row_weight = total_rows / (MB * row_count)
-    sc = jnp.concatenate(
-        [jnp.stack([me % GROUP, (me // GROUP) * (GROUP * rows)]).astype(jnp.int32), doc_first]
-    )
-
-    def bias_qkv(l):
-        three = jnp.stack([b_qv[l, 0], jnp.zeros_like(b_qv[l, 0]), b_qv[l, 1]])
-        return three.reshape(3, GROUP, cols).transpose(1, 0, 2).reshape(1, 3 * out_cols)
-
-    def row(vector):
-        return vector.reshape(1, vector.shape[0])
-
-    stored = []
-    stream, low_one, pieces, kv_back = first_segment(
-        tokens, row(ln1_gain[0]), row(ln1_bias[0]), full_a, bias_qkv(0)
-    )
     for l in range(LAYERS - 1):
         mixed, out, log_total = attend(sc, docs, pieces, kv_back)
         vectors = (b_out[l], ln2_gain[l], ln2_bias[l], b_fc[l], b_proj[l], ln1_gain[l + 1], ln1_bias[l + 1])
@@ -1555,15 +1727,16 @@
             stream,
             [row(vector) for vector in vectors],
             bias_qkv(l + 1),
-            rest_of[l],
-            fc_at,
-            proj_at,
-            *qkv_of[l + 1],
+            rest,
+            rest_at(l),
+            units,
+            pack_qkv(l + 1),
         )
         stored.append(
             (stream, low_one, pieces, kv_back, out, log_total, mixed_full, middle, low_two, hidden, act)
         )
-        stream, low_one, pieces, kv_back = later
+        stream, low_one, full_qkv, pieces, kv_back = later
+        qkv_of.append(full_qkv)
 
     l = LAYERS - 1
     mixed, out, log_total = attend(sc, docs, pieces, kv_back)
@@ -1590,9 +1763,9 @@
         stream,
         grad,
         [row(vector) for vector in (b_out[l], ln2_gain[l], ln2_bias[l], b_fc[l])],
-        rest_of[l],
-        fc_at,
-        proj_at,
+        rest,
+        rest_at(l),
+        units,
     )
     other_two = swap_tp(part_two)
     outputs = (middle + (part_two.astype(F32) + other_two.astype(F32)) + b_proj[l][None]).astype(BF16)
@@ -1605,7 +1778,6 @@
     sums_one = [sum_bout, sum_gain_two, sum_bias_two, sum_bfc, sum_bproj]
     low_one_kept, low_out_kept, mixed_kept = low_one, low_out, mixed_full
     (stream_below, low_one, pieces, kv_back, out, log_total, mixed_full, middle, low_two, hidden, act) = stored[0]
-    weights, first = qkv_of[1]
     (
         grad_qkv,
         sum_bqkv,
@@ -1621,90 +1793,68 @@
         sum_bias_two,
         sum_bout,
         grad_mixed,
-        *feed_totals,
+        *later,
     ) = pull_both_segment(
         pulls,
         row(ln1_gain[1]),
         row(ln2_gain[0]),
-        weights,
-        first,
-        rest_of[0],
-        fc_at,
-        proj_at,
+        qkv_of[1],
+        rest,
+        rest_at(0),
+        units,
         grad,
         stream,
         hidden,
         middle,
         [stay0, met0, stay1, go1],
-    )
-    stay0, go0, stay1, go1 = weight_pull(5, low_one_kept, grad_qkv, low_out_kept, mixed_kept)
-    met0, met1 = swap_fsdp(go0, 2), swap_fsdp(go1, 2)
-
-    def join_small(sums):
-        return butterfly(jnp.concatenate([jnp.sum(value, 0) for value in sums]))
-
-    small_one = join_small([sum_gain_one, sum_bias_one, sum_bqkv] + sums_one)
-    grad_mixed, stay0 = tie(grad_mixed, stay0)
+        [low_two, act],
+    )
+    feed_totals, near, far, (stay0, go0) = later[:2], later[2], later[3:-2], later[-2:]
+    came = []
+    for onward, value in enumerate(far, 1):
+        size = lax.axis_size("fsdp")
+        pairs = [(i, (i + GROUP * onward) % size) for i in range(size)]
+        came.append(lax.ppermute(value, "fsdp", pairs))
+    met0 = swap_fsdp(go0, 2)
+    sums_one = [sum_gain_one, sum_bias_one, sum_bqkv] + sums_one
     pulls = attend_pull(sc, docs, pieces, grad_mixed, kv_back, out, log_total)
-    *pulls, met0, met1 = tie(*pulls, met0, met1)
+    *pulls, came, met0 = tie(*pulls, came, met0)
     sums_zero = [sum_bout, sum_gain_two, sum_bias_two, sum_bfc, sum_bproj]
-    weights, first = qkv_of[0]
-    grad_qkv, sum_bqkv, sum_gain_one, sum_bias_one, grad, *totals = pull_last_segment(
+    grad, small, proj0, qkv1, out1, qkv0, out0 = pull_last_segment(
         pulls,
         row(ln1_gain[0]),
-        weights,
-        first,
+        qkv_of[0],
         grad,
         stream_below,
-        [low_two, grad_hidden, low_proj, act, low_one, low_out, mixed_full],
-        [stay0, met0, stay1, met1],
-    )
-    small_zero = join_small([sum_gain_one, sum_bias_one, sum_bqkv] + sums_zero)
-    small = [small_zero, small_one]
-    large = [totals[2:], feed_totals + totals[:2]]
-
-    def small_parts(vector):
-        ends, at = [], 0
-        for size in (width, width, 3 * out_cols, width, width, width, units, width):
-            ends.append(vector[at : at + size])
-            at += size
-        three = ends[2].reshape(GROUP, 3, cols).transpose(1, 0, 2).reshape(3, out_cols)
-        ends[2] = three[0::2]
-        return ends
-
-    small = [small_parts(vector) for vector in small]
-
-    def stack_small(member):
-        return jnp.stack([small[l][member] for l in range(LAYERS)])
-
+        [low_one_kept, grad_qkv, low_out_kept, mixed_kept, low_one, low_out, mixed_full],
+        [stay0, met0],
+        sums_one + sums_zero,
+    )
+    gain1, bias1, bqv, bout, gain2, bias2, bfc, bproj, grad_wfc, grad_wproj, grad_wout = finish(
+        small, [*feed_totals, out1, proj0, out0], near, came, out_cols, units
+    )
     grad_wqkv = jnp.stack(
         [
-            large[l][2]
-            .reshape(depth, GROUP, 3, cols)
-            .transpose(0, 2, 1, 3)
-            .reshape(depth, 3, out_cols)
-            for l in range(LAYERS)
+            value.reshape(depth, GROUP, 3, cols).transpose(0, 2, 1, 3).reshape(depth, 3, out_cols)
+            for value in (qkv0, qkv1)
         ]
     )
-    grad_wout = jnp.stack([large[l][3].T for l in range(LAYERS)])
-    grad_wfc = jnp.stack([large[l][0] for l in range(LAYERS)])
-    grad_wproj = jnp.stack([large[l][1].T for l in range(LAYERS)])
 
     return (
         outputs,
         grad,
-        stack_small(0),
-        stack_small(1),
+        gain1,
+        bias1,
         grad_wqkv,
-        stack_small(2),
+        bqv,
         grad_wout,
-        stack_small(3),
-        stack_small(4),
-        stack_small(5),
+        bout,
+        gain2,
+        bias2,
         grad_wfc,
-        stack_small(6),
+        bfc,
         grad_wproj,
-        stack_small(7),
+        bproj,
     )
 
 

time: 703 us -> 634 us (0.902); the launches traced: 701 us -> 624 us
  waiting for transfers between devices: 92.5 us -> 16.4 us
  Pallas kernels: 515 us -> 552 us
  starting transfers between devices: 38.8 us -> 10.2 us
  other arithmetic: 27.6 us -> 8.35 us
  local copies, waits for them, and re-layouts: 11.6 us -> 22.3 us
    all_gather x3 -> x1, waiting for transfers between devices: 83.4 us -> 14.7 us  [gather(): return lax.all_gather(shard, 'fsdp', axis=0, tiled=True)]
    ppermute x15 -> x2, starting transfers between devices: 38.2 us -> 2.3 us  [swap_fsdp(): lax.ppermute(value, 'fsdp', [(i, i ^ s) for i in range(lax.axis_size('fsd...]
    pallas_call x6 -> x5, Pallas kernels: 450 us -> 474 us  [run_links(): pl.pallas_call(body, in_specs=[spec for spec, _ in ins], out_specs=[spec...]
    another operation x13 -> x1, other arithmetic: 10.9 us -> 0.93 us  [shards(): jnp.stack([value.reshape(depth, GROUP, 3, cols).transpose(0, 2, 1, 3).res...]
    unnamed x71 -> x48, local copies, waits for them, and re-layouts: 3.37 us -> 13.3 us
    reduce_sum x17 -> x0, other arithmetic: 8.94 us -> none  [the longest x16 8.83 us: join_small(): return butterfly(jnp.concatenate([jnp.sum(value, 0) for value in sums]))]
    pallas_call x4, Pallas kernels: 66 us -> 74.1 us  [run_kernel(): pl.pallas_call(body, grid_spec=pltpu.PrefetchScalarGridSpec(num_scalar_pr...]
    ppermute x15 -> x2, waiting for transfers between devices: 8.98 us -> 1.72 us  [swap_fsdp(): lax.ppermute(value, 'fsdp', [(i, i ^ s) for i in range(lax.axis_size('fsd...]
  transfers between devices with their start and end apart: 19 -> 7, of which waited for: 11 -> 2; matrix products, arithmetic and copies ran while one was open for 4% -> 2% of each run, Pallas kernels for 46% -> 43%
where the time goes in v4:
time: 634 us; the launch traced here: 624 us
  Pallas kernels  552 us (87%)
  local copies, waits for them, and re-layouts  22.3 us (4%)
  waiting for transfers between devices  16.4 us (3%)
  between operations  14.8 us (2%)
  starting transfers between devices  10.2 us (2%)
  other arithmetic  8.35 us (1%)
    pallas_call x5, Pallas kernels, run_links(): pl.pallas_call(body, in_specs=[spec for spec, _ in ins], out_specs=[spec...  474 us
    pallas_call x4, Pallas kernels, run_kernel(): pl.pallas_call(body, grid_spec=pltpu.PrefetchScalarGridSpec(num_scalar_pr...  74.1 us
    all_gather x1, waiting for transfers between devices, gather(): return lax.all_gather(shard, 'fsdp', axis=0, tiled=True)  14.7 us
    unnamed x48, local copies, waits for them, and re-layouts  13.3 us
  transfers between devices with their start and end apart: 7, of which 2 were waited for; matrix products, arithmetic and copies ran while one was open for 2% of the time, Pallas kernels for 43%

profile of v4, /device:TPU:0, one launch (start us, length us, event | category | flops | bytes accessed | tf_op | source)
XLA Modules:
  0.0 624.3 jit_solution(5028400915334100615)
XLA Ops:
  10.9 1.0 bitcast_dynamic-update-slice_fusion.2
  12.9 1.0 copy-done.1
  18.2 94.9 %shard_map.263 = (f32[512,1024]{1,0:T(8,128)}, bf16[512,1024]{1,0:T(8,128)(2,1)}, bf16[1024,1536]{1,0:T(8,128)(2,1)}, f32[8,128]{1,0:T(8,128)}, f32[8,128]{1,0:T...) custom-call(bf16[512,1024]{1,0:T(8,128)(2,1)} %base.1, f32[1,1024]{1,0:T(1,128)} %get-tuple-element.282.gain, ...), custom_call_target="tpu_custom_call" | custom-call | flops 1610612736 | bytes 7340032 | tf_op jit(solution)/shard_map/pallas_call | solution.py:396
  115.6 15.7 %shard_map.264 = (bf16[2048,128]{1,0:T(8,128)(2,1)}, f32[2048,128]{1,0:T(8,128)}, f32[8,2048]{1,0:T(8,128)}) custom-call(s32[10]{0:T(128)} %pad_add_fusion.sc, bf16[2048,384]{1,0:T(8,128)(2,1)} %bitcast.89, bf16[2048,256]{1,0:T(8,128)(2,1)} %bitcast.93), custom_call_target="tpu_custom_call" | custom-call | flops 2147483648 | bytes 5242880 | tf_op jit(solution)/shard_map/pallas_call | solution.py:48
  132.5 1.5 convert_multiply_fusion.grad_in
  134.6 14.7 %all-gather.2.cloned.1.call-done.rest = bf16[1024,9216]{1,0:T(8,128)(2,1)} async-done(((bf16[64,9216]{1,0:T(8,128)(2,1)}), bf16[1024,9216]{1,0:T(8,128)(2,1)}) %all-gather.2.cloned.1.call-update) | async-done | bytes 18874384 | tf_op jit(solution)/shard_map/all_gather | solution.py:1647
  149.3 89.2 %shard_map.265 = (bf16[512,512]{1,0:T(8,128)(2,1)}, f32[512,1024]{1,0:T(8,128)}, bf16[512,1024]{1,0:T(8,128)(2,1)}, f32[512,2048]{1,0:T(8,128)}, bf16[512,2048]{...) custom-call(bf16[4,512,128]{2,1,0:T(8,128)(2,1)} %bitcast.101, ...), custom_call_target="tpu_custom_call" | custom-call | flops 6442450944 | bytes 29360128 | tf_op jit(solution)/shard_map/pallas_call | solution.py:396
  238.5 15.4 %shard_map.266 = (bf16[2048,128]{1,0:T(8,128)(2,1)}, f32[2048,128]{1,0:T(8,128)}, f32[8,2048]{1,0:T(8,128)}) custom-call(s32[10]{0:T(128)} %pad_add_fusion.sc, bf16[2048,384]{1,0:T(8,128)(2,1)} %bitcast.91, bf16[2048,256]{1,0:T(8,128)(2,1)} %bitcast.97), custom_call_target="tpu_custom_call" | custom-call | flops 2147483648 | bytes 5242880 | tf_op jit(solution)/shard_map/pallas_call | solution.py:48
  253.9 66.8 %shard_map.267 = (bf16[512,512]{1,0:T(8,128)(2,1)}, f32[512,1024]{1,0:T(8,128)}, bf16[512,1024]{1,0:T(8,128)(2,1)}, bf16[512,2048]{1,0:T(8,128)(2,1)}, bf16[512,...) custom-call(bf16[4,512,128]{2,1,0:T(8,128)(2,1)} %bitcast.102, ...), custom_call_target="tpu_custom_call" | custom-call | flops 9663676416 | bytes 25165824 | tf_op jit(solution)/shard_map/pallas_call | solution.py:396
  320.7 1.6 collective-permute-start.1
  323.2 21.3 %shard_map.268 = (bf16[2048,128]{1,0:T(8,128)(2,1)}, bf16[2048,256]{1,0:T(8,128)(2,1)}, bf16[2048,256]{1,0:T(8,128)(2,1)}) custom-call(s32[10]{0:T(128)} %pad_add_fusion.sc, bf16[2048,384]{1,0:T(8,128)(2,1)} %bitcast.92, bf16[2048,128]{1,0:T(8,128)(2,1)} %bitcast.100, bf16[2048,256]{1,0:T(8,128)(2,1)} %bitcast.98, f32[2048,128]{1,0:T(8,128)} %get-tuple-element.124.out, ...), custom_call_target="tpu_custom_call" | custom-call | flops 4831838208 | bytes 7864320 | tf_op jit(solution)/shard_map/pallas_call | solution.py:48
  344.5 1.7 collective-permute-done.1.met0_in
  347.2 112.2 %shard_map.269 = (bf16[512,1536]{1,0:T(8,128)(2,1)}, f32[8,1536]{1,0:T(8,128)}, f32[8,1024]{1,0:T(8,128)}, f32[8,1024]{1,0:T(8,128)}, bf16[512,1024]{1,0:T(8,128...) custom-call(bf16[4,512,128]{2,1,0:T(8,128)(2,1)} %bitcast.85, ...), custom_call_target="tpu_custom_call" | custom-call | flops 6442450944 | bytes 30408704 | tf_op jit(solution)/shard_map/pallas_call | solution.py:396
  460.0 3.1 collective-permute-start.2
  463.1 1.1 collective-permute-start.3
  464.2 2.9 collective-permute-start.4
  467.1 21.7 %shard_map.270 = (bf16[2048,128]{1,0:T(8,128)(2,1)}, bf16[2048,256]{1,0:T(8,128)(2,1)}, bf16[2048,256]{1,0:T(8,128)(2,1)}) custom-call(s32[10]{0:T(128)} %pad_add_fusion.sc, bf16[2048,384]{1,0:T(8,128)(2,1)} %bitcast.90, bf16[2048,128]{1,0:T(8,128)(2,1)} %bitcast.88, bf16[2048,256]{1,0:T(8,128)(2,1)} %bitcast.94, f32[2048,128]{1,0:T(8,128)} %get-tuple-element.144.out, ...), custom_call_target="tpu_custom_call" | custom-call | flops 4831838208 | bytes 7864320 | tf_op jit(solution)/shard_map/pallas_call | solution.py:48
  488.8 3.4 add_convert_fusion
  492.2 110.7 %shard_map.271 = (f32[512,1024]{1,0:T(8,128)}, f32[24,1024]{1,0:T(8,128)}, f32[64,2048]{1,0:T(8,128)}, f32[64,1536]{1,0:T(8,128)}, f32[64,512]{1,0:T(8,128)}, /*index=5*/f32[64,1536]{1,0:T(8,128)}, f32[64,512]{1,0:T(8,128)}) custom-call(bf16[4,512,128]{2,1,0:T(8,128)(2,1)} %bitcast.99, bf16[4,512,256]{2,1,0:T(8,128)(2,1)} %bitcast.95, ...), custom_call_target="tpu_custom_call" | custom-call | flops 5905580032 | bytes 15728640 | tf_op jit(solution)/shard_map/pallas_call | solution.py:396
  603.0 1.3 reshape.137
  605.1 4.4 shard_map.272
  609.6 1.9 copy.66
  611.5 3.3 copy.67
  615.7 1.3 copy.78
  (82 shorter events, 17.4 us)
Async XLA Ops:
  7.2 6.8 %copy-start.6 = (bf16[2,64,3,512]{3,1,2,0:T(8,128)(2,1)S(1)}, bf16[2,64,3,512]{3,1,2,0:T(8,128)(2,1)}, u32[]{:S(2)}) copy-start(bf16[2,64,3,512]{3,1,2,0:T(8,128)(2,1)} %param.22) | copy-start | bytes 1179652
  7.2 142.1 %all-gather.2.cloned.1.call-start = ((), (), s32[]{:S(2)}) async-start(), calls=%async_computation | async-start | bytes 20054016 | tf_op jit(solution)/shard_map/all_gather | solution.py:1647
  10.9 4.2 copy-start.11
  12.9 4.7 copy-start.12
  12.9 4.7 copy-start.13
  18.2 97.0 %copy-start.19 = (s32[8]{0:T(128)S(1)}, s32[8]{0:T(128)}, u32[]{:S(2)}) copy-start(s32[8]{0:T(128)} %param.19) | copy-start | bytes 100
  18.2 97.3 %copy-start.18 = (s32[512]{0:T(512)S(1)}, s32[512]{0:T(512)}, u32[]{:S(2)}) copy-start(s32[512]{0:T(512)} %param.18) | copy-start | bytes 6148
  115.5 15.7 %copy-start.14 = (f32[2,1024]{1,0:T(2,128)S(1)}, f32[2,1024]{1,0:T(2,128)}, u32[]{:S(2)}) copy-start(f32[2,1024]{1,0:T(2,128)} %param.26) | copy-start | bytes 24580
  115.5 15.8 %copy-start.15 = (f32[2,1024]{1,0:T(2,128)S(1)}, f32[2,1024]{1,0:T(2,128)}, u32[]{:S(2)}) copy-start(f32[2,1024]{1,0:T(2,128)} %param.25) | copy-start | bytes 24580
  115.5 16.4 %copy-start.16 = (f32[2,1024]{1,0:T(2,128)S(1)}, f32[2,1024]{1,0:T(2,128)}, u32[]{:S(2)}) copy-start(f32[2,1024]{1,0:T(2,128)} %param.31) | copy-start | bytes 24580
  115.5 16.4 %copy-start.17 = (f32[2,1024]{1,0:T(2,128)S(1)}, f32[2,1024]{1,0:T(2,128)}, u32[]{:S(2)}) copy-start(f32[2,1024]{1,0:T(2,128)} %param.27) | copy-start | bytes 24580
  115.5 17.0 %copy-start.3 = (bf16[512,1024]{1,0:T(8,128)(2,1)S(1)}, bf16[512,1024]{1,0:T(8,128)(2,1)}, u32[]{:S(2)}) copy-start(bf16[512,1024]{1,0:T(8,128)(2,1)} %param.17) | copy-start | bytes 3145732
  131.2 2.8 copy-start.10
  320.7 25.5 %collective-permute-start.1 = (bf16[256,2048]{1,0:T(8,128)(2,1)}, bf16[256,2048]{1,0:T(8,128)(2,1)S(1)}, u32[]{:S(2)}, u32[]{:S(2)}) collective-permute-start(bf16[256,2048]{1,0:T(8,128)(2,1)} %get-tuple-element.129), channel_id=1, source_target_pairs={{0,4},{2,6},{4,0},{6,2},{8,12},{10,14},{12,8},{14,10},{16,20},{18,... | collective-permute-start | bytes 3145736 | tf_op jit(solution)/shard_map/ppermute | solution.py:1638
  322.4 166.4 %collective-permute-start = (bf16[512,1024]{1,0:T(8,128)(2,1)}, bf16[512,1024]{1,0:T(8,128)(2,1)}, u32[]{:S(2)}, u32[]{:S(2)}) collective-permute-start(bf16[512,1024]{1,0:T(8,128)(2,1)} %get-tuple-element.120), channel_id=1, source_target_pairs={{0,1},{1,0},{2,3},{3,2},{4,5},{5,4},{6,7},{7,6},{8,9},{9,8},{10,11... | collective-permute-start | bytes 3145736 | tf_op jit(solution)/shard_map/ppermute | solution.py:1634
  459.4 32.8 %collective-permute-start.5 = (bf16[256,2048]{1,0:T(8,128)(2,1)}, bf16[256,2048]{1,0:T(8,128)(2,1)}, u32[]{:S(2)}, u32[]{:S(2)}) collective-permute-start(bf16[256,2048]{1,0:T(8,128)(2,1)} %get-tuple-element.152), channel_id=1, source_target_pairs={{0,4},{2,6},{4,0},{6,2},{8,12},{10,14},{12,8},{14,10},{16,20},{18,... | collective-permute-start | bytes 3145736 | tf_op jit(solution)/shard_map/ppermute | solution.py:1638
  460.0 32.1 %collective-permute-start.2 = (bf16[64,2048]{1,0:T(8,128)(2,1)}, bf16[64,2048]{1,0:T(8,128)(2,1)S(1)}, u32[]{:S(2)}, u32[]{:S(2)}) collective-permute-start(bf16[64,2048]{1,0:T(8,128)(2,1)} %get-tuple-element.149), channel_id=1, source_target_pairs={{0,8},{2,10},{4,12},{6,14},{8,16},{10,18},{12,20},{14,22},{16,24},... | collective-permute-start | bytes 786440 | tf_op jit(solution)/shard_map/ppermute | solution.py:1817
  463.1 29.0 %collective-permute-start.3 = (bf16[64,2048]{1,0:T(8,128)(2,1)}, bf16[64,2048]{1,0:T(8,128)(2,1)S(1)}, u32[]{:S(2)}, u32[]{:S(2)}) collective-permute-start(bf16[64,2048]{1,0:T(8,128)(2,1)} %get-tuple-element.150), channel_id=1, source_target_pairs={{0,16},{2,18},{4,20},{6,22},{8,24},{10,26},{12,28},{14,30},{16,0},... | collective-permute-start | bytes 786440 | tf_op jit(solution)/shard_map/ppermute | solution.py:1817
  464.2 28.0 %collective-permute-start.4 = (bf16[64,2048]{1,0:T(8,128)(2,1)}, bf16[64,2048]{1,0:T(8,128)(2,1)S(1)}, u32[]{:S(2)}, u32[]{:S(2)}) collective-permute-start(bf16[64,2048]{1,0:T(8,128)(2,1)} %get-tuple-element.151), channel_id=1, source_target_pairs={{0,24},{2,26},{4,28},{6,30},{8,0},{10,2},{12,4},{14,6},{16,8},{18,... | collective-permute-start | bytes 786440 | tf_op jit(solution)/shard_map/ppermute | solution.py:1817
  467.1 21.7 %copy-start.4 = (bf16[512,1024]{1,0:T(8,128)(2,1)S(1)}, bf16[512,1024]{1,0:T(8,128)(2,1)}, u32[]{:S(2)}) copy-start(bf16[512,1024]{1,0:T(8,128)(2,1)} %get-tuple-element.120) | copy-start | bytes 3145732
  492.1 110.8 %copy-start.7 = (bf16[64,2048]{1,0:T(8,128)(2,1)}, bf16[64,2048]{1,0:T(8,128)(2,1)S(1)}, u32[]{:S(2)}) copy-start(bf16[64,2048]{1,0:T(8,128)(2,1)S(1)} %collective-permute-done.2.refs_0_) | copy-start | bytes 786436
  492.2 110.8 %copy-start.8 = (bf16[64,2048]{1,0:T(8,128)(2,1)}, bf16[64,2048]{1,0:T(8,128)(2,1)S(1)}, u32[]{:S(2)}) copy-start(bf16[64,2048]{1,0:T(8,128)(2,1)S(1)} %collective-permute-done.3.refs_1_) | copy-start | bytes 786436
  492.2 110.8 %copy-start.9 = (bf16[64,2048]{1,0:T(8,128)(2,1)}, bf16[64,2048]{1,0:T(8,128)(2,1)S(1)}, u32[]{:S(2)}) copy-start(bf16[64,2048]{1,0:T(8,128)(2,1)S(1)} %collective-permute-done.4.refs_2_) | copy-start | bytes 786436
  611.5 4.2 copy-start
  (3 other events, 3.6 us)
Sparse Core Ops, SparseCore 0:
  14.1 135.2 all-gather.1

commit v5 on v4

--- a/solution.py
+++ b/solution.py
@@ -110,7 +110,8 @@
     return value
 
 
-ROWS = 256
+CHUNK = [256]
+SIZES = (256, 128, 256, 128, 256)
 MESH = pl.DeviceIdType.MESH
 
 
@@ -168,7 +169,7 @@
         body(pl.ds(pl.multiple_of(first + at * LN_ROWS, LN_ROWS), LN_ROWS))
         return carry
 
-    lax.fori_loop(0, ROWS // LN_ROWS, step, 0)
+    lax.fori_loop(0, CHUNK[0] // LN_ROWS, step, 0)
 
 
 def out_rows(rows, mixed, w, target):
@@ -209,9 +210,9 @@
     cols = bq.shape[1] // GROUP
     copies = []
     order = (2, 3, 1, 0)
-    chunks = low.shape[0] // ROWS
+    chunks = low.shape[0] // CHUNK[0]
     for c in range(chunks):
-        rows = pl.ds(c * ROWS, ROWS)
+        rows = pl.ds(c * CHUNK[0], CHUNK[0])
         across = {
             s: links.copy(ready.at[s, rows], pieces.at[links.place, rows], links.peer(s)) for s in order if s
         }
@@ -228,7 +229,7 @@
     last = links.group == links.groups - 1
 
     def start(c):
-        rows = pl.ds(c * ROWS, ROWS)
+        rows = pl.ds(c * CHUNK[0], CHUNK[0])
         across, onward, own = copies[c]
         for s in order:
             at = columns(links.place ^ s, cols)
@@ -261,7 +262,7 @@
 
 
 def qkv_copies(rows):
-    return rows // ROWS * (2 * GROUP - 1)
+    return rows // CHUNK[0] * (2 * GROUP - 1)
 
 
 class ShardGather:
@@ -365,9 +366,9 @@
     )
     gathered.start()
     counted.near[0].start()
-    chunks = base.shape[0] // ROWS
+    chunks = base.shape[0] // CHUNK[0]
     for c in range(chunks):
-        norm_rows(c * ROWS, base, None, gain, bias, stream, low)
+        norm_rows(c * CHUNK[0], base, None, gain, bias, stream, low)
     counted.step(0)
     counted.near[1].start()
     gathered.pass_x()
@@ -407,6 +408,7 @@
 
 
 def first_segment(base, gain, bias, shard, bq, segments, docs):
+    CHUNK[0] = SIZES[0]
     rows, width = base.shape
     total = bq.shape[1]
     cols = total // GROUP
@@ -433,7 +435,7 @@
             pltpu.VMEM((groups - 1, docs, 128), F32),
             copies,
             copies,
-            pltpu.SemaphoreType.DMA((rows // ROWS,)),
+            pltpu.SemaphoreType.DMA((rows // CHUNK[0],)),
         ],
         flops=2 * rows * width * total,
         moved=rows * width * 8 + width * total * 2,
@@ -443,8 +445,8 @@
 def trade_mixed(links, mixed_all, mixed):
     cols = mixed_all.shape[2]
     copies = []
-    for c in range(mixed.shape[0] // ROWS):
-        rows = pl.ds(c * ROWS, ROWS)
+    for c in range(mixed.shape[0] // CHUNK[0]):
+        rows = pl.ds(c * CHUNK[0], CHUNK[0])
         copies.append(
             [
                 links.copy(
@@ -497,7 +499,7 @@
         + group_greets(links)
     )
     gathered = ShardGather(links, shard, w_qkv)
-    chunks = [pl.ds(c * ROWS, ROWS) for c in range(base.shape[0] // ROWS)]
+    chunks = [pl.ds(c * CHUNK[0], CHUNK[0]) for c in range(base.shape[0] // CHUNK[0])]
     start_mixed, wait_mixed, finish_mixed = trade_mixed(links, mixed_all, mixed)
     swaps = [links.swap(part.at[rows], got.at[rows]) for rows in chunks]
     swaps_two = [links.swap(part_two.at[rows], got_two.at[rows]) for rows in chunks]
@@ -513,14 +515,17 @@
     loads[2].wait()
     for c, rows in enumerate(chunks):
         swaps[c].wait()
-        norm_rows(c * ROWS, base, (part, got, bout), gain_two, bias_two, middle, low_two)
+        norm_rows(c * CHUNK[0], base, (part, got, bout), gain_two, bias_two, middle, low_two)
         feed_rows(rows, low_two, w_fc, bfc, hidden, act, w_proj, part_two)
         swaps_two[c].start()
-        (gathered.pass_core if c else gathered.pass_x)()
+        if c == 0:
+            gathered.pass_x()
+        if c == 1:
+            gathered.pass_core()
     gathered.arrive()
     for c, rows in enumerate(chunks):
         swaps_two[c].wait()
-        norm_rows(c * ROWS, middle, (part_two, got_two, bproj), gain, bias, stream, low)
+        norm_rows(c * CHUNK[0], middle, (part_two, got_two, bproj), gain, bias, stream, low)
         start_qkv(c)
     finish_mixed()
     gathered.finish()
@@ -528,11 +533,12 @@
 
 
 def between_segment(mixed_all, base, vectors, bq, rest, at, units, shard):
+    CHUNK[0] = SIZES[1]
     rows, width = base.shape
     total = bq.shape[1]
     cols = total // GROUP
     out_cols = at[1] - at[0]
-    chunks = rows // ROWS
+    chunks = rows // CHUNK[0]
     copies = pltpu.SemaphoreType.DMA((qkv_copies(rows) + chunks * (GROUP - 1) + 2 * chunks + gather_copies(),))
     whole_f32 = (VMEM, shape((rows, width), F32))
     whole_low = (VMEM, shape((rows, width), BF16))
@@ -574,7 +580,7 @@
 
 def pull_qkv_rows(first, back, links, full, back_got, w, target, sums):
     cols = full.shape[1] // GROUP
-    rows = pl.ds(first, ROWS)
+    rows = pl.ds(first, CHUNK[0])
 
     @pl.when(links.group < links.groups - 1)
     def _():
@@ -598,8 +604,8 @@
 def trade_pulls(links, grad_q, grad_kv, grad_kv_back, full, back_got):
     part = grad_q.shape[2]
     copies = []
-    for c in range(full.shape[0] // ROWS):
-        rows = pl.ds(c * ROWS, ROWS)
+    for c in range(full.shape[0] // CHUNK[0]):
+        rows = pl.ds(c * CHUNK[0], CHUNK[0])
         across, back = [], []
         for s in (2, 3, 1):
             for source, start, size in ((grad_kv, part, 2 * part), (grad_q, 0, part)):
@@ -655,7 +661,7 @@
 
 
 def pull_copies(rows):
-    return rows // ROWS * (2 * (GROUP - 1) + GROUP)
+    return rows // CHUNK[0] * (2 * (GROUP - 1) + GROUP)
 
 
 def pull_norm_rows(first, grad, own, got, inputs, gain, grad_new, sums, low=None):
@@ -696,8 +702,8 @@
 def send_mixed_pull(links, low, w, ready, pieces, kept):
     cols = ready.shape[2]
     copies = []
-    for c in range(low.shape[0] // ROWS):
-        rows = pl.ds(c * ROWS, ROWS)
+    for c in range(low.shape[0] // CHUNK[0]):
+        rows = pl.ds(c * CHUNK[0], CHUNK[0])
         across = {
             s: links.copy(ready.at[s, rows], pieces.at[links.place, rows], links.peer(s))
             for s in range(1, GROUP)
@@ -706,7 +712,7 @@
         copies.append((across, own))
 
     def start(c):
-        rows = pl.ds(c * ROWS, ROWS)
+        rows = pl.ds(c * CHUNK[0], CHUNK[0])
         across, own = copies[c]
         for s in (2, 3, 1, 0):
             at = columns(links.place ^ s, cols)
@@ -753,7 +759,7 @@
         load,
     )
     links.greet([links.peer(s) for s in range(1, GROUP)] + [{"tp": links.other}])
-    chunks = [pl.ds(c * ROWS, ROWS) for c in range(base.shape[0] // ROWS)]
+    chunks = [pl.ds(c * CHUNK[0], CHUNK[0]) for c in range(base.shape[0] // CHUNK[0])]
     start_mixed, wait_mixed, finish_mixed = trade_mixed(links, mixed_all, mixed)
     swaps = [links.swap(part.at[rows], got.at[rows]) for rows in chunks]
     swaps_three = [links.swap(part_three.at[rows], got_three.at[rows]) for rows in chunks]
@@ -773,10 +779,10 @@
     for one in loads[1:]:
         one.wait()
     for c in range(len(chunks)):
-        round_rows(c * ROWS, grad, low_proj, sum_proj)
+        round_rows(c * CHUNK[0], grad, low_proj, sum_proj)
     for c, rows in enumerate(chunks):
         swaps[c].wait()
-        norm_rows(c * ROWS, base, (part, got, bout), gain_two, bias_two, middle, low_two)
+        norm_rows(c * CHUNK[0], base, (part, got, bout), gain_two, bias_two, middle, low_two)
 
         def tile(at):
             value = dot(low_two[rows, :], w_fc[:, at]) + bfc[:, at]
@@ -799,7 +805,7 @@
     for c, rows in enumerate(chunks):
         swaps_three[c].wait()
         pull_norm_rows(
-            c * ROWS, grad, part_three, got_three, middle, gain_two, grad_new, (sum_gain, sum_bias, sum_out), low_out
+            c * CHUNK[0], grad, part_three, got_three, middle, gain_two, grad_new, (sum_gain, sum_bias, sum_out), low_out
         )
         start_pull(c)
     for one in core_sums:
@@ -809,10 +815,11 @@
 
 
 def turn_segment(mixed_all, base, grad, vectors, rest, at, units):
+    CHUNK[0] = SIZES[2]
     rows, width = base.shape
     out_cols = at[1] - at[0]
     cols = out_cols // GROUP
-    chunks = rows // ROWS
+    chunks = rows // CHUNK[0]
     copies = pltpu.SemaphoreType.DMA((2 * chunks * (GROUP - 1) + 2 * chunks + 2,))
     high = (VMEM, shape((rows, width), F32))
     low = (VMEM, shape((rows, width), BF16))
@@ -885,7 +892,7 @@
             (grad_in, None, grad),
             (stream_in, None, stream),
             (rest, proj_at, w_proj),
-            (hidden_in.at[pl.ds(0, ROWS)], None, hidden),
+            (hidden_in.at[pl.ds(0, CHUNK[0])], None, hidden),
             (rest, fc_at, w_fc),
             (rest, out_at, w_out),
             (stay0_in, None, stay0),
@@ -905,7 +912,7 @@
         + [{"tp": links.other}]
         + group_greets(links)
     )
-    chunks = [pl.ds(c * ROWS, ROWS) for c in range(grad.shape[0] // ROWS)]
+    chunks = [pl.ds(c * CHUNK[0], CHUNK[0]) for c in range(grad.shape[0] // CHUNK[0])]
     start_pulls, wait_pulls, finish_pulls = trade_pulls(
         links, grad_q, grad_kv, grad_kv_back, full, back_got
     )
@@ -923,66 +930,68 @@
     )
     feed_x = links.copy(go2, met2, links.peer(2))
     start_pulls()
-    late_x.start()
     for total in (sum_qkv, sum_gain_one, sum_bias_one, sum_proj, sum_fc, sum_gain, sum_bias, sum_out):
         total[...] = jnp.zeros_like(total)
     for one in loads:
         one.wait()
-    group_sums[0].add()
-    group_sums[0].start()
     for c, rows in enumerate(chunks):
         wait_pulls(c)
-        pull_qkv_rows(c * ROWS, None, links, full, back_got, w_qkv, part, sum_qkv)
+        if c == len(chunks) // 2:
+            late_x.start()
+            group_sums[0].send(0)
+        pull_qkv_rows(c * CHUNK[0], None, links, full, back_got, w_qkv, part, sum_qkv)
         swaps[c].start()
     for c, rows in enumerate(chunks):
         swaps[c].wait()
         pull_norm_rows(
-            c * ROWS, grad, part, got, stream, gain, grad_new, (sum_gain_one, sum_bias_one)
+            c * CHUNK[0], grad, part, got, stream, gain, grad_new, (sum_gain_one, sum_bias_one)
         )
         if c == len(chunks) - 1:
             load_middle.start()
-        round_rows(c * ROWS, grad_new, low_proj, sum_proj)
+        round_rows(c * CHUNK[0], grad_new, low_proj, sum_proj)
         if c:
             load_hidden.wait()
         pull_feed_rows(
-            rows, low_proj, w_proj, hidden, pl.ds(0, ROWS), grad_hidden, sum_fc, w_fc, part_two
+            rows, low_proj, w_proj, hidden, pl.ds(0, CHUNK[0]), grad_hidden, sum_fc, w_fc, part_two
         )
         swaps_two[c].start()
         if c + 1 < len(chunks):
             load_hidden = pltpu.make_async_copy(
-                hidden_in.at[pl.ds((c + 1) * ROWS, ROWS)], hidden, load.at[len(loads) + 1 + c]
+                hidden_in.at[pl.ds((c + 1) * CHUNK[0], CHUNK[0])], hidden, load.at[len(loads) + 1 + c]
             )
             load_hidden.start()
     core_sums[0].multiply(left, grad_hidden, plain, flipped)
     load_middle.wait()
-    late_x.wait()
-    group_sums[1].add()
-    group_sums[1].start()
     for c, rows in enumerate(chunks):
         swaps_two[c].wait()
         pull_norm_rows(
-            c * ROWS, grad_new, part_two, got_two, middle, gain_two, grad_new, (sum_gain, sum_bias, sum_out), low_out
+            c * CHUNK[0], grad_new, part_two, got_two, middle, gain_two, grad_new, (sum_gain, sum_bias, sum_out), low_out
         )
         start_pull(c)
         if c == 0:
             core_sums[0].add()
             feed_x.start()
+            late_x.wait()
+            group_sums[1].send(0)
+            group_sums[0].pass_on(0)
             core_sums[1].multiply(low_proj, wide, plain, flipped)
+    group_sums[1].pass_on(0)
     core_sums[1].add()
     feed_x.wait()
     add_slots(stay2, met2, (near2, *far2))
     finish_pulls()
     finish_pull()
     for one in group_sums:
-        one.finish()
+        one.finish(2)
 
 
 def pull_both_segment(pulls, gain, gain_two, qkv, rest, at, units, grad, stream, hidden, middle, sums_in, factors):
+    CHUNK[0] = SIZES[3]
     rows, width = grad.shape
     out_cols = at[1] - at[0]
     cols = out_cols // GROUP
     total = 3 * out_cols
-    chunks = rows // ROWS
+    chunks = rows // CHUNK[0]
     groups = lax.axis_size("fsdp") // GROUP
     stay = sums_in[0]
     copies = pltpu.SemaphoreType.DMA((pull_copies(rows) + chunks * (GROUP - 1) + 2 * chunks + 2 * groups + 2,))
@@ -1023,7 +1032,7 @@
             pltpu.VMEM((width, units), BF16),
             pltpu.VMEM((rows, width), F32),
             pltpu.VMEM((rows, width), F32),
-            pltpu.VMEM((ROWS, units), F32),
+            pltpu.VMEM((CHUNK[0], units), F32),
             pltpu.VMEM((GROUP, rows, 2 * cols), BF16),
         ]
         + [pltpu.VMEM((rows, width), BF16)] * 4
@@ -1070,8 +1079,53 @@
             at += 1
 
 
-def finish_body(small, fc1, proj1, out1, proj0, out0, near, *refs):
-    *came, gain1, bias1, bqv, bout, gain2, bias2, bfc, bproj, wfc, wproj, wout = refs
+def pack_body(wqkv, bqv, wout, wfc, wproj, rest, qkv0, qkv1, bq0, bq1):
+    cols = bqv.shape[2] // GROUP
+    at = 0
+    for l in range(LAYERS):
+        for part in (wout, wfc, wproj):
+            size = part.shape[2]
+            rest[:, at : at + size] = part[l]
+            at += size
+    for l, (qkv, bq) in enumerate(((qkv0, bq0), (qkv1, bq1))):
+        bq[...] = jnp.zeros_like(bq)
+        for place in range(GROUP):
+            here = slice(place * cols, (place + 1) * cols)
+            for c in range(3):
+                where = (3 * place + c) * cols
+                qkv[:, where : where + cols] = wqkv[l, c, :, here]
+                if c != 1:
+                    bq[:, where : where + cols] = bqv[l, c // 2 : c // 2 + 1, here]
+
+
+def pack(w_qkv, b_qv, w_out, w_fc, w_proj):
+    depth, out_cols, units = w_fc.shape[1], w_out.shape[1], w_fc.shape[2]
+    rest = LAYERS * (out_cols + 2 * units)
+    outs = [shape((depth, rest), BF16)] + [shape((depth, 3 * out_cols), BF16)] * 2
+    outs += [shape((1, 3 * out_cols), F32)] * 2
+    return pl.pallas_call(
+        pack_body,
+        in_specs=[VMEM] * 5,
+        out_specs=[VMEM] * 5,
+        out_shape=outs,
+        compiler_params=pltpu.CompilerParams(vmem_limit_bytes=VMEM_BYTES),
+    )(
+        w_qkv.transpose(0, 2, 1, 3),
+        b_qv,
+        w_out.transpose(0, 2, 1),
+        w_fc,
+        w_proj.transpose(0, 2, 1),
+    )
+
+
+def finish_body(small, fc1, proj1, qkv1, out1, proj0, qkv0, out0, near, *refs):
+    *came, grad_in, middle, own, other, bproj_in, outputs, grad, gain1, bias1, bqv, bout, gain2, bias2, bfc, bproj, wfc, wproj, wout, wqkv = refs
+    def rows(at):
+        grad[at, :] = grad_in[at, :]
+        total = own[at, :].astype(F32) + other[at, :].astype(F32)
+        outputs[at, :] = (middle[at, :] + total + bproj_in[...]).astype(BF16)
+
+    each_rows(grad.shape[0], LN_ROWS, rows)
     fc0 = near[...]
     for one in came:
         fc0 = fc0 + one[...].astype(F32)
@@ -1079,7 +1133,7 @@
     cols = bqv.shape[2] // GROUP
     wfc[0] = fc0
     wfc[1] = fc1[...]
-    for l, proj, out in ((0, proj0, out0), (1, proj1, out1)):
+    for l, proj, qkv, out in ((0, proj0, qkv0, out0), (1, proj1, qkv1, out1)):
         at = l * (small.shape[0] // 2)
         for target, where in ((gain1, 0), (bias1, 1), (bout, 4), (gain2, 5), (bias2, 6), (bproj, 9)):
             target[l : l + 1, :] = small[at + where : at + where + 1, :]
@@ -1092,23 +1146,30 @@
                 bqv[l, i : i + 1, place * cols : (place + 1) * cols] = small[
                     line : line + 1, lane : lane + cols
                 ]
-        wproj[l] = proj[...].T
-        wout[l] = out[...].T
-
-
-def finish(small, totals, near, came, out_cols, units):
+        wproj[l] = proj[...]
+        wout[l] = out[...]
+        for place in range(GROUP):
+            for c in range(3):
+                at = (3 * place + c) * cols
+                wqkv[l, c, :, place * cols : (place + 1) * cols] = qkv[:, at : at + cols]
+
+
+def finish(small, totals, near, came, last, out_cols, units):
     depth, width = totals[0].shape[0], small.shape[1]
     vector = shape((LAYERS, width), F32)
-    outs = [vector, vector, shape((LAYERS, 2, out_cols), F32), vector, vector, vector]
+    grad = last[0].shape
+    outs = [shape(grad, BF16), shape(grad, F32)]
+    outs += [vector, vector, shape((LAYERS, 2, out_cols), F32), vector, vector, vector]
     outs += [shape((LAYERS, units), F32), vector, shape((LAYERS, depth, units), F32)]
-    outs += [shape((LAYERS, units, depth), F32), shape((LAYERS, out_cols, depth), F32)]
+    outs += [shape((LAYERS, depth, units), F32), shape((LAYERS, depth, out_cols), F32)]
+    outs += [shape((LAYERS, 3, depth, out_cols), F32)]
     return pl.pallas_call(
         finish_body,
-        in_specs=[VMEM] * (2 + len(totals) + len(came)),
+        in_specs=[VMEM] * (2 + len(totals) + len(came) + len(last)),
         out_specs=[VMEM] * len(outs),
         out_shape=outs,
         compiler_params=pltpu.CompilerParams(vmem_limit_bytes=VMEM_BYTES),
-    )(small, *totals, near, *came)
+    )(small, *totals, near, *came, *last)
 
 
 def pull_last_body(
@@ -1150,7 +1211,7 @@
         + [{"tp": links.other}]
         + group_greets(links)
     )
-    chunks = [pl.ds(c * ROWS, ROWS) for c in range(grad.shape[0] // ROWS)]
+    chunks = [pl.ds(c * CHUNK[0], CHUNK[0]) for c in range(grad.shape[0] // CHUNK[0])]
     start_pulls, wait_pulls, finish_pulls = trade_pulls(
         links, grad_q, grad_kv, grad_kv_back, full, back_got
     )
@@ -1181,8 +1242,7 @@
         total[...] = jnp.zeros_like(total)
     for one in loads:
         one.wait()
-    early_sum.add()
-    early_sum.start()
+    early_sum.send(0)
     core_sums[0].multiply(left1, wide1, plain, flipped)
     core_sums[1].multiply(right1, narrow1, plain, flipped)
     held[0] = jnp.zeros(held.shape[1:], F32)
@@ -1193,8 +1253,9 @@
         over_x[at].start()
     for c, rows in enumerate(chunks):
         wait_pulls(c)
-        pull_qkv_rows(c * ROWS, None, links, full, back_got, w_qkv, part, sum_qkv)
+        pull_qkv_rows(c * CHUNK[0], None, links, full, back_got, w_qkv, part, sum_qkv)
         swaps[c].start()
+    early_sum.pass_on(0)
     core_sums[2].multiply(left, full, plain, flipped)
     core_sums[3].multiply(right, narrow, plain, flipped)
     core_sums[2].add()
@@ -1205,33 +1266,36 @@
         over_x[at].start()
     for c, rows in enumerate(chunks):
         swaps[c].wait()
-        pull_norm_rows(c * ROWS, grad, part, got, stream, gain, grad_new, (sum_gain, sum_bias))
+        pull_norm_rows(c * CHUNK[0], grad, part, got, stream, gain, grad_new, (sum_gain, sum_bias))
     pack_sums(sums_zero, held.at[0], 0)
     smalls.near[0].start()
     smalls.step(0)
     smalls.near[1].start()
     for at, one in enumerate(group_sums):
         over_x[at].wait()
-        one.add()
-        one.start()
+        one.send(0)
+        if at:
+            group_sums[at - 1].pass_on(0)
         if at == 3:
             smalls.step(1)
             for far_one in smalls.along:
                 far_one.start()
+    group_sums[-1].pass_on(0)
     finish_pulls()
     small[...] = smalls.finish()
-    early_sum.finish()
+    early_sum.finish(2)
     for one in group_sums:
-        one.finish()
+        one.finish(2)
 
 
 def pull_last_segment(pulls, gain, qkv, grad, stream, factors, sums_in, smalls):
+    CHUNK[0] = SIZES[4]
     rows, width = grad.shape
     cols = pulls[0].shape[2]
     out_cols = GROUP * cols
     total = 3 * out_cols
     units = sums_in[0].shape[1]
-    chunks = rows // ROWS
+    chunks = rows // CHUNK[0]
     groups = lax.axis_size("fsdp") // GROUP
     copies = pltpu.SemaphoreType.DMA(
         (pull_copies(rows) + chunks + 10 + 7 * (groups - 1) + groups + 1,)
@@ -1291,13 +1355,22 @@
     )
 
 
+def halving_order(count):
+    order = [0]
+    bit = count // 2
+    while bit:
+        order = order + [at + bit for at in order]
+        bit //= 2
+    return order
+
+
 def flip_slots(links, source, plain, flipped):
     plain[...] = source[...].T
     depth = plain.shape[0] // (GROUP * links.groups)
     slot = 0
     for s in (0, 2, 1, 3):
-        for onward in range(links.groups):
-            owner = lax.rem(links.group + onward, links.groups) * GROUP + (links.place ^ s)
+        for other in halving_order(links.groups):
+            owner = (links.group ^ other) * GROUP + (links.place ^ s)
             flipped[slot * depth : (slot + 1) * depth, :] = plain[
                 pl.ds(pl.multiple_of(owner * depth, depth), depth), :
             ]
@@ -1349,43 +1422,43 @@
     def __init__(self, links, stay, met, far, came, result):
         self.stay, self.met, self.far, self.came, self.result = stay, met, far, came, result
         self.depth = result.shape[0]
-        self.copies = []
-        for onward in range(1, links.groups):
-            rows = pl.ds((onward - 1) * self.depth, self.depth)
-            self.copies.append(links.copy(far.at[rows], came.at[rows], links.beyond(onward, 0)))
-
-    def add(self):
+        self.copies, self.counts = [], []
+        first, count, bit = 0, links.groups // 2, 1
+        while count:
+            rows = pl.ds(first * self.depth, count * self.depth)
+            device = {"fsdp": (links.group ^ bit) * GROUP + links.place}
+            self.copies.append(links.copy(far.at[rows], came.at[rows], device))
+            self.counts.append((first, count))
+            first, count, bit = first + count, count // 2, bit * 2
+
+    def add(self, step, target, target_first, first, count):
         chunk = 16
 
-        def near(at):
-            self.result[at, :] = self.stay[at, :].astype(F32) + self.met[at, :].astype(F32)
-
-        each_rows(self.depth, chunk, near)
-
-        def far(at):
-            from_row = pl.ds(pl.multiple_of(at.start + self.depth, chunk), chunk)
-            total = self.stay[from_row, :].astype(F32) + self.met[from_row, :].astype(F32)
-            self.far[at, :] = total.astype(BF16)
-
-        each_rows(self.far.shape[0], chunk, far)
-
-    def start(self):
-        for one in self.copies:
-            one.start()
-
-    def finish(self):
-        for one in self.copies:
-            one.wait()
-        chunk = 16
-
         def body(at):
-            total = self.result[at, :]
-            for onward in range(len(self.copies)):
-                from_row = pl.ds(pl.multiple_of(at.start + onward * self.depth, chunk), chunk)
-                total = total + self.came[from_row, :].astype(F32)
-            self.result[at, :] = total
-
-        each_rows(self.depth, chunk, body)
+            def rows(slot):
+                return pl.ds(pl.multiple_of(at.start + slot * self.depth, chunk), chunk)
+
+            total = self.stay[rows(first), :].astype(F32) + self.met[rows(first), :].astype(F32)
+            for came_first, _ in self.counts[:step]:
+                total = total + self.came[rows(came_first + first), :].astype(F32)
+            target[rows(target_first), :] = total.astype(target.dtype)
+
+        each_rows(count * self.depth, chunk, body)
+
+    def send(self, step):
+        first, count = self.counts[step]
+        self.add(step, self.far, first, count, count)
+        self.copies[step].start()
+
+    def pass_on(self, step):
+        self.copies[step].wait()
+        self.send(step + 1)
+
+    def finish(self, sent=1):
+        for step in range(sent, len(self.copies)):
+            self.pass_on(step - 1)
+        self.copies[-1].wait()
+        self.add(len(self.copies), self.result, 0, 0, 1)
 
 
 def group_scratch(stay, groups, met):
@@ -1678,21 +1751,13 @@
     me = lax.axis_index("fsdp")
     total_rows = rows * lax.axis_size("fsdp")
 
-    def pack_qkv(l):
-        return w_qkv[l].reshape(depth, 3, GROUP, cols).transpose(0, 2, 1, 3).reshape(depth, 3 * out_cols)
-
-    def pack_rest(l):
-        return [w_out[l].T, w_fc[l], w_proj[l].T]
-
-    rest = gather(jnp.concatenate(pack_rest(0) + pack_rest(1), 1))
+    rest, *packed = pack(w_qkv, b_qv, w_out, w_fc, w_proj)
+    rest = gather(rest)
+    shards_qkv, bias_qkv = packed[:LAYERS], packed[LAYERS:]
 
     def rest_at(l):
         first = l * (out_cols + 2 * units)
         return (first, first + out_cols, first + out_cols + units)
-
-    def bias_qkv(l):
-        three = jnp.stack([b_qv[l, 0], jnp.zeros_like(b_qv[l, 0]), b_qv[l, 1]])
-        return three.reshape(3, GROUP, cols).transpose(1, 0, 2).reshape(1, 3 * out_cols)
 
     def row(vector):
         return vector.reshape(1, vector.shape[0])
@@ -1702,8 +1767,8 @@
         tokens,
         row(ln1_gain[0]),
         row(ln1_bias[0]),
-        pack_qkv(0),
-        bias_qkv(0),
+        shards_qkv[0],
+        bias_qkv[0],
         segments.reshape(rows // 128, 128),
         docs,
     )
@@ -1726,11 +1791,11 @@
             mixed,
             stream,
             [row(vector) for vector in vectors],
-            bias_qkv(l + 1),
+            bias_qkv[l + 1],
             rest,
             rest_at(l),
             units,
-            pack_qkv(l + 1),
+            shards_qkv[l + 1],
         )
         stored.append(
             (stream, low_one, pieces, kv_back, out, log_total, mixed_full, middle, low_two, hidden, act)
@@ -1767,8 +1832,7 @@
         rest_at(l),
         units,
     )
-    other_two = swap_tp(part_two)
-    outputs = (middle + (part_two.astype(F32) + other_two.astype(F32)) + b_proj[l][None]).astype(BF16)
+    last = [middle, part_two, swap_tp(part_two), row(b_proj[l])]
 
     stay0, go0, stay1, go1 = feed_parts
     met0 = swap_fsdp(go0, 2)
@@ -1811,10 +1875,9 @@
     )
     feed_totals, near, far, (stay0, go0) = later[:2], later[2], later[3:-2], later[-2:]
     came = []
-    for onward, value in enumerate(far, 1):
-        size = lax.axis_size("fsdp")
-        pairs = [(i, (i + GROUP * onward) % size) for i in range(size)]
-        came.append(lax.ppermute(value, "fsdp", pairs))
+    others = halving_order(lax.axis_size("fsdp") // GROUP)[1:]
+    for other, value in zip(others, far):
+        came.append(swap_fsdp(value, GROUP * other))
     met0 = swap_fsdp(go0, 2)
     sums_one = [sum_gain_one, sum_bias_one, sum_bqkv] + sums_one
     pulls = attend_pull(sc, docs, pieces, grad_mixed, kv_back, out, log_total)
@@ -1830,15 +1893,27 @@
         [stay0, met0],
         sums_one + sums_zero,
     )
-    gain1, bias1, bqv, bout, gain2, bias2, bfc, bproj, grad_wfc, grad_wproj, grad_wout = finish(
-        small, [*feed_totals, out1, proj0, out0], near, came, out_cols, units
-    )
-    grad_wqkv = jnp.stack(
-        [
-            value.reshape(depth, GROUP, 3, cols).transpose(0, 2, 1, 3).reshape(depth, 3, out_cols)
-            for value in (qkv0, qkv1)
-        ]
-    )
+    (
+        outputs,
+        grad,
+        gain1,
+        bias1,
+        bqv,
+        bout,
+        gain2,
+        bias2,
+        bfc,
+        bproj,
+        grad_wfc,
+        grad_wproj,
+        grad_wout,
+        grad_wqkv,
+    ) = finish(
+        small, [*feed_totals, qkv1, out1, proj0, qkv0, out0], near, came, [grad, *last], out_cols, units
+    )
+    grad_wproj = grad_wproj.transpose(0, 2, 1)
+    grad_wout = grad_wout.transpose(0, 2, 1)
+    grad_wqkv = grad_wqkv.transpose(0, 2, 1, 3)
 
     return (
         outputs,

time: 634 us -> 606 us (0.956)
  local copies, waits for them, and re-layouts: 22.3 us -> 3.48 us
    unnamed x48 -> x30, local copies, waits for them, and re-layouts: 13.3 us -> 1.03 us
    pallas_call x5, Pallas kernels: 474 us -> 466 us  [run_links(): pl.pallas_call(body, in_specs=[spec for spec, _ in ins], out_specs=[spec...]
    ppermute x3 -> x0, starting transfers between devices: 7.07 us -> none  [shards(): came.append(lax.ppermute(value, 'fsdp', pairs))]
  transfers between devices with their start and end apart: 7 -> 7, of which waited for: 2 -> 2; matrix products, arithmetic and copies ran while one was open for 2% -> 1% of each run, Pallas kernels for 43% -> 44%
where the time goes in v5:
time: 606 us; the launch traced here: 600 us
  Pallas kernels  550 us (91%)
  waiting for transfers between devices  19.7 us (3%)
  between operations  14.7 us (2%)
  starting transfers between devices  8.08 us (1%)
    pallas_call x5, Pallas kernels, run_links(): pl.pallas_call(body, in_specs=[spec for spec, _ in ins], out_specs=[spec...  466 us
    pallas_call x4, Pallas kernels, run_kernel(): pl.pallas_call(body, grid_spec=pltpu.PrefetchScalarGridSpec(num_scalar_pr...  73.9 us
    all_gather x1, waiting for transfers between devices, gather(): return lax.all_gather(shard, 'fsdp', axis=0, tiled=True)  16.9 us
  transfers between devices with their start and end apart: 7, of which 2 were waited for; matrix products, arithmetic and copies ran while one was open for 1% of the time, Pallas kernels for 44%

profile of v5, /device:TPU:0, one launch (start us, length us, event | category | flops | bytes accessed | tf_op | source)
XLA Modules:
  0.0 599.6 jit_solution(5547946442586290238)
XLA Ops:
  7.2 2.6 shard_map.263
  10.5 94.6 %shard_map.264 = (f32[512,1024]{1,0:T(8,128)}, bf16[512,1024]{1,0:T(8,128)(2,1)}, bf16[1024,1536]{1,0:T(8,128)(2,1)}, f32[8,128]{1,0:T(8,128)}, f32[8,128]{1,0:T...) custom-call(bf16[512,1024]{1,0:T(8,128)(2,1)} %base.1, f32[1,1024]{1,0:T(1,128)} %get-tuple-element.234.gain, ...), custom_call_target="tpu_custom_call" | custom-call | flops 1610612736 | bytes 7340032 | tf_op jit(solution)/shard_map/pallas_call | solution.py:397
  105.1 0.8 convert_reduce_fusion.1
  106.5 0.8 convert_reduce_fusion
  107.7 15.6 %shard_map.265 = (bf16[2048,128]{1,0:T(8,128)(2,1)}, f32[2048,128]{1,0:T(8,128)}, f32[8,2048]{1,0:T(8,128)}) custom-call(s32[10]{0:T(128)} %pad_add_fusion.sc, bf16[2048,384]{1,0:T(8,128)(2,1)} %bitcast.34, bf16[2048,256]{1,0:T(8,128)(2,1)} %bitcast.38), custom_call_target="tpu_custom_call" | custom-call | flops 2147483648 | bytes 5242880 | tf_op jit(solution)/shard_map/pallas_call | solution.py:48
  123.3 0.6 fusion.3
  124.5 1.5 convert_multiply_fusion.grad_in
  126.0 0.6 fusion
  126.7 16.9 %all-gather.2.cloned.1.call-done.rest = bf16[1024,9216]{1,0:T(8,128)(2,1)} async-done(((bf16[64,9216]{1,0:T(8,128)(2,1)}), bf16[1024,9216]{1,0:T(8,128)(2,1)}) %all-gather.2.cloned.1.call-update) | async-done | bytes 18874384 | tf_op jit(solution)/shard_map/all_gather | solution.py:1720
  143.5 84.1 %shard_map.266 = (bf16[512,512]{1,0:T(8,128)(2,1)}, f32[512,1024]{1,0:T(8,128)}, bf16[512,1024]{1,0:T(8,128)(2,1)}, f32[512,2048]{1,0:T(8,128)}, bf16[512,2048]{...) custom-call(bf16[4,512,128]{2,1,0:T(8,128)(2,1)} %bitcast.45, ...), custom_call_target="tpu_custom_call" | custom-call | flops 6442450944 | bytes 29360128 | tf_op jit(solution)/shard_map/pallas_call | solution.py:397
  227.6 15.4 %shard_map.267 = (bf16[2048,128]{1,0:T(8,128)(2,1)}, f32[2048,128]{1,0:T(8,128)}, f32[8,2048]{1,0:T(8,128)}) custom-call(s32[10]{0:T(128)} %pad_add_fusion.sc, bf16[2048,384]{1,0:T(8,128)(2,1)} %bitcast.36, bf16[2048,256]{1,0:T(8,128)(2,1)} %bitcast.40), custom_call_target="tpu_custom_call" | custom-call | flops 2147483648 | bytes 5242880 | tf_op jit(solution)/shard_map/pallas_call | solution.py:48
  243.1 67.0 %shard_map.268 = (bf16[512,512]{1,0:T(8,128)(2,1)}, f32[512,1024]{1,0:T(8,128)}, bf16[512,1024]{1,0:T(8,128)(2,1)}, bf16[512,2048]{1,0:T(8,128)(2,1)}, bf16[512,...) custom-call(bf16[4,512,128]{2,1,0:T(8,128)(2,1)} %bitcast.47, ...), custom_call_target="tpu_custom_call" | custom-call | flops 9663676416 | bytes 25165824 | tf_op jit(solution)/shard_map/pallas_call | solution.py:397
  310.1 1.0 collective-permute-start
  311.1 21.3 %shard_map.269 = (bf16[2048,128]{1,0:T(8,128)(2,1)}, bf16[2048,256]{1,0:T(8,128)(2,1)}, bf16[2048,256]{1,0:T(8,128)(2,1)}) custom-call(s32[10]{0:T(128)} %pad_add_fusion.sc, bf16[2048,384]{1,0:T(8,128)(2,1)} %bitcast.37, bf16[2048,128]{1,0:T(8,128)(2,1)} %bitcast.46, bf16[2048,256]{1,0:T(8,128)(2,1)} %bitcast.41, f32[2048,128]{1,0:T(8,128)} %get-tuple-element.135.out, ...), custom_call_target="tpu_custom_call" | custom-call | flops 4831838208 | bytes 7864320 | tf_op jit(solution)/shard_map/pallas_call | solution.py:48
  332.4 2.8 collective-permute-done.met0_in
  335.2 1.0 copy-done.1
  336.1 110.9 %shard_map.270 = (bf16[512,1536]{1,0:T(8,128)(2,1)}, f32[8,1536]{1,0:T(8,128)}, f32[8,1024]{1,0:T(8,128)}, f32[8,1024]{1,0:T(8,128)}, bf16[512,1024]{1,0:T(8,128...) custom-call(bf16[4,512,128]{2,1,0:T(8,128)(2,1)} %bitcast.25, ...), custom_call_target="tpu_custom_call" | custom-call | flops 6442450944 | bytes 30408704 | tf_op jit(solution)/shard_map/pallas_call | solution.py:397
  447.1 1.1 collective-permute-start.4
  448.1 1.6 collective-permute-start.5
  449.8 2.5 collective-permute-start.2
  452.3 1.9 collective-permute-start.3
  454.1 21.6 %shard_map.271 = (bf16[2048,128]{1,0:T(8,128)(2,1)}, bf16[2048,256]{1,0:T(8,128)(2,1)}, bf16[2048,256]{1,0:T(8,128)(2,1)}) custom-call(s32[10]{0:T(128)} %pad_add_fusion.sc, bf16[2048,384]{1,0:T(8,128)(2,1)} %bitcast.35, bf16[2048,128]{1,0:T(8,128)(2,1)} %bitcast.32, bf16[2048,256]{1,0:T(8,128)(2,1)} %bitcast.39, f32[2048,128]{1,0:T(8,128)} %get-tuple-element.155.out, ...), custom_call_target="tpu_custom_call" | custom-call | flops 4831838208 | bytes 7864320 | tf_op jit(solution)/shard_map/pallas_call | solution.py:48
  475.8 109.3 %shard_map.272 = (f32[512,1024]{1,0:T(8,128)}, f32[24,1024]{1,0:T(8,128)}, f32[64,2048]{1,0:T(8,128)}, f32[64,1536]{1,0:T(8,128)}, f32[64,512]{1,0:T(8,128)}, /*index=5*/f32[64,1536]{1,0:T(8,128)}, f32[64,512]{1,0:T(8,128)}) custom-call(bf16[4,512,128]{2,1,0:T(8,128)(2,1)} %bitcast.44, bf16[4,512,256]{2,1,0:T(8,128)(2,1)} %bitcast.42, ...), custom_call_target="tpu_custom_call" | custom-call | flops 5905580032 | bytes 15728640 | tf_op jit(solution)/shard_map/pallas_call | solution.py:397
  585.1 7.1 %shard_map.273 = (bf16[512,1024]{1,0:T(8,128)(2,1)}, f32[512,1024]{1,0:T(8,128)}, f32[2,1024]{1,0:T(2,128)}, f32[2,1024]{1,0:T(2,128)}, f32[2,2,512]{2,1,0:T(2,1...) custom-call(f32[24,1024]{1,0:T(8,128)} %get-tuple-element.191.small,, ...), custom_call_target="tpu_custom_call" | custom-call | tf_op jit(solution)/shard_map/pallas_call | solution.py:1166
  (44 shorter events, 2.2 us)
Async XLA Ops:
  7.2 2.7 copy-start.7
  7.2 2.7 copy-start.8
  7.2 136.3 %all-gather.2.cloned.1.call-start = ((), (), s32[]{:S(2)}) async-start(), calls=%async_computation | async-start | bytes 20054016 | tf_op jit(solution)/shard_map/all_gather | solution.py:1720
  10.5 96.8 %copy-start.14 = (s32[8]{0:T(128)S(1)}, s32[8]{0:T(128)}, u32[]{:S(2)}) copy-start(s32[8]{0:T(128)} %param.19) | copy-start | bytes 100
  10.5 97.0 %copy-start.13 = (s32[512]{0:T(512)S(1)}, s32[512]{0:T(512)}, u32[]{:S(2)}) copy-start(s32[512]{0:T(512)} %param.18) | copy-start | bytes 6148
  107.6 15.6 %copy-start.9 = (f32[2,1024]{1,0:T(2,128)S(1)}, f32[2,1024]{1,0:T(2,128)}, u32[]{:S(2)}) copy-start(f32[2,1024]{1,0:T(2,128)} %param.26) | copy-start | bytes 24580
  107.6 15.6 %copy-start.10 = (f32[2,1024]{1,0:T(2,128)S(1)}, f32[2,1024]{1,0:T(2,128)}, u32[]{:S(2)}) copy-start(f32[2,1024]{1,0:T(2,128)} %param.25) | copy-start | bytes 24580
  107.6 16.3 %copy-start.11 = (f32[2,1024]{1,0:T(2,128)S(1)}, f32[2,1024]{1,0:T(2,128)}, u32[]{:S(2)}) copy-start(f32[2,1024]{1,0:T(2,128)} %param.31) | copy-start | bytes 24580
  107.6 16.3 %copy-start.12 = (f32[2,1024]{1,0:T(2,128)S(1)}, f32[2,1024]{1,0:T(2,128)}, u32[]{:S(2)}) copy-start(f32[2,1024]{1,0:T(2,128)} %param.27) | copy-start | bytes 24580
  107.6 16.9 %copy-start.2 = (bf16[512,1024]{1,0:T(8,128)(2,1)S(1)}, bf16[512,1024]{1,0:T(8,128)(2,1)}, u32[]{:S(2)}) copy-start(bf16[512,1024]{1,0:T(8,128)(2,1)} %param.17) | copy-start | bytes 3145732
  123.2 2.8 copy-start.6
  310.1 25.1 %collective-permute-start = (bf16[256,2048]{1,0:T(8,128)(2,1)}, bf16[256,2048]{1,0:T(8,128)(2,1)S(1)}, u32[]{:S(2)}, u32[]{:S(2)}) collective-permute-start(bf16[256,2048]{1,0:T(8,128)(2,1)} %get-tuple-element.140), channel_id=1, source_target_pairs={{0,4},{2,6},{4,0},{6,2},{8,12},{10,14},{12,8},{14,10},{16,20},{18,... | collective-permute-start | bytes 3145736 | tf_op jit(solution)/shard_map/ppermute | solution.py:1711
  335.2 1.0 copy-start.1
  336.1 112.0 %copy-start = (bf16[512,1024]{1,0:T(8,128)(2,1)S(1)}, bf16[512,1024]{1,0:T(8,128)(2,1)}, u32[]{:S(2)}) copy-start(bf16[512,1024]{1,0:T(8,128)(2,1)} %get-tuple-element.205.refs_5_) | copy-start | bytes 3145732
  447.1 28.7 %collective-permute-start.4 = (bf16[256,2048]{1,0:T(8,128)(2,1)}, bf16[256,2048]{1,0:T(8,128)(2,1)}, u32[]{:S(2)}, u32[]{:S(2)}) collective-permute-start(bf16[256,2048]{1,0:T(8,128)(2,1)} %get-tuple-element.163), channel_id=1, source_target_pairs={{0,4},{2,6},{4,0},{6,2},{8,12},{10,14},{12,8},{14,10},{16,20},{18,... | collective-permute-start | bytes 3145736 | tf_op jit(solution)/shard_map/ppermute | solution.py:1711
  448.1 137.0 %collective-permute-start.5 = (bf16[512,1024]{1,0:T(8,128)(2,1)S(1)}, bf16[512,1024]{1,0:T(8,128)(2,1)}, u32[]{:S(2)}, u32[]{:S(2)}) collective-permute-start(bf16[512,1024]{1,0:T(8,128)(2,1)S(1)} %copy-done), channel_id=1, source_target_pairs={{0,1},{1,0},{2,3},{3,2},{4,5},{5,4},{6,7},{7,6},{8,9},{9,8},{10,11... | collective-permute-start | bytes 3145736 | tf_op jit(solution)/shard_map/ppermute | solution.py:1707
  449.7 26.0 %collective-permute-start.1 = (bf16[64,2048]{1,0:T(8,128)(2,1)}, bf16[64,2048]{1,0:T(8,128)(2,1)S(1)}, u32[]{:S(2)}, u32[]{:S(2)}) collective-permute-start(bf16[64,2048]{1,0:T(8,128)(2,1)} %get-tuple-element.160), channel_id=1, source_target_pairs={{0,16},{2,18},{4,20},{6,22},{8,24},{10,26},{12,28},{14,30},{16,0},... | collective-permute-start | bytes 786440 | tf_op jit(solution)/shard_map/ppermute | solution.py:1711
  449.8 26.0 %collective-permute-start.2 = (bf16[64,2048]{1,0:T(8,128)(2,1)}, bf16[64,2048]{1,0:T(8,128)(2,1)S(1)}, u32[]{:S(2)}, u32[]{:S(2)}) collective-permute-start(bf16[64,2048]{1,0:T(8,128)(2,1)} %get-tuple-element.161), channel_id=1, source_target_pairs={{0,8},{2,10},{4,12},{6,14},{8,0},{10,2},{12,4},{14,6},{16,24},{18,... | collective-permute-start | bytes 786440 | tf_op jit(solution)/shard_map/ppermute | solution.py:1711
  452.3 23.5 %collective-permute-start.3 = (bf16[64,2048]{1,0:T(8,128)(2,1)}, bf16[64,2048]{1,0:T(8,128)(2,1)S(1)}, u32[]{:S(2)}, u32[]{:S(2)}) collective-permute-start(bf16[64,2048]{1,0:T(8,128)(2,1)} %get-tuple-element.162), channel_id=1, source_target_pairs={{0,24},{2,26},{4,28},{6,30},{8,16},{10,18},{12,20},{14,22},{16,8},... | collective-permute-start | bytes 786440 | tf_op jit(solution)/shard_map/ppermute | solution.py:1711
  475.7 109.4 %copy-start.3 = (bf16[64,2048]{1,0:T(8,128)(2,1)}, bf16[64,2048]{1,0:T(8,128)(2,1)S(1)}, u32[]{:S(2)}) copy-start(bf16[64,2048]{1,0:T(8,128)(2,1)S(1)} %collective-permute-done.1.refs_0_) | copy-start | bytes 786436
  475.7 109.4 %copy-start.4 = (bf16[64,2048]{1,0:T(8,128)(2,1)}, bf16[64,2048]{1,0:T(8,128)(2,1)S(1)}, u32[]{:S(2)}) copy-start(bf16[64,2048]{1,0:T(8,128)(2,1)S(1)} %collective-permute-done.2.refs_1_) | copy-start | bytes 786436
  475.7 109.4 %copy-start.5 = (bf16[64,2048]{1,0:T(8,128)(2,1)}, bf16[64,2048]{1,0:T(8,128)(2,1)S(1)}, u32[]{:S(2)}) copy-start(bf16[64,2048]{1,0:T(8,128)(2,1)S(1)} %collective-permute-done.3.refs_2_) | copy-start | bytes 786436
Sparse Core Ops, SparseCore 0:
  10.0 133.5 all-gather.1
